TPU v7x, 32 devices: a whole 2x2x4 slice. The times are simulated.
32 devices in a mesh: dp: 32 (over z, y, x, core).
Axes of the slice: x: 2, y: 2, z: 4, core: 2. Of those that a mesh axis runs over, the one named last changes fastest.
Arguments:
- big_crops: bfloat16 [1024, 7, 7, 2048], P('dp'), may hold values from -6 to 6
- small_crops: bfloat16 [4096, 3, 3, 2048], P('dp'), may hold values from -6 to 6
- small_count: int32 [512], P('dp'), may hold values from 2 to 8
- w_reduce: bfloat16 [2048, 512], replicated, may hold values from -0.125 to 0.125
- w_spatial: bfloat16 [512, 9, 512], replicated, may hold values from -0.09375 to 0.09375
- w_expand: bfloat16 [512, 2048], replicated, may hold values from -0.25 to 0.25
- gain_mid: float32 [2, 512], replicated, may hold values from 0.5 to 1.5
- bias_mid: float32 [2, 512], replicated, may hold values from -3 to 3
- gain_wide: float32 [2048], replicated, may hold values from 0.5 to 1.5
- bias_wide: float32 [2048], replicated, may hold values from -3 to 3
- w_hidden: bfloat16 [2048, 2048], replicated, may hold values from -0.125 to 0.125
- gain_head: float32 [2048], replicated, may hold values from 0.5 to 1.5
- bias_head: float32 [2048], replicated, may hold values from -3 to 3
- w_project: bfloat16 [2048, 128], replicated, may hold values from -0.125 to 0.125
- prototypes: bfloat16 [128, 3000], replicated, may hold values from -0.8984375 to 0.8984375
- queue: bfloat16 [2, 960, 128], P(None, 'dp'), may hold values from -6 to 6
Outputs:
- loss: float32 [], replicated
- grad_big: bfloat16 [1024, 7, 7, 2048], P('dp')
- grad_small: bfloat16 [4096, 3, 3, 2048], P('dp')
- grad_w_reduce: float32 [2048, 512], P('dp')
- grad_w_spatial: float32 [512, 9, 512], P('dp')
- grad_w_expand: float32 [512, 2048], P('dp')
- grad_gain_mid: float32 [2, 512], replicated
- grad_bias_mid: float32 [2, 512], replicated
- grad_gain_wide: float32 [2048], replicated
- grad_bias_wide: float32 [2048], replicated
- grad_w_hidden: float32 [2048, 2048], P('dp')
- grad_gain_head: float32 [2048], replicated
- grad_bias_head: float32 [2048], replicated
- grad_w_project: float32 [2048, 128], P('dp')
- grad_prototypes: float32 [128, 3000], P('dp')
All inputs are finite; a program needn't handle non-finite values.
Results may differ from a plain program's by a relative error of at most 0.025.
Values sent between devices are 32-bit elements; how exact they have to be, the bound alone decides.
No kernel may reach another device: no remote copies, remote signals or barrier semaphores. Data moves between devices by JAX's collectives and lax.ppermute only.
A program may use at most 320 MiB of HBM per device.

v0:
```python
import jax
import jax.numpy as jnp
from jax import lax
from jax.sharding import PartitionSpec as P

ITERS = 3


EPS_NORM = 1e-05
EPS_UNIT = 1e-06
EPS_CODE = 0.05
SOFTMAX_HEAT = 0.1


def product(left, right):
    return jnp.dot(left, right, preferred_element_type=jnp.float32)


def product_inner(left, right):
    return lax.dot_general(
        left, right, (((0,), (0,)), ((), ())), preferred_element_type=jnp.float32
    )


def product_outer(left, right):
    return lax.dot_general(
        left, right, (((1,), (1,)), ((), ())), preferred_element_type=jnp.float32
    )


def silu_slope(value_entries, grad):
    sigmoid = jax.nn.sigmoid(value_entries)
    return grad * sigmoid * (1.0 + value_entries * (1.0 - sigmoid))


def forward_norm(value_entries, weight, extra, count_of):
    weighted = value_entries * weight[:, None]
    total, extra_sum = lax.psum((jnp.sum(weighted, axis=0), extra), "dp")
    count = count_of(extra_sum)
    mean = total / count
    centered = value_entries - mean
    spread = lax.psum(jnp.sum(weight[:, None] * centered * centered, axis=0), "dp") / count
    scale = lax.rsqrt(spread + EPS_NORM)
    return ((value_entries - mean) * scale, scale, count, extra_sum)


def backward_norm(grad, normed, scale, weight, count, gain, extra):
    weighted = grad * weight[:, None]
    bias_sum, gain_sum, extra_sum = lax.psum(
        (jnp.sum(weighted, axis=0), jnp.sum(weighted * normed, axis=0), extra), "dp"
    )
    back = weight[:, None] * (gain * scale) * (grad - bias_sum / count - normed * gain_sum / count)
    return (back, gain_sum, bias_sum, extra_sum)


def spatial_forward(field, weight, crops, side):
    channels = field.shape[1]
    padded = jnp.pad(field.reshape(crops, side, side, channels), ((0, 0), (1, 1), (1, 1), (0, 0)))
    total = jnp.zeros((crops * side * side, weight.shape[2]), jnp.float32)
    for tap in range(9):
        row = tap // 3
        column = tap % 3
        window = padded[:, row : row + side, column : column + side, :].reshape(
            crops * side * side, channels
        )
        total = total + product(window, weight[:, tap, :])
    return total


def spatial_backward(field, weight, grad, crops, side):
    channels = field.shape[1]
    padded = jnp.pad(field.reshape(crops, side, side, channels), ((0, 0), (1, 1), (1, 1), (0, 0)))
    grad_padded = jnp.zeros((crops, side + 2, side + 2, channels), jnp.float32)
    taps = []
    for tap in range(9):
        row = tap // 3
        column = tap % 3
        window = padded[:, row : row + side, column : column + side, :].reshape(
            crops * side * side, channels
        )
        taps.append(product_inner(window, grad))
        back = product_outer(grad, weight[:, tap, :]).reshape(crops, side, side, channels)
        grad_padded = grad_padded + jnp.pad(
            back, ((0, 0), (row, 2 - row), (column, 2 - column), (0, 0))
        )
    inner = grad_padded[:, 1 : side + 1, 1 : side + 1, :].reshape(crops * side * side, channels)
    return (inner, jnp.stack(taps, axis=1))


def local(
    big_crops,
    small_crops,
    small_count,
    w_reduce,
    w_spatial,
    w_expand,
    gain_mid,
    bias_mid,
    gain_wide,
    bias_wide,
    w_hidden,
    gain_head,
    bias_head,
    w_project,
    prototypes,
    queue,
):
    devices = lax.axis_size("dp")
    image_rows = small_count.shape[0]
    images = image_rows * devices
    big_rows = big_crops.shape[0]
    big_side = big_crops.shape[1]
    small_rows = small_crops.shape[0]
    small_side = small_crops.shape[1]
    views = big_rows // image_rows
    slots = small_rows // image_rows
    wide = big_crops.shape[3]
    big_area = big_side * big_side
    small_area = small_side * small_side
    big_pixels = big_rows * big_area
    slot_mask = (jnp.arange(slots)[None, :] < small_count[:, None]).astype(jnp.float32)
    slot_flags = slot_mask.reshape(-1)
    crop_weight = jnp.concatenate([jnp.ones((big_rows,), jnp.float32), slot_flags])
    pixel_weight = jnp.concatenate(
        [jnp.ones((big_pixels,), jnp.float32), jnp.repeat(slot_flags, small_area)]
    )
    local_count = jnp.sum(small_count).astype(jnp.float32)
    nothing = jnp.zeros((), jnp.float32)
    inputs = jnp.concatenate(
        [big_crops.reshape(big_pixels, wide), small_crops.reshape(small_rows * small_area, wide)]
    )
    first = product(inputs, w_reduce)
    normed_one, scale_one, pixel_count, count_sum = forward_norm(
        first, pixel_weight, local_count, lambda total: devices * big_pixels + small_area * total
    )
    crop_count = devices * big_rows + count_sum
    pre_one = normed_one * gain_mid[0] + bias_mid[0]
    mid_one = jax.nn.silu(pre_one).astype(jnp.bfloat16)
    second = jnp.concatenate(
        [
            spatial_forward(mid_one[:big_pixels], w_spatial, big_rows, big_side),
            spatial_forward(mid_one[big_pixels:], w_spatial, small_rows, small_side),
        ]
    )
    normed_two, scale_two, _, _ = forward_norm(
        second, pixel_weight, nothing, lambda total: pixel_count
    )
    pre_two = normed_two * gain_mid[1] + bias_mid[1]
    mid_two = jax.nn.silu(pre_two).astype(jnp.bfloat16)
    third = product(mid_two, w_expand)
    normed_three, scale_three, _, _ = forward_norm(
        third, pixel_weight, nothing, lambda total: pixel_count
    )
    residual = normed_three * gain_wide + bias_wide + inputs.astype(jnp.float32)
    output = jax.nn.silu(residual)
    pooled = jnp.concatenate(
        [
            jnp.mean(output[:big_pixels].reshape(big_rows, big_area, wide), axis=1),
            jnp.mean(output[big_pixels:].reshape(small_rows, small_area, wide), axis=1),
        ]
    ).astype(jnp.bfloat16)
    hidden = product(pooled, w_hidden)
    normed_head, scale_head, _, _ = forward_norm(
        hidden, crop_weight, nothing, lambda total: crop_count
    )
    pre_head = normed_head * gain_head + bias_head
    active = jax.nn.silu(pre_head).astype(jnp.bfloat16)
    embedded = product(active, w_project)

    def to_unit(value_entries):
        return value_entries * lax.rsqrt(
            jnp.sum(value_entries * value_entries, axis=1, keepdims=True) + EPS_UNIT
        )

    unit, unit_pull = jax.vjp(to_unit, embedded)
    unit_low = unit.astype(jnp.bfloat16)
    prototype_scores = product(unit_low, prototypes)
    proto = prototype_scores.shape[1]
    queue_float = queue.astype(jnp.float32)
    queue_unit = (
        queue_float
        * lax.rsqrt(jnp.sum(queue_float * queue_float, axis=2, keepdims=True) + EPS_UNIT)
    ).astype(jnp.bfloat16)
    queue_score_rows = jnp.einsum(
        "vqp,pk->vqk", queue_unit, prototypes, preferred_element_type=jnp.float32
    )
    batch_exp = jnp.exp(
        jnp.transpose(prototype_scores[:big_rows].reshape(image_rows, views, proto), (1, 0, 2))
        / EPS_CODE
    )
    queue_exp = jnp.exp(queue_score_rows / EPS_CODE)
    for step in range(ITERS):
        column_totals = lax.psum(jnp.sum(batch_exp, axis=1) + jnp.sum(queue_exp, axis=1), "dp")
        batch_exp = batch_exp / column_totals[:, None, :]
        batch_exp = batch_exp / jnp.sum(batch_exp, axis=2, keepdims=True)
        if step + 1 < ITERS:
            queue_exp = queue_exp / column_totals[:, None, :]
            queue_exp = queue_exp / jnp.sum(queue_exp, axis=2, keepdims=True)
    code_targets = jnp.transpose(batch_exp, (1, 0, 2))

    def local_loss(value_entries):
        log_probability = jax.nn.log_softmax(value_entries / SOFTMAX_HEAT, axis=1)
        big_logp = log_probability[:big_rows].reshape(image_rows, views, proto)
        small_logp = log_probability[big_rows:].reshape(image_rows, slots, proto)
        total = jnp.sum(big_logp, axis=1) + jnp.sum(small_logp * slot_mask[:, :, None], axis=1)
        per_view = jnp.sum(code_targets * (total[:, None, :] - big_logp), axis=2)
        share = 1.0 / (views * (views - 1.0 + small_count.astype(jnp.float32)))
        return -jnp.sum(jnp.sum(per_view, axis=1) * share) / images

    loss_part, loss_pull = jax.vjp(local_loss, prototype_scores)
    grad_scores = loss_pull(jnp.ones((), jnp.float32))[0].astype(jnp.bfloat16)
    grad_unit = product_outer(grad_scores, prototypes)
    proto_part = product_inner(unit_low, grad_scores)
    grad_embedded = unit_pull(grad_unit)[0].astype(jnp.bfloat16)
    project_part = product_inner(active, grad_embedded)
    grad_active = product_outer(grad_embedded, w_project)
    grad_hidden, gain_head_grad, bias_head_grad, loss = backward_norm(
        silu_slope(pre_head, grad_active),
        normed_head,
        scale_head,
        crop_weight,
        crop_count,
        gain_head,
        loss_part,
    )
    grad_hidden = grad_hidden.astype(jnp.bfloat16)
    grad_pooled = product_outer(grad_hidden, w_hidden)
    hidden_part = product_inner(pooled, grad_hidden)
    hidden_grad, project_grad, proto_grad = (
        lax.psum_scatter(hidden_part, "dp", scatter_dimension=0, tiled=True),
        lax.psum_scatter(project_part, "dp", scatter_dimension=0, tiled=True),
        lax.psum_scatter(proto_part, "dp", scatter_dimension=0, tiled=True),
    )
    grad_output = jnp.concatenate(
        [
            jnp.broadcast_to(
                grad_pooled[:big_rows, None, :] / big_area, (big_rows, big_area, wide)
            ).reshape(big_pixels, wide),
            jnp.broadcast_to(
                grad_pooled[big_rows:, None, :] / small_area, (small_rows, small_area, wide)
            ).reshape(small_rows * small_area, wide),
        ]
    )
    grad_residual = silu_slope(residual, grad_output)
    grad_third, gain_three, bias_three, _ = backward_norm(
        grad_residual, normed_three, scale_three, pixel_weight, pixel_count, gain_wide, nothing
    )
    grad_third = grad_third.astype(jnp.bfloat16)
    expand_part = product_inner(mid_two, grad_third)
    grad_mid_two = product_outer(grad_third, w_expand)
    grad_second, gain_two, bias_two, _ = backward_norm(
        silu_slope(pre_two, grad_mid_two),
        normed_two,
        scale_two,
        pixel_weight,
        pixel_count,
        gain_mid[1],
        nothing,
    )
    grad_second = grad_second.astype(jnp.bfloat16)
    big_back, big_taps = spatial_backward(
        mid_one[:big_pixels], w_spatial, grad_second[:big_pixels], big_rows, big_side
    )
    small_back, small_taps = spatial_backward(
        mid_one[big_pixels:], w_spatial, grad_second[big_pixels:], small_rows, small_side
    )
    grad_mid_one = jnp.concatenate([big_back, small_back])
    grad_first, gain_one, bias_one, _ = backward_norm(
        silu_slope(pre_one, grad_mid_one),
        normed_one,
        scale_one,
        pixel_weight,
        pixel_count,
        gain_mid[0],
        nothing,
    )
    grad_first = grad_first.astype(jnp.bfloat16)
    grad_inputs = grad_residual + product_outer(grad_first, w_reduce)
    reduce_part = product_inner(inputs, grad_first)
    spatial_part = big_taps + small_taps
    reduce_grad, spatial_grad, expand_grad = (
        lax.psum_scatter(reduce_part, "dp", scatter_dimension=0, tiled=True),
        lax.psum_scatter(spatial_part, "dp", scatter_dimension=0, tiled=True),
        lax.psum_scatter(expand_part, "dp", scatter_dimension=0, tiled=True),
    )
    grad_big = grad_inputs[:big_pixels].reshape(big_crops.shape).astype(jnp.bfloat16)
    grad_small = grad_inputs[big_pixels:].reshape(small_crops.shape).astype(jnp.bfloat16)
    return (
        loss,
        grad_big,
        grad_small,
        reduce_grad,
        spatial_grad,
        expand_grad,
        jnp.stack([gain_one, gain_two]),
        jnp.stack([bias_one, bias_two]),
        gain_three,
        bias_three,
        hidden_grad,
        gain_head_grad,
        bias_head_grad,
        project_grad,
        proto_grad,
    )


def solution(mesh):
    placed = (
        P("dp", None, None, None),
        P("dp", None, None, None),
        P("dp"),
        P(),
        P(),
        P(),
        P(),
        P(),
        P(),
        P(),
        P(),
        P(),
        P(),
        P(),
        P(),
        P(None, "dp", None),
    )
    return jax.shard_map(
        local,
        mesh=mesh,
        in_specs=placed,
        out_specs=(
            P(),
            P("dp", None, None, None),
            P("dp", None, None, None),
            P("dp", None),
            P("dp", None, None),
            P("dp", None),
            P(),
            P(),
            P(),
            P(),
            P("dp", None),
            P(),
            P(),
            P("dp", None),
            P("dp", None),
        ),
        check_vma=False,
    )
```

profile of v0, /device:TPU:0, one launch (start us, length us, event | category | flops | bytes accessed | tf_op | source)
XLA Modules:
  0.0 1721.1 jit_solution(2789913338056792144)
XLA Ops:
  14.0 9.1 copy.82
  23.1 12.5 reshape.315
  35.6 9.4 copy.81
  44.9 9.9 reshape.314
  61.3 8.0 multiply_reduce_fusion.6
  69.3 42.0 %all-reduce.29 = (f32[512]{0:T(512)S(1)}, f32[]{:T(128)}) all-reduce(f32[512]{0:T(512)S(1)} %get-tuple-element.117, f32[]{:T(128)S(6)} %convert_element_type.112), channel_id=1, replica_groups=mesh['dp'=32] {'dp'}, use_global_device_ids=true, to_apply=%region_1.0 | all-reduce | flops 513 | bytes 4104 | tf_op jit(solution)/shard_map/psum | solution.py:38
  115.2 40.6 %psum.149 = f32[512]{0:T(512)S(1)} all-reduce(f32[512]{0:T(512)S(1)} %fusion.5), channel_id=1, replica_groups=mesh['dp'=32] {'dp'}, use_global_device_ids=true, to_apply=%region_5.0 | all-reduce | flops 512 | bytes 4096 | tf_op jit(solution)/shard_map/psum | solution.py:42
  169.0 13.0 pad_slice_fusion
  224.4 5.9 pad_slice_fusion.8
  285.3 40.0 %psum.150 = f32[512]{0:T(512)S(1)} all-reduce(f32[512]{0:T(512)S(1)} %multiply_reduce_fusion.5), channel_id=1, replica_groups=mesh['dp'=32] {'dp'}, use_global_device_ids=true, to_apply=%region_7.8 | all-reduce | flops 512 | bytes 4096 | tf_op jit(solution)/shard_map/psum | solution.py:38
  328.7 40.3 %psum.151 = f32[512]{0:T(512)S(1)} all-reduce(f32[512]{0:T(512)S(1)} %fusion.6), channel_id=1, replica_groups=mesh['dp'=32] {'dp'}, use_global_device_ids=true, to_apply=%region_9.10 | all-reduce | flops 512 | bytes 4096 | tf_op jit(solution)/shard_map/psum | solution.py:42
  369.6 13.7 multiply_reduce_fusion.1
  383.4 40.0 %psum.152 = f32[2048]{0:T(1024)S(1)} all-reduce(f32[2048]{0:T(1024)S(1)} %get-tuple-element.119), channel_id=1, replica_groups=mesh['dp'=32] {'dp'}, use_global_device_ids=true, to_apply=%region_11.12 | all-reduce | flops 2048 | bytes 16384 | tf_op jit(solution)/shard_map/psum | solution.py:38
  423.3 9.3 fusion.2
  432.7 40.2 %psum.153 = f32[2048]{0:T(1024)S(1)} all-reduce(f32[2048]{0:T(1024)S(1)} %fusion.2), channel_id=1, replica_groups=mesh['dp'=32] {'dp'}, use_global_device_ids=true, to_apply=%region_13.14 | all-reduce | flops 2048 | bytes 16384 | tf_op jit(solution)/shard_map/psum | solution.py:42
  474.1 20.8 %fusion.4 = f32[2720,2048]{1,0:T(8,128)} fusion(bf16[2720,2048]{1,0:T(8,128)(2,1)} %copy-done.6, f32[2048]{0:T(1024)S(1)} %copy-done.82, f32[2048]{0:T(1024)S(1)} %copy-done.70, f32[2048]{0:T(1024)S(1)} %get-tuple-element.85, f32[2720,2048]{1,0:T(8,128)} %get-tuple-element.120, f32[2048]{0:T(1024)S(1)} %broadcast_divide_fusion.5), kind=kLoop, calls=%fused_computation.10 | loop fusion | flops 55705600 | bytes 55738368 | tf_op jit(solution)/shard_map/jit(silu)/mul | solution.py:155
  494.9 8.7 slice.232
  503.6 11.5 slice.231
  516.0 10.1 reshape.335
  526.1 7.3 reduce_sum.393
  534.2 11.2 reshape.336
  545.3 9.8 reduce_sum.394
  555.3 5.2 multiply_reduce_fusion.11
  560.5 40.0 %psum.154 = f32[2048]{0:T(1024)S(1)} all-reduce(f32[2048]{0:T(1024)S(1)} %get-tuple-element.121), channel_id=1, replica_groups=mesh['dp'=32] {'dp'}, use_global_device_ids=true, to_apply=%region_17.18 | all-reduce | flops 2048 | bytes 16384 | tf_op jit(solution)/shard_map/psum | solution.py:38
  600.8 40.3 %psum.155 = f32[2048]{0:T(1024)S(1)} all-reduce(f32[2048]{0:T(1024)S(1)} %fusion.35), channel_id=1, replica_groups=mesh['dp'=32] {'dp'}, use_global_device_ids=true, to_apply=%region_19.20 | all-reduce | flops 2048 | bytes 16384 | tf_op jit(solution)/shard_map/psum | solution.py:42
  649.2 40.1 %psum.156 = f32[2,3000]{1,0:T(2,128)S(1)} all-reduce(f32[2,3000]{1,0:T(2,128)S(1)} %add.368), channel_id=1, replica_groups=mesh['dp'=32] {'dp'}, use_global_device_ids=true, to_apply=%region_24.25 | all-reduce | flops 6000 | bytes 48000 | tf_op jit(solution)/shard_map/psum | solution.py:193
  692.8 40.9 %psum.157 = f32[2,3000]{1,0:T(2,128)S(1)} all-reduce(f32[2,3000]{1,0:T(2,128)S(1)} %add.369), channel_id=1, replica_groups=mesh['dp'=32] {'dp'}, use_global_device_ids=true, to_apply=%region_29.30 | all-reduce | flops 6000 | bytes 48000 | tf_op jit(solution)/shard_map/psum | solution.py:193
  737.0 40.0 %psum.158 = f32[2,3000]{1,0:T(2,128)S(1)} all-reduce(f32[2,3000]{1,0:T(2,128)S(1)} %add.370), channel_id=1, replica_groups=mesh['dp'=32] {'dp'}, use_global_device_ids=true, to_apply=%region_34.35 | all-reduce | flops 6000 | bytes 48000 | tf_op jit(solution)/shard_map/psum | solution.py:193
  806.2 40.8 %all-reduce.28 = (f32[2048]{0:T(1024)S(1)}, f32[2048]{0:T(1024)S(1)}) all-reduce(f32[2048]{0:T(1024)S(1)} %get-tuple-element.67, f32[2048]{0:T(1024)S(1)} %get-tuple-element.66), channel_id=1, replica_groups=mesh['dp'=32] {'dp'}, use_global_device_ids=true, to_apply=%region_50.51 | all-reduce | flops 4096 | bytes 32768 | tf_op jit(solution)/shard_map/psum | solution.py:49
  848.8 6.6 fusion.207
  855.5 7.1 broadcast_in_dim.49
  862.6 10.0 reshape.339
  872.6 7.8 broadcast_in_dim.50
  880.5 11.5 reshape.340
  892.0 29.5 %multiply_reduce_fusion.2 = (f32[2048]{0:T(1024)S(1)}, f32[2048]{0:T(1024)S(1)}, f32[2720,2048]{1,0:T(8,128)}) fusion(f32[2720]{0:T(1024)S(1)} %concatenate.23, f32[2048]{0:T(1024)S(1)} %copy-done.65, f32[2720,2048]{1,0:T(8,128)} %get-tuple-element.120, f32[2048]{0:T(1024)S(1)} %broadcast_divide_fusion.5, bf16[2720,2048]{1,0:T(8,128)(2,1)} %copy-done.6, ...), kind=kLoop, calls=%fused_computation.13 | loop fusion | flops 105836544 | bytes 78047872 | tf_op jit(solution)/shard_map/reduce_sum | solution.py:50
  921.5 40.1 %all-reduce.27 = (f32[2048]{0:T(1024)S(1)}, f32[2048]{0:T(1024)S(1)}) all-reduce(f32[2048]{0:T(1024)S(1)} %get-tuple-element.61, f32[2048]{0:T(1024)S(1)} %get-tuple-element.60), channel_id=1, replica_groups=mesh['dp'=32] {'dp'}, use_global_device_ids=true, to_apply=%region_54.55 | all-reduce | flops 4096 | bytes 32768 | tf_op jit(solution)/shard_map/psum | solution.py:49
  961.7 16.9 multiply_convert_fusion
  982.7 8.3 fusion.191
  995.5 14.5 multiply_reduce_fusion.8
  1010.0 40.5 %all-reduce.26 = (f32[512]{0:T(512)S(1)}, f32[512]{0:T(512)S(1)}) all-reduce(f32[512]{0:T(512)S(1)} %get-tuple-element.65, f32[512]{0:T(512)S(1)} %get-tuple-element.64), channel_id=1, replica_groups=mesh['dp'=32] {'dp'}, use_global_device_ids=true, to_apply=%region_58.59 | all-reduce | flops 1024 | bytes 8192 | tf_op jit(solution)/shard_map/psum | solution.py:49
  1050.5 5.5 multiply_convert_fusion.2
  1112.7 8.1 pad_add_fusion.1
  1120.9 6.2 slice_add_fusion
  1128.3 5.7 copy.93
  1134.0 4.7 reshape.341
  1153.4 4.7 fusion.50
  1158.1 4.6 fusion.54
  1162.7 5.4 slice_add_fusion.4
  1176.4 8.4 multiply_reduce_fusion.7
  1184.8 39.5 %all-reduce.25 = (f32[]{:T(128)}, f32[512]{0:T(512)S(1)}, f32[512]{0:T(512)S(1)}) all-reduce(f32[]{:T(128)S(6)} %div.330, f32[512]{0:T(512)S(1)} %get-tuple-element.63, f32[512]{0:T(512)S(1)} %get-tuple-element.62), channel_id=1, replica_groups=mesh['dp'=32] {'dp'}, use_global_device_ids=true, to_apply=%region_43.44 | all-reduce | flops 1025 | bytes 8200 | tf_op jit(solution)/shard_map/psum | solution.py:49
  1224.4 5.2 multiply_convert_fusion.1
  1231.1 10.4 fusion.208
  1275.5 12.5 add.394
  1289.3 8.2 fusion.94
  1297.6 14.4 add_convert_fusion
  1312.0 5.2 slice.251
  1317.2 6.7 slice.250
  1324.0 9.8 convert_element_type.128
  1333.8 10.3 copy.104
  1344.1 12.0 convert_element_type.129
  1356.1 8.4 copy.105
  1367.3 15.9 reduce-scatter.6.cloned.1.call-done
  1383.2 149.4 %reduce-scatter.8.cloned.1.call-done = f32[16,9,512]{2,0,1:T(8,128)} async-done(((f32[512,9,512]{2,0,1:T(8,128)}), f32[16,9,512]{2,0,1:T(8,128)}) %reduce-scatter.8.cloned.1.call-update) | async-done | bytes 294928 | tf_op jit(solution)/shard_map/reduce_scatter | solution.py:283
  1532.5 181.5 %reduce-scatter.12.cloned.1.call-done = f32[64,2048]{1,0:T(8,128)} async-done(((f32[2048,2048]{1,0:T(8,128)}), f32[64,2048]{1,0:T(8,128)}) %reduce-scatter.12.cloned.1.call-update) | async-done | bytes 524304 | tf_op jit(solution)/shard_map/reduce_scatter | solution.py:230
  (449 shorter events, 306.6 us)
Async XLA Ops:
  7.2 362.4 %copy-start = (bf16[512,2048]{1,0:T(8,128)(2,1)S(1)}, bf16[512,2048]{1,0:T(8,128)(2,1)}, u32[]{:S(2)}) copy-start(bf16[512,2048]{1,0:T(8,128)(2,1)} %param.21) | copy-start | bytes 6291460
  7.2 1358.6 %all-reduce.32.cloned.1.call-start = ((), (), s32[]{:S(2)}) async-start(), calls=%async_computation.10 | async-start | bytes 3145728
  12.1 144.3 %copy-start.75 = (f32[1,512]{1,0:T(1,128)}, f32[1,512]{1,0:T(1,128)S(1)}, u32[]{:S(2)}) copy-start(f32[1,512]{1,0:T(1,128)S(1)} %get-tuple-element.111) | copy-start | bytes 6148
  12.1 357.5 %copy-start.98 = (f32[1,512]{1,0:T(1,128)}, f32[1,512]{1,0:T(1,128)S(1)}, u32[]{:S(2)}) copy-start(f32[1,512]{1,0:T(1,128)S(1)} %get-tuple-element.112) | copy-start | bytes 6148
  12.8 143.5 %copy-start.84 = (f32[1,512]{1,0:T(1,128)}, f32[1,512]{1,0:T(1,128)S(1)}, u32[]{:S(2)}) copy-start(f32[1,512]{1,0:T(1,128)S(1)} %get-tuple-element.113) | copy-start | bytes 6148
  12.9 356.8 %copy-start.111 = (f32[1,512]{1,0:T(1,128)}, f32[1,512]{1,0:T(1,128)S(1)}, u32[]{:S(2)}) copy-start(f32[1,512]{1,0:T(1,128)S(1)} %get-tuple-element.114) | copy-start | bytes 6148
  61.3 8.0 copy-start.6
  111.9 44.4 %copy-start.73 = (f32[512]{0:T(512)}, f32[512]{0:T(512)S(1)}, u32[]{:S(2)}) copy-start(f32[512]{0:T(512)S(1)} %broadcast_divide_fusion.9) | copy-start | bytes 6148
  196.6 22.1 %copy-start.52 = (bf16[1152,512]{1,0:T(8,128)(2,1)}, bf16[1152,512]{1,0:T(8,128)(2,1)S(1)}, u32[]{:S(2)}) copy-start(bf16[1152,512]{1,0:T(8,128)(2,1)S(1)} %reshape.330) | copy-start | bytes 3538948
  256.6 6.5 slice-start
  275.5 6.2 copy-start.7
  369.6 13.7 copy-start.106
  423.3 49.5 %copy-start.70 = (f32[2048]{0:T(1024)S(1)}, f32[2048]{0:T(1024)}, u32[]{:S(2)}) copy-start(f32[2048]{0:T(1024)} %param.24) | copy-start | bytes 24580
  423.3 50.7 %copy-start.82 = (f32[2048]{0:T(1024)S(1)}, f32[2048]{0:T(1024)}, u32[]{:S(2)}) copy-start(f32[2048]{0:T(1024)} %param.25) | copy-start | bytes 24580
  503.6 11.5 copy-start.72
  545.3 9.9 copy-start.88
  555.3 85.8 %copy-start.77 = (f32[2048]{0:T(1024)S(1)}, f32[2048]{0:T(1024)}, u32[]{:S(2)}) copy-start(f32[2048]{0:T(1024)} %param.27) | copy-start | bytes 24580
  555.3 87.0 %copy-start.93 = (f32[2048]{0:T(1024)S(1)}, f32[2048]{0:T(1024)}, u32[]{:S(2)}) copy-start(f32[2048]{0:T(1024)} %param.28) | copy-start | bytes 24580
  560.5 87.0 %copy-start.30 = (f32[160,2048]{1,0:T(8,128)}, f32[160,2048]{1,0:T(8,128)S(1)}, u32[]{:S(2)}) copy-start(f32[160,2048]{1,0:T(8,128)S(1)} %get-tuple-element.122) | copy-start | bytes 3932164
  600.5 41.2 %copy-start.62 = (f32[2048]{0:T(1024)}, f32[2048]{0:T(1024)S(1)}, u32[]{:S(2)}) copy-start(f32[2048]{0:T(1024)S(1)} %broadcast_divide_fusion.3) | copy-start | bytes 24580
  734.2 43.5 %copy-start.110 = (f32[16]{0:T(128)S(1)}, f32[16]{0:T(128)}, u32[]{:S(2)}) copy-start(f32[16]{0:T(128)} %get-tuple-element.91) | copy-start | bytes 196
  736.5 47.7 %copy-start.103 = (f32[128]{0:T(128)S(1)}, f32[128]{0:T(128)}, u32[]{:S(2)}) copy-start(f32[128]{0:T(128)} %copy-done.102) | copy-start | bytes 1540
  782.2 8.7 copy-start.92
  797.5 5.6 copy-start.31
  797.5 569.7 %reduce-scatter.14.cloned.1.call-start = ((), (), s32[]{:S(2)}) async-start(), calls=%async_computation.9 | async-start | bytes 1081344 | tf_op jit(solution)/shard_map/reduce_scatter | solution.py:231
  803.0 44.0 %copy-start.63 = (f32[2048]{0:T(1024)S(1)}, f32[2048]{0:T(1024)}, u32[]{:S(2)}) copy-start(f32[2048]{0:T(1024)} %copy-done.62) | copy-start | bytes 24580
  803.1 44.0 %copy-start.67 = (f32[2048]{0:T(1024)S(1)}, f32[2048]{0:T(1024)}, u32[]{:S(2)}) copy-start(f32[2048]{0:T(1024)} %copy-done.66) | copy-start | bytes 24580
  803.1 44.0 %copy-start.79 = (f32[2048]{0:T(1024)S(1)}, f32[2048]{0:T(1024)}, u32[]{:S(2)}) copy-start(f32[2048]{0:T(1024)} %get-tuple-element.87) | copy-start | bytes 24580
  803.1 44.0 %copy-start.89 = (f32[160]{0:T(256)S(1)}, f32[160]{0:T(256)}, u32[]{:S(2)}) copy-start(f32[160]{0:T(256)} %concatenate.26) | copy-start | bytes 1924
  803.1 564.2 %reduce-scatter.10.cloned.1.call-start = ((), (), s32[]{:S(2)}) async-start(), calls=%async_computation.7 | async-start | bytes 4325376 | tf_op jit(solution)/shard_map/reduce_scatter | solution.py:284
  847.0 8.4 copy-start.94
  847.0 8.4 copy-start.96
  848.8 6.6 copy-start.40
  880.5 11.5 copy-start.65
  880.5 11.5 copy-start.71
  880.5 11.5 copy-start.83
  892.0 69.6 %copy-start.78 = (f32[2048]{0:T(1024)S(1)}, f32[2048]{0:T(1024)}, u32[]{:S(2)}) copy-start(f32[2048]{0:T(1024)} %get-tuple-element.84) | copy-start | bytes 24580
  961.6 17.0 copy-start.95
  961.6 17.0 copy-start.97
  961.6 21.1 %copy-start.5 = (f32[1568,512]{1,0:T(8,128)S(1)}, f32[1568,512]{1,0:T(8,128)}, u32[]{:S(2)}) copy-start(f32[1568,512]{1,0:T(8,128)} %copy-done.4) | copy-start | bytes 9633796
  961.6 21.1 %copy-start.8 = (f32[1152,512]{1,0:T(8,128)S(1)}, f32[1152,512]{1,0:T(8,128)}, u32[]{:S(2)}) copy-start(f32[1152,512]{1,0:T(8,128)} %copy-done.7) | copy-start | bytes 7077892
  961.7 21.1 %copy-start.99 = (f32[1,512]{1,0:T(1,128)S(1)}, f32[1,512]{1,0:T(1,128)}, u32[]{:S(2)}) copy-start(f32[1,512]{1,0:T(1,128)} %copy-done.98) | copy-start | bytes 6148
  961.7 21.0 %copy-start.107 = (f32[512]{0:T(512)S(1)}, f32[512]{0:T(512)}, u32[]{:S(2)}) copy-start(f32[512]{0:T(512)} %copy-done.106) | copy-start | bytes 6148
  961.7 21.0 %copy-start.112 = (f32[1,512]{1,0:T(1,128)S(1)}, f32[1,512]{1,0:T(1,128)}, u32[]{:S(2)}) copy-start(f32[1,512]{1,0:T(1,128)} %copy-done.111) | copy-start | bytes 6148
  991.1 392.1 %reduce-scatter.6.cloned.1.call-start = ((), (), s32[]{:S(2)}) async-start(), calls=%async_computation.5 | async-start | bytes 4325376 | tf_op jit(solution)/shard_map/reduce_scatter | solution.py:282
  995.5 55.0 %copy-start.105 = (f32[512]{0:T(512)S(1)}, f32[512]{0:T(512)}, u32[]{:S(2)}) copy-start(f32[512]{0:T(512)} %get-tuple-element.82) | copy-start | bytes 6148
  1058.0 13.7 slice-start.2
  1063.4 8.3 slice-start.3
  1095.5 9.7 copy-start.43
  1107.4 13.4 slice-start.10
  1109.2 11.6 slice-start.6
  1109.3 11.6 slice-start.8
  1112.7 8.1 slice-start.7
  1112.7 8.2 slice-start.9
  1112.7 8.2 slice-start.11
  1112.7 8.2 copy-start.29
  1120.9 6.2 copy-start.114
  1138.7 7.8 slice-start.4
  1176.4 48.0 %copy-start.104 = (f32[512]{0:T(512)S(1)}, f32[512]{0:T(512)}, u32[]{:S(2)}) copy-start(f32[512]{0:T(512)} %get-tuple-element.79) | copy-start | bytes 6148
  1241.6 291.0 %reduce-scatter.8.cloned.1.call-start = ((), (), s32[]{:S(2)}) async-start(), calls=%async_computation.6 | async-start | bytes 9732096 | tf_op jit(solution)/shard_map/reduce_scatter | solution.py:283
  1255.4 11.6 copy-start.34
  1288.1 426.0 %reduce-scatter.12.cloned.1.call-start = ((), (), s32[]{:S(2)}) async-start(), calls=%async_computation.8 | async-start | bytes 17301504 | tf_op jit(solution)/shard_map/reduce_scatter | solution.py:230
  1356.1 8.5 copy-start.101
  1356.1 9.0 copy-start.109
  (69 other events, 172.1 us)
Sparse Core Ops, SparseCore 0:
  797.7 132.1 all-reduce.31
  932.7 133.9 reduce-scatter.13
  1069.6 136.8 reduce-scatter.9
  1241.7 141.4 reduce-scatter.5
  1386.0 146.4 reduce-scatter.7
  1535.3 178.6 reduce-scatter.11
where the time goes:
time: 1730 us; the launch traced here: 1720 us
  blocking collectives  605 us (35%)
  waiting for transfers between devices  347 us (20%)
  local copies, waits for them, and re-layouts  342 us (20%)
  matrix products  216 us (12%)
  other arithmetic  193 us (11%)
  between operations  18.3 us (1%)
    reduce_scatter x1, waiting for transfers between devices, local(): lax.psum_scatter(hidden_part, 'dp', scatter_dimension=0, tiled=True)  181 us
    psum x4, blocking collectives, forward_norm(): total, extra_sum = lax.psum((jnp.sum(weighted, axis=0), extra), 'dp')  162 us
    psum x4, blocking collectives, forward_norm(): lax.psum(jnp.sum(weight[:, None] * centered * centered, axis=0), 'dp')  161 us
    psum x4, blocking collectives, backward_norm(): lax.psum((jnp.sum(weighted, axis=0), jnp.sum(weighted * normed, axis=0),...  161 us
    reduce_scatter x1, waiting for transfers between devices, local(): lax.psum_scatter(spatial_part, 'dp', scatter_dimension=0, tiled=True)  149 us
    psum x3, blocking collectives, local(): lax.psum(jnp.sum(batch_exp, axis=1) + jnp.sum(queue_exp, axis=1), 'dp')  121 us
    unnamed x260, local copies, waits for them, and re-layouts  70.8 us
    dot_general x15, matrix products, product_outer(): lax.dot_general(left, right, (((1,), (1,)), ((), ())), preferred_element_...  67.4 us
  transfers between devices with their start and end apart: 6, of which 3 were waited for; matrix products, arithmetic and copies ran while one was open for 23% of the time, Pallas kernels for 0%

commit v1 on v0

v1 whole, which is shorter than its diff:
```python
import math

import jax
import jax.numpy as jnp
from jax import lax
from jax.experimental import pallas as pl
from jax.experimental.pallas import tpu as pltpu
from jax.sharding import PartitionSpec as P

ITERS = 3

EPS_NORM = 1e-05
EPS_UNIT = 1e-06
EPS_CODE = 0.05
SOFTMAX_HEAT = 0.1
LANES = 128
PLANE = 8
CHUNK = 512
TILE = 256
ROWS = 32
VMEM_LIMIT = 60 << 20
FLOAT = jnp.float32
HALF = jnp.bfloat16


def product(left, right):
    return jnp.dot(left, right, preferred_element_type=FLOAT)


def product_inner(left, right):
    return lax.dot_general(left, right, (((0,), (0,)), ((), ())), preferred_element_type=FLOAT)


def product_outer(left, right):
    return lax.dot_general(left, right, (((1,), (1,)), ((), ())), preferred_element_type=FLOAT)


def sigmoid(value):
    return 0.5 * jnp.tanh(0.5 * value) + 0.5


def silu(value):
    return value * sigmoid(value)


def slope(value):
    gate = sigmoid(value)
    return gate * (1.0 + value * (1.0 - gate))


def column_sum(value):
    return jnp.sum(value, axis=0, keepdims=True)


def shape(dims, dtype=FLOAT):
    return jax.ShapeDtypeStruct(dims, dtype)


def far_shape(dims, dtype=FLOAT):
    return pltpu.HBM(dims, dtype)


def far(array):
    return pltpu.with_memory_space_constraint(array, pltpu.HBM)


def whole(dims):
    return pl.BlockSpec(dims, lambda *_: (0,) * len(dims))


def call(
    kernel,
    out_shape,
    args,
    grid=None,
    in_specs=None,
    out_specs=None,
    flops=0,
    after=(),
    scalars=(),
    streamed=(),
    aliases=None,
    spill=0,
):
    flat = out_shape if isinstance(out_shape, (list, tuple)) else [out_shape]
    size = sum(a.size * a.dtype.itemsize for a in args)
    size += sum(math.prod(a.shape) * jnp.dtype(a.dtype).itemsize for a in flat)
    args = [far(a) if k in streamed else a for k, a in enumerate(args)]
    here = pl.BlockSpec(memory_space=pltpu.VMEM)
    limit = spill
    if grid is None:
        in_specs = [here] * len(args)
        out_specs = jax.tree.map(lambda _: here, out_shape)
        limit = max(limit, size + size // 4 + (2 << 20))
    else:
        limit = 20 << 20
    first, last = len(scalars), len(scalars) + len(args)

    def run(*refs):
        kernel(*refs[:last], *refs[last + len(after) :])

    specs = dict(out_specs=out_specs)
    if grid is not None:
        specs["grid"] = grid
    return pl.pallas_call(
        run,
        out_shape=out_shape,
        in_specs=[pl.BlockSpec(memory_space=pltpu.SMEM)] * first
        + list(in_specs)
        + [pl.BlockSpec(memory_space=pl.ANY)] * len(after),
        input_output_aliases={first + k: v for k, v in (aliases or {}).items()},
        compiler_params=pltpu.CompilerParams(vmem_limit_bytes=min(limit, VMEM_LIMIT)),
        cost_estimate=pl.CostEstimate(flops=flops, bytes_accessed=size, transcendentals=0),
        **specs,
    )(*scalars, *args, *after)


def copy_kernel(source, out):
    out[...] = source[...]


def tie(value, after):
    return call(copy_kernel, shape(value.shape, value.dtype), [value], after=after)


def rounds(devices):
    bits = [1 << k for k in range(devices.bit_length() - 1)]
    return [bits[:1]] + [bits[k : k + 2] for k in range(1, len(bits), 2)]


def peers(value, bits, devices):
    masks = [0]
    for bit in bits:
        masks = masks + [mask | bit for mask in masks]
    return [value] + [
        lax.ppermute(value, "dp", [(i, i ^ mask) for i in range(devices)]) for mask in masks[1:]
    ]


def tree(values):
    while len(values) > 1:
        values = [values[k] + values[k + 1] for k in range(0, len(values), 2)]
    return values[0]


def exchange(value, devices, merge, works=()):
    first, *others = rounds(devices)
    parts = peers(value, first, devices)
    for k, bits in enumerate(others):
        value = merge(parts)
        parts = peers(value, bits, devices)
        if k < len(works):
            parts[0] = tie(value, works[k](value))
    return parts


def sum_parts(value, devices, works=()):
    return exchange(value, devices, tree, works)


def merged(parts):
    channels = (parts[0].shape[1] - LANES) // 2
    counts = [part[:, 2 * channels : 2 * channels + 1] for part in parts]
    means = [part[:, :channels] for part in parts]
    spreads = [part[:, channels : 2 * channels] for part in parts]
    total = tree(counts)
    mean = tree([c * m for c, m in zip(counts, means)]) / total
    spread = tree([s + c * jnp.square(m - mean) for s, c, m in zip(spreads, counts, means)])
    return total, mean, spread


def merge_kernel(*refs):
    *parts, out = refs
    channels = (out.shape[1] - LANES) // 2
    total, mean, spread = merged([part[...] for part in parts])
    out[:, :channels] = mean
    out[:, channels : 2 * channels] = spread
    out[:, 2 * channels :] = jnp.broadcast_to(total, (1, LANES))


def merge_norms(parts):
    return call(merge_kernel, shape(parts[0].shape), parts)


def settle_kernel(*refs):
    *parts, gain, bias, scale, offset, mean_out, root_out, count = refs
    total, mean, spread = merged([part[...] for part in parts])
    root = lax.rsqrt(spread / total + EPS_NORM)
    factor = gain[...] * root
    scale[...] = factor
    offset[...] = bias[...] - mean * factor
    mean_out[...] = mean
    root_out[...] = root
    count[...] = jnp.broadcast_to(total, (1, LANES))


def settle_norm(packed, gain, bias, devices):
    channels = gain.shape[0]
    parts = exchange(packed, devices, merge_norms)
    row = shape((1, channels))
    return call(
        settle_kernel,
        [row, row, row, row, shape((1, LANES))],
        [*parts, gain[None], bias[None]],
    )


def settle_back_kernel(*refs):
    *parts, gain, mean, root, count, first, second, third, gain_sum, bias_sum, extra = refs
    channels = gain.shape[1]
    packed = tree([part[...] for part in parts])
    total = count[:, :1]
    low, high = packed[:, :channels], packed[:, channels : 2 * channels]
    factor = gain[...] * root[...]
    pull = root[...] * high / total
    first[...] = factor
    second[...] = factor * (mean[...] * pull - low / total)
    third[...] = -factor * pull
    gain_sum[...] = high
    bias_sum[...] = low
    extra[...] = packed[:, 2 * channels :]


def settle_back(packed, gain, mean, root, count, devices, works=()):
    parts = sum_parts(packed, devices, works)
    row = shape((1, gain.shape[0]))
    return call(
        settle_back_kernel,
        [row, row, row, row, row, shape((1, LANES))],
        [*parts, gain[None], mean, root, count],
    )


def pick(bits, place):
    return (bits[0] >> place) & 1


def send_kernel(bits, value, send):
    other = 1 - pick(bits, 0)

    def step(t, _):
        for k in range(send.shape[1]):
            send[t, k] = value[t, 2 * k + other]
        return _

    lax.fori_loop(0, value.shape[0], step, 0)


def send_rows(value, me, after):
    taps, devices, rows, width = value.shape
    out = shape((taps, devices // 2, rows, width))
    return call(send_kernel, out, [value], scalars=[me], after=after)


def first_kernel(bits, keep, got, keep_one, send_one, keep_two, send_two):
    taps, blocks, _, width = got.shape
    uncut = keep.shape[1] // blocks
    half = pick(bits, 0) * (uncut - 1)
    left, right = slice(0, width // 2), slice(width // 2, width)
    one, two = pick(bits, 1), pick(bits, 2)

    def step(t, _):
        for k in range(blocks // 2):
            for out, there in ((keep_one, 2 * k + one), (send_one, 2 * k + 1 - one)):
                out[t, k] = keep[t, uncut * there + half, :, left] + got[t, there, :, left]
            low = 4 * (k // 2) + k % 2
            for out, there in ((keep_two, low + 2 * two), (send_two, low + 2 * (1 - two))):
                out[t, k] = keep[t, uncut * there + half, :, right] + got[t, there, :, right]
        return _

    lax.fori_loop(0, taps, step, 0)


def second_kernel(bits, keep_one, got_one, keep_two, got_two, *outs):
    def step(t, _):
        for keep, got, place, out_keep, out_send in (
            (keep_one, got_one, 2, outs[0], outs[1]),
            (keep_two, got_two, 1, outs[2], outs[3]),
        ):
            half = pick(bits, place)
            for k in range(out_keep.shape[1]):
                out_keep[t, k] = keep[t, 2 * k + half] + got[t, 2 * k + half]
                out_send[t, k] = keep[t, 2 * k + 1 - half] + got[t, 2 * k + 1 - half]
        return _

    lax.fori_loop(0, keep_one.shape[0], step, 0)


def third_kernel(bits, keep_one, got_one, keep_two, got_two, out_keep, out_send):
    half = pick(bits, 3)
    width = keep_one.shape[3]

    def step(t, _):
        for k in range(out_keep.shape[1]):
            for out, there in ((out_keep, 2 * k + half), (out_send, 2 * k + 1 - half)):
                out[t, k, :, :width] = keep_one[t, there] + got_one[t, there]
                out[t, k, :, width:] = keep_two[t, there] + got_two[t, there]
        return _

    lax.fori_loop(0, keep_one.shape[0], step, 0)


def later_kernel(place, bits, keep, got, out_keep, out_send):
    half = pick(bits, place)

    def step(t, _):
        for k in range(out_keep.shape[1]):
            for out, there in ((out_keep, 2 * k + half), (out_send, 2 * k + 1 - half)):
                out[t, k] = keep[t, there] + got[t, there]
        return _

    lax.fori_loop(0, keep.shape[0], step, 0)


def last_kernel(keep, got, out):
    out[...] = keep[...] + got[...]


class Scatter:
    def __init__(self, keep, send, devices, me):
        self.devices, self.me = devices, me
        self.bits = devices.bit_length() - 1
        self.held = [keep]
        self.got = [self.cross(send, 0)]
        self.stage = 0

    def cross(self, value, place):
        return lax.ppermute(
            value, "dp", [(i, i ^ (1 << place)) for i in range(self.devices)]
        )

    def go(self, after=()):
        taps, blocks, rows, width = self.got[0].shape
        if self.stage == 0:
            out = shape((taps, blocks // 2, rows, width // 2))
            kernel, places = first_kernel, (1, 2)
        elif self.stage == 1:
            out = shape((taps, blocks // 2, rows, width))
            kernel, places = second_kernel, (2, 1)
        elif self.stage == 2:
            out = shape((taps, blocks // 2, rows, 2 * width))
            kernel, places = third_kernel, (3,)
        else:
            place = self.stage + 1
            out = shape((taps, blocks // 2, rows, width))
            kernel, places = (lambda *refs: later_kernel(place, *refs)), (place,)
        args = [a for pair in zip(self.held, self.got) for a in pair]
        made = call(kernel, [out] * (2 * len(places)), args, after=after, scalars=[self.me])
        self.held = list(made[::2])
        self.got = [self.cross(send, place) for send, place in zip(made[1::2], places)]
        self.stage += 1
        return self.held[0]

    def complete(self):
        return self.got[0].shape[1] == 1

    def end(self):
        while not self.complete():
            self.go()
        taps, _, rows, width = self.held[0].shape
        done = call(last_kernel, shape(self.held[0].shape), [self.held[0], self.got[0]])
        return done.reshape(taps, rows, width)


def weight_grad_kernel(rows, bits, left_big, right_big, left_small, right_small, keep, send):
    value = product_inner(left_big[...], right_big[...])
    value = value + product_inner(left_small[...], right_small[...])
    half = pick(bits, 0)
    for k in range(value.shape[0] // (2 * rows)):
        even = value[2 * k * rows : (2 * k + 1) * rows]
        odd = value[(2 * k + 1) * rows : (2 * k + 2) * rows]
        keep[0, k] = jnp.where(half == 0, even, odd)
        send[0, k] = jnp.where(half == 0, odd, even)


def weight_grad(left, right, devices, me, along, after=(), streamed=()):
    height, width = left[0].shape[1], right[0].shape[1]
    rows = height // devices
    out = shape((1, devices // 2, rows, width))

    def spec(pair, k, moves):
        dims = (pair[k].shape[0], CHUNK if moves else pair[k].shape[1])
        return pl.BlockSpec(dims, lambda j: (0, j if moves else 0))

    if along == 0:
        steps = height // CHUNK
        block = pl.BlockSpec((1, devices // 2 // steps, rows, width), lambda j: (0, j, 0, 0))
    else:
        steps = width // CHUNK
        block = pl.BlockSpec((1, devices // 2, rows, CHUNK), lambda j: (0, 0, 0, j))
    return call(
        lambda *refs: weight_grad_kernel(rows, *refs),
        [out, out],
        [left[0], right[0], left[1], right[1]],
        grid=(steps,),
        in_specs=[
            spec(left, 0, along == 0),
            spec(right, 0, along == 1),
            spec(left, 1, along == 0),
            spec(right, 1, along == 1),
        ],
        out_specs=[block, block],
        flops=2 * (left[0].shape[0] + left[1].shape[0]) * height * width,
        after=after,
        streamed=streamed,
        scalars=[me],
    )


class Rows:
    def __init__(self, big_side, big_crops, small_side, small_crops):
        self.steps = big_side, small_side
        self.rows = big_side * big_crops, small_side * small_crops
        self.crops = big_crops, small_crops

    def specs(self, channels):
        first = self.steps[0]
        return [
            pl.BlockSpec((self.rows[0], channels), lambda i: (jnp.minimum(i, first - 1), 0)),
            pl.BlockSpec((self.rows[1], channels), lambda i: (jnp.maximum(i - first, 0), 0)),
        ]

    def shapes(self, channels, dtype, place=shape):
        return [place((s * r, channels), dtype) for s, r in zip(self.steps, self.rows)]

    def run(self, body, args, row_outs, whole_outs, flops, after=(), streamed=(), aliases=None):
        pairs = [a for a in args if isinstance(a, tuple)]
        rest = [a for a in args if not isinstance(a, tuple)]
        in_specs, flat = [], []
        for pair in pairs:
            in_specs += self.specs(pair[0].shape[1])
            flat += list(pair)
        in_specs += [whole(a.shape) for a in rest]
        out_shapes, out_specs = [], []
        for channels, dtype, *place in row_outs:
            out_shapes += self.shapes(channels, dtype, *place)
            out_specs += self.specs(channels)
        out_shapes += [shape(dims) for dims in whole_outs]
        out_specs += [whole(dims) for dims in whole_outs]
        n_in, n_rest, n_out = len(pairs), len(rest), len(row_outs)

        def kernel(*refs):
            i = pl.program_id(0)
            given, fixed = refs[: 2 * n_in], refs[2 * n_in : 2 * n_in + n_rest]
            made = refs[2 * n_in + n_rest :]
            for kind in range(2):
                here = i < self.steps[0] if kind == 0 else i >= self.steps[0]

                @pl.when(here)
                def _(kind=kind):
                    body(
                        i,
                        kind,
                        given[kind : 2 * n_in : 2],
                        fixed,
                        made[kind : 2 * n_out : 2],
                        made[2 * n_out :],
                    )

        made = call(
            kernel,
            out_shapes,
            flat + rest,
            grid=(sum(self.steps),),
            in_specs=in_specs,
            out_specs=out_specs,
            flops=flops,
            after=after,
            streamed=[2 * k + j for k in streamed for j in range(2)],
            aliases={2 * k + j: 2 * v + j for k, v in (aliases or {}).items() for j in range(2)},
        )
        return [tuple(made[2 * k : 2 * k + 2]) for k in range(n_out)] + list(made[2 * n_out :])

    def total(self):
        return sum(s * r for s, r in zip(self.steps, self.rows))


def add_norm(i, kind, packed, value, weight, start):
    channels = (packed.shape[1] - LANES) // 2
    width = value.shape[1]
    here = slice(start, start + width)
    there = slice(channels + start, channels + start + width)
    if kind == 0:
        count = jnp.full((1, 1), value.shape[0], FLOAT)
        mean = column_sum(value) * (1.0 / value.shape[0])
        spread = column_sum(jnp.square(value - mean))
    else:
        count = column_sum(weight)
        mean = column_sum(value * weight) / count
        spread = column_sum(jnp.square(value - mean) * weight)

    def begin():
        packed[:, here] = mean
        packed[:, there] = spread

    def go_on():
        before = packed[:, 2 * channels : 2 * channels + 1]
        part = count / (before + count)
        old = packed[:, here]
        delta = mean - old
        packed[:, here] = old + delta * part
        packed[:, there] = packed[:, there] + spread + jnp.square(delta) * (before * part)

    if kind == 0:
        pl.when(i == 0)(begin)
        pl.when(i > 0)(go_on)
    else:
        go_on()
    return count


def add_count(i, kind, packed, count):
    channels = (packed.shape[1] - LANES) // 2
    lanes = slice(2 * channels, 2 * channels + LANES)
    wide_count = jnp.broadcast_to(count, (1, LANES))

    def begin():
        packed[:, lanes] = wide_count

    def go_on():
        packed[:, lanes] = packed[:, lanes] + wide_count

    if kind == 0:
        pl.when(i == 0)(begin)
        pl.when(i > 0)(go_on)
    else:
        go_on()


def add_sums(i, kind, packed, low, high, start):
    channels = (packed.shape[1] - LANES) // 2
    width = low.shape[1]
    here = slice(start, start + width)
    there = slice(channels + start, channels + start + width)

    def begin():
        packed[:, here] = low
        packed[:, there] = high
        if start == 0:
            packed[:, 2 * channels :] = jnp.zeros((1, LANES), FLOAT)

    def go_on():
        packed[:, here] = packed[:, here] + low
        packed[:, there] = packed[:, there] + high

    if kind == 0:
        pl.when(i == 0)(begin)
        pl.when(i > 0)(go_on)
    else:
        go_on()


def reduce_stage(rows, inputs, weight, live):
    mid = weight.shape[1]

    def body(i, kind, given, fixed, made, totals):
        value = product(given[0][...], fixed[0][...])
        made[0][...] = value
        count = add_norm(i, kind, totals[0], value, fixed[1][...], 0)
        add_count(i, kind, totals[0], count)

    return rows.run(
        body,
        [inputs, weight, live],
        [(mid, FLOAT)],
        [(1, 2 * mid + LANES)],
        2 * rows.total() * weight.size,
        streamed=[0],
    )


def norm_kernel(crops, big, small, live, packed):
    channels = big.shape[1]
    weights = [None] + [live[low : low + ROWS, :] for low in range(0, crops, ROWS)]
    big_steps, small_steps = big.shape[0] // ROWS, small.shape[0] // crops

    def gather(value_of):
        def fold(value):
            return jnp.sum(value.reshape(-1, 8, channels), axis=0)

        def step(p, total):
            return total + fold(value_of(big[pl.ds(p * ROWS, ROWS), :]))

        total = lax.fori_loop(0, big_steps, step, jnp.zeros((8, channels), FLOAT), unroll=7)
        for k, weight in enumerate(weights[1:]):

            def step(p, part):
                return part + value_of(small[pl.ds(p * crops + k * ROWS, ROWS), :])

            part = lax.fori_loop(
                0, small_steps, step, jnp.zeros((ROWS, channels), FLOAT), unroll=True
            )
            total = total + fold(part * weight)
        return column_sum(total)

    count = big.shape[0] + small_steps * column_sum(live[:crops, :])
    mean = gather(lambda value: value) / count
    packed[:, :channels] = mean
    packed[:, channels : 2 * channels] = gather(lambda value: jnp.square(value - mean))
    packed[:, 2 * channels :] = jnp.broadcast_to(count, (1, LANES))


def norm_stage(rows, value, live):
    return call(
        lambda *refs: norm_kernel(rows.crops[1], *refs),
        shape((1, 2 * value[0].shape[1] + LANES)),
        [*value, live],
    )


def expand_stage(rows, second, scale, offset, weight, live):
    mid, wide = weight.shape

    def body(i, kind, given, fixed, made, totals):
        scale, offset, weight, live = fixed
        active = silu(given[0][...] * scale[...] + offset[...]).astype(HALF)
        made[1][...] = active
        for start in range(0, wide, CHUNK):
            columns = slice(start, start + CHUNK)
            value = product(active, weight[:, columns])
            made[0][:, columns] = value.astype(HALF)
            count = add_norm(i, kind, totals[0], value, live[...], start)
        add_count(i, kind, totals[0], count)

    return rows.run(
        body,
        [second, scale, offset, weight, live],
        [(wide, HALF, far_shape), (mid, HALF)],
        [(1, 2 * wide + LANES)],
        2 * rows.total() * weight.size,
    )


def pool_stage(rows, third, inputs, scale, offset):
    wide = scale.shape[1]

    def body(i, kind, given, fixed, made, totals):
        scale, offset = fixed
        steps, crops = rows.steps[kind], rows.crops[kind]
        step = i if kind == 0 else i - rows.steps[0]
        out = totals[kind]

        @pl.when(step == 0)
        def _():
            out[...] = jnp.zeros(out.shape, FLOAT)

        for start in range(0, wide, TILE):
            columns = slice(start, start + TILE)
            factor, shift = scale[:, columns], offset[:, columns]
            for low in range(0, crops, ROWS):
                total = out[low : low + ROWS, columns]
                for place in range(steps):
                    here = slice(place * crops + low, place * crops + low + ROWS)
                    residual = given[0][here, columns].astype(FLOAT) * factor + shift
                    residual = residual + given[1][here, columns].astype(FLOAT)
                    half = 0.5 * residual
                    total = total + (half * jnp.tanh(half) + half)
                out[low : low + ROWS, columns] = total

        @pl.when(step == steps - 1)
        def _():
            out[...] = out[...] * (1.0 / (steps * steps))

    return rows.run(
        body,
        [third, inputs, scale, offset],
        [],
        [(crops, wide) for crops in rows.crops],
        12 * rows.total() * wide,
        streamed=[0, 1],
    )


def residual_back_stage(rows, third, inputs, grads, scale, offset, mean, root, live, after):
    wide = scale.shape[1]

    def body(i, kind, given, fixed, made, totals):
        scale, offset, mean, root, live = fixed[2:]
        grads, crops = fixed[kind], rows.crops[kind]
        for start in range(0, wide, TILE):
            columns = slice(start, start + TILE)
            factor, shift, center = scale[:, columns], offset[:, columns], mean[:, columns]
            lows, highs = 0.0, 0.0
            for low in range(0, crops, ROWS):
                spread = grads[low : low + ROWS, columns]
                total, product_total = 0.0, 0.0
                for place in range(rows.steps[kind]):
                    here = slice(place * crops + low, place * crops + low + ROWS)
                    value = given[0][here, columns].astype(FLOAT)
                    residual = value * factor + shift + given[1][here, columns].astype(FLOAT)
                    grad = slope(residual) * spread
                    made[0][here, columns] = grad.astype(HALF)
                    total = total + grad
                    product_total = product_total + grad * (value - center)
                if kind == 1:
                    weight = live[low : low + ROWS, :]
                    total, product_total = total * weight, product_total * weight
                lows, highs = lows + column_sum(total), highs + column_sum(product_total)
            add_sums(i, kind, totals[0], lows, highs * root[:, columns], start)

    return rows.run(
        body,
        [third, inputs, *grads, scale, offset, mean, root, live],
        [(wide, HALF, far_shape)],
        [(1, 2 * wide + LANES)],
        16 * rows.total() * wide,
        after,
        streamed=[0, 1],
    )


def expand_back_stage(rows, grad, third, second, back, weight, norm, live, after):
    mid, wide = weight.shape

    def body(i, kind, given, fixed, made, totals):
        first, second, third, weight, scale, offset, mean, root, live = fixed
        total = jnp.zeros((rows.rows[kind], mid), FLOAT)
        for start in range(0, wide, CHUNK):
            columns = slice(start, start + CHUNK)
            value = (
                given[0][:, columns].astype(FLOAT) * first[:, columns]
                + given[1][:, columns].astype(FLOAT) * third[:, columns]
                + second[:, columns]
            )
            if kind == 1:
                value = value * live[...]
            value = value.astype(HALF)
            made[0][:, columns] = value
            total = total + product_outer(value, weight[:, columns])
        before = given[2][...]
        total = total * slope(before * scale[...] + offset[...])
        made[1][...] = total
        if kind == 1:
            total = total * live[...]
        high = column_sum(total * (before - mean[...])) * root[...]
        add_sums(i, kind, totals[0], column_sum(total), high, 0)

    return rows.run(
        body,
        [grad, third, second, *back, weight, *norm, live],
        [(wide, HALF, far_shape), (mid, FLOAT)],
        [(1, 2 * mid + LANES)],
        2 * rows.total() * weight.size,
        after,
        streamed=[0, 1],
    )


def slope_stage(rows, grad, value, norm, live):
    mid = grad[0].shape[1]

    def body(i, kind, given, fixed, made, totals):
        scale, offset, mean, root, live = fixed
        before = given[1][...]
        total = given[0][...] * slope(before * scale[...] + offset[...])
        made[0][...] = total
        if kind == 1:
            total = total * live[...]
        high = column_sum(total * (before - mean[...])) * root[...]
        add_sums(i, kind, totals[0], column_sum(total), high, 0)

    return rows.run(
        body,
        [grad, value, *norm, live],
        [(mid, FLOAT)],
        [(1, 2 * mid + LANES)],
        16 * rows.total() * mid,
    )


def norm_back_stage(rows, grad, value, back, live, after):
    mid = grad[0].shape[1]

    def body(i, kind, given, fixed, made, totals):
        first, second, third, live = fixed
        total = given[0][...] * first[...] + given[1][...] * third[...] + second[...]
        if kind == 1:
            total = total * live[...]
        made[0][...] = total.astype(HALF)

    return rows.run(
        body, [grad, value, *back, live], [(mid, HALF)], [], 6 * rows.total() * mid, after
    )[0]


def input_grad_stage(rows, grad, first, weight, after):
    wide, mid = weight.shape

    def body(i, kind, given, fixed, made, totals):
        first = given[1][...]
        for start in range(0, wide, CHUNK):
            columns = slice(start, start + CHUNK)
            value = product_outer(first, fixed[0][columns, :])
            made[0][:, columns] = (value + given[0][:, columns].astype(FLOAT)).astype(HALF)

    return rows.run(
        body,
        [grad, first, weight],
        [(wide, HALF, far_shape)],
        [],
        2 * rows.total() * weight.size,
        after,
        streamed=[0],
    )[0]


def hidden_kernel(big, small, weight, live, out, packed):
    j = pl.program_id(0)
    channels = (packed.shape[1] - LANES) // 2
    pooled = jnp.concatenate([big[...].astype(HALF), small[...].astype(HALF)])
    value = product(pooled, weight[...])
    out[...] = value
    count = column_sum(live[...])
    mean = column_sum(value * live[...]) / count
    spread = column_sum(jnp.square(value - mean) * live[...])
    packed[:, pl.ds(pl.multiple_of(j * CHUNK, CHUNK), CHUNK)] = mean
    packed[:, pl.ds(pl.multiple_of(channels + j * CHUNK, CHUNK), CHUNK)] = spread
    packed[:, 2 * channels :] = jnp.broadcast_to(count, (1, LANES))


def hidden_stage(big, small, weight, live):
    crops = live.shape[0]
    wide, channels = weight.shape
    return call(
        hidden_kernel,
        [shape((crops, channels)), shape((1, 2 * channels + LANES))],
        [big, small, weight, live],
        grid=(channels // CHUNK,),
        in_specs=[
            whole(big.shape),
            whole(small.shape),
            pl.BlockSpec((wide, CHUNK), lambda j: (0, j)),
            whole(live.shape),
        ],
        out_specs=[
            pl.BlockSpec((crops, CHUNK), lambda j: (0, j)),
            whole((1, 2 * channels + LANES)),
        ],
        flops=2 * crops * weight.size,
        streamed=[2],
    )


def lanes_of(dims):
    return lax.broadcasted_iota(jnp.int32, dims, 1)


def sums_by_view(batch, stored, views):
    row = lax.broadcasted_iota(jnp.int32, batch.shape, 0) % views
    size = stored.shape[0] // views
    return jnp.concatenate(
        [
            column_sum(jnp.where(row == v, batch, 0.0))
            + column_sum(stored[v * size : (v + 1) * size])
            for v in range(views)
        ],
        axis=1,
    )


def queue_kernel(proto, views, queue, prototypes, stored):
    rows = queue.shape[0] // views
    value = queue[...].astype(FLOAT)
    unit = value * lax.rsqrt(jnp.sum(value * value, axis=1, keepdims=True) + EPS_UNIT)
    scores = product_outer(unit.astype(HALF), prototypes[...])
    value = jnp.where(lanes_of(scores.shape) < proto, jnp.exp(scores / EPS_CODE), 0.0)
    size = stored.shape[0] // views
    stored[...] = jnp.zeros(stored.shape, FLOAT)
    for v in range(views):
        stored[v * size : v * size + rows, :] = value[v * rows : (v + 1) * rows]


def score_kernel(
    proto, views, big_rows, hidden, scale, offset, project, prototypes, stored,
    active_out, embedded_out, unit_out, scores_out, batch_out, sums,
):
    active = silu(hidden[...] * scale[...] + offset[...]).astype(HALF)
    active_out[...] = active
    embedded = product(active, project[...])
    embedded_out[...] = embedded
    root = lax.rsqrt(jnp.sum(embedded * embedded, axis=1, keepdims=True) + EPS_UNIT)
    unit = (embedded * root).astype(HALF)
    unit_out[...] = unit
    scores = product_outer(unit, prototypes[...])
    scores_out[...] = scores
    batch = scores[:big_rows]
    batch = jnp.where(lanes_of(batch.shape) < proto, jnp.exp(batch / EPS_CODE), 0.0)
    batch_out[...] = batch
    sums[...] = sums_by_view(batch, stored[...], views)


def balanced(proto, views, parts, batch, stored):
    totals = tree([part[...] for part in parts])
    width = batch.shape[1]
    totals = [totals[:, v * width : (v + 1) * width] for v in range(views)]
    totals = [jnp.where(lanes_of(t.shape) < proto, t, 1.0) for t in totals]
    row = lax.broadcasted_iota(jnp.int32, batch.shape, 0) % views
    own = jnp.zeros(batch.shape, FLOAT)
    for v in range(views):
        own = jnp.where(row == v, totals[v], own)
    batch = batch / own
    batch = batch / jnp.sum(batch, axis=1, keepdims=True)
    if stored is None:
        return batch, None
    size = stored.shape[0] // views
    stored = jnp.concatenate(
        [stored[v * size : (v + 1) * size] / totals[v] for v in range(views)]
    )
    sums = jnp.sum(stored, axis=1, keepdims=True)
    return batch, jnp.where(sums > 0.0, stored / jnp.where(sums > 0.0, sums, 1.0), 0.0)


def balance_kernel(proto, views, *refs):
    *parts, batch, stored, batch_out, stored_out, sums = refs
    batch, stored = balanced(proto, views, parts, batch[...], stored[...])
    batch_out[...] = batch
    stored_out[...] = stored
    sums[...] = sums_by_view(batch, stored, views)


def loss_kernel(proto, views, *refs):
    (
        *parts, batch, scores, share, live, embedded, hidden, scale, offset, mean, root, project, prototypes,
        grad_scores_out, grad_embedded_out, grad_out, packed,
    ) = refs
    codes, _ = balanced(proto, views, parts, batch[...], None)
    big = codes.shape[0]
    images = big // views
    slots = (scores.shape[0] - big) // images
    row = lax.broadcasted_iota(jnp.int32, codes.shape, 0) % views
    others = jnp.zeros(codes.shape, FLOAT)
    for turn in range(1, views):
        ahead = jnp.concatenate([codes[turn:], codes[:turn]])
        behind = jnp.concatenate([codes[turn - views :], codes[: turn - views]])
        others = others + jnp.where(row + turn < views, ahead, behind)
    both = codes + others
    targets = jnp.concatenate(
        [others]
        + [
            jnp.broadcast_to(both[k * views : k * views + 1], (slots, both.shape[1]))
            for k in range(images)
        ]
    )
    lanes = lanes_of(scores.shape)
    logits = jnp.where(lanes < proto, scores[...] / SOFTMAX_HEAT, -1e30)
    top = jnp.max(logits, axis=1, keepdims=True)
    powers = jnp.where(lanes < proto, jnp.exp(logits - top), 0.0)
    sums = jnp.sum(powers, axis=1, keepdims=True)
    logs = jnp.where(lanes < proto, logits - top - jnp.log(sums), 0.0)
    loss = -column_sum(jnp.sum(targets * logs, axis=1, keepdims=True) * share[...])
    mass = jnp.sum(targets, axis=1, keepdims=True)
    grad = (share[...] / SOFTMAX_HEAT) * (powers * (mass / sums) - targets)
    grad = grad.astype(HALF)
    grad_scores_out[...] = grad
    grad = product(grad, prototypes[...])
    value = embedded[...]
    scaled = lax.rsqrt(jnp.sum(value * value, axis=1, keepdims=True) + EPS_UNIT)
    unit = value * scaled
    grad = scaled * (grad - unit * jnp.sum(unit * grad, axis=1, keepdims=True))
    grad = grad.astype(HALF)
    grad_embedded_out[...] = grad
    channels = scale.shape[1]
    for start in range(0, channels, CHUNK):
        columns = slice(start, start + CHUNK)
        before = hidden[:, columns]
        part = product_outer(grad, project[columns, :])
        part = part * slope(before * scale[:, columns] + offset[:, columns])
        grad_out[:, columns] = part
        part = part * live[...]
        packed[:, columns] = column_sum(part)
        packed[:, channels + start : channels + start + CHUNK] = (
            column_sum(part * (before - mean[:, columns])) * root[:, columns]
        )
    packed[:, 2 * channels :] = jnp.broadcast_to(loss, (1, LANES))


def pooled_back_kernel(areas, big_rows, grad, hidden, live, first, second, third, weight, grad_out, big, small):
    value = grad[...] * first[...] + hidden[...] * third[...] + second[...]
    value = value * live[...]
    grad_out[...] = value
    part = product_outer(value.astype(HALF), weight[...])
    big[...] = part[:big_rows] / areas[0]
    small[...] = part[big_rows:] / areas[1]


def turn_kernel(blocks, big, small, out):
    value = jnp.concatenate([big[...], small[...]]).T
    rows = value.shape[0] // blocks
    planes = out.shape[0]
    for k in range(planes):
        parts = [value[j * rows : (j + 1) * rows] for j in range(k, blocks, planes)]
        out[k] = jnp.concatenate(parts).T


def hidden_grad_kernel(left, right, out):
    out[...] = product_inner(left[...].astype(HALF), right[...].astype(HALF))


def hidden_grad_stage(left, right, after):
    crops, height = left.shape
    width = right.shape[1]
    return call(
        hidden_grad_kernel,
        shape((height, width)),
        [left, right],
        grid=(width // CHUNK,),
        in_specs=[whole(left.shape), pl.BlockSpec((crops, CHUNK), lambda j: (0, j))],
        out_specs=pl.BlockSpec((height, CHUNK), lambda j: (0, j)),
        flops=2 * crops * height * width,
        streamed=[0, 1],
        after=after,
    )


def head_grad_kernel(devices, bits, active, grad_embedded, unit, grad_scores, keep, send):
    half = pick(bits, 0)
    project = product_inner(active[...], grad_embedded[...])
    proto = product_inner(unit[...], grad_scores[...])
    rows, lines = project.shape[0] // devices, proto.shape[0] // devices

    def store(k, here, columns, even, odd):
        keep[0, k, here, columns] = jnp.where(half == 0, even, odd)
        send[0, k, here, columns] = jnp.where(half == 0, odd, even)

    for k in range(devices // 2):
        pair = project[2 * k * rows : 2 * (k + 1) * rows]
        for part in range(2):
            start = part * rows // 2
            store(
                k,
                slice(0, rows // 2),
                slice(part * LANES, (part + 1) * LANES),
                pair[start : start + rows // 2],
                pair[rows + start : rows + start + rows // 2],
            )
        pair = proto[2 * k * lines : 2 * (k + 1) * lines]
        for part in range(proto.shape[1] // TILE):
            piece = pair[:, part * TILE : (part + 1) * TILE]
            start = rows // 2 + part * lines
            store(k, slice(start, start + lines), slice(0, TILE), piece[:lines], piece[lines:])


def head_grad_stage(active, grad_embedded, unit, grad_scores, devices, me, after):
    rows = active.shape[1] * grad_embedded.shape[1] + unit.shape[1] * grad_scores.shape[1]
    out = shape((1, devices // 2, rows // (devices * TILE), TILE))
    return call(
        lambda *refs: head_grad_kernel(devices, *refs),
        [out, out],
        [active, grad_embedded, unit, grad_scores],
        scalars=[me],
        after=after,
    )


def conv(field, weight):
    return lax.conv_general_dilated(
        field,
        weight,
        (1, 1),
        ((1, 1), (1, 1)),
        dimension_numbers=("HWNC", "HWIO", "HWNC"),
        preferred_element_type=FLOAT,
    )


def conv_back(field, weight):
    return lax.conv_general_dilated(
        field,
        lax.rev(weight, (0, 1)),
        (1, 1),
        ((1, 1), (1, 1)),
        dimension_numbers=("HWNC", "HWOI", "HWNC"),
        preferred_element_type=FLOAT,
    )


def conv_filter(field, grad):
    return lax.conv_general_dilated(
        field,
        grad,
        (1, 1),
        ((1, 1), (1, 1)),
        dimension_numbers=("HWCN", "HWIO", "HWNC"),
        preferred_element_type=FLOAT,
    )


def local(
    big_crops,
    small_crops,
    small_count,
    w_reduce,
    w_spatial,
    w_expand,
    gain_mid,
    bias_mid,
    gain_wide,
    bias_wide,
    w_hidden,
    gain_head,
    bias_head,
    w_project,
    prototypes,
    queue,
):
    devices = lax.axis_size("dp")
    image_rows = small_count.shape[0]
    images = image_rows * devices
    big_rows, big_side = big_crops.shape[:2]
    small_rows, small_side = small_crops.shape[:2]
    views = big_rows // image_rows
    slots = small_rows // image_rows
    wide = big_crops.shape[3]
    mid = w_reduce.shape[1]
    hid = w_hidden.shape[1]
    proj, proto = prototypes.shape
    proto_wide = -(-proto // CHUNK) * CHUNK
    crops = big_rows + small_rows
    areas = (big_side * big_side, small_side * small_side)
    rows = Rows(big_side, big_rows, small_side, small_rows)
    sides = ((big_side, big_side, big_rows), (small_side, small_side, small_rows))
    planes = [[k * PLANE + j for j in range(PLANE)] for k in range(devices // PLANE)]
    stacks = [[k * PLANE + j for k in range(devices // PLANE)] for j in range(PLANE)]
    me = lax.axis_index("dp").astype(jnp.int32).reshape(1)

    slot_mask = (jnp.arange(slots)[None, :] < small_count[:, None]).astype(FLOAT)
    slot_flags = slot_mask.reshape(-1)
    live = jnp.tile(slot_flags, small_side)[:, None]
    crop_live = jnp.concatenate([jnp.ones((big_rows,), FLOAT), slot_flags])[:, None]
    share = 1.0 / (images * views * (views - 1.0 + small_count.astype(FLOAT)))
    share = jnp.concatenate(
        [jnp.repeat(share, views), jnp.repeat(share, slots) * slot_flags]
    )[:, None]

    def fields(pair):
        return [a.reshape(*s, a.shape[-1]) for a, s in zip(pair, sides)]

    def flat(pair):
        return tuple(a.reshape(-1, a.shape[-1]) for a in pair)

    inputs = flat((jnp.transpose(big_crops, (1, 2, 0, 3)), jnp.transpose(small_crops, (1, 2, 0, 3))))
    taps = jnp.transpose(w_spatial, (1, 0, 2))
    filters = taps.reshape(3, 3, mid, mid)
    lines = jnp.pad(jnp.transpose(prototypes), ((0, proto_wide - proto), (0, 0)))

    first, packed = reduce_stage(rows, inputs, w_reduce, live)
    scale_one, offset_one, mean_one, root_one, pixel_count = settle_norm(
        packed, gain_mid[0], bias_mid[0], devices
    )
    mid_one = fields([silu(a * scale_one + offset_one).astype(HALF) for a in first])
    second = flat([conv(a, filters) for a in mid_one])
    packed = norm_stage(rows, second, live)
    scale_two, offset_two, mean_two, root_two, _ = settle_norm(
        packed, gain_mid[1], bias_mid[1], devices
    )
    third, mid_two, packed = expand_stage(rows, second, scale_two, offset_two, w_expand, live)
    scale_three, offset_three, mean_three, root_three, _ = settle_norm(
        packed, gain_wide, bias_wide, devices
    )
    pooled_big, pooled_small = pool_stage(rows, third, inputs, scale_three, offset_three)

    hidden, packed = hidden_stage(pooled_big, pooled_small, w_hidden, crop_live)
    scale_head, offset_head, mean_head, root_head, crop_count = settle_norm(
        packed, gain_head, bias_head, devices
    )
    stored_rows = views * (-(-queue.shape[1] // 8) * 8)
    stored = call(
        lambda *refs: queue_kernel(proto, views, *refs),
        shape((stored_rows, proto_wide)),
        [queue.reshape(-1, proj), lines],
    )
    active, embedded, unit, scores, batch, sums = call(
        lambda *refs: score_kernel(proto, views, big_rows, *refs),
        [
            shape((crops, hid), HALF),
            shape((crops, proj)),
            shape((crops, proj), HALF),
            shape((crops, proto_wide)),
            shape((big_rows, proto_wide)),
            shape((1, views * proto_wide)),
        ],
        [hidden, scale_head, offset_head, w_project, lines, stored],
    )
    for step in range(ITERS - 1):
        batch, stored, sums = call(
            lambda *refs: balance_kernel(proto, views, *refs),
            [shape(batch.shape), shape(stored.shape), shape(sums.shape)],
            [*sum_parts(sums, devices), batch, stored],
            )

    loss_outs = [
        shape((crops, proto_wide), HALF),
        shape((crops, proj), HALF),
        shape((crops, hid)),
        shape((1, 2 * hid + LANES)),
    ]
    parts = sum_parts(sums, devices)
    loss_args = [
        batch,
        scores,
        share,
        crop_live,
        embedded,
        hidden,
        scale_head,
        offset_head,
        mean_head,
        root_head,
        w_project,
        lines,
    ]
    grad_scores, grad_embedded, grad_active, packed = call(
        lambda *refs: loss_kernel(proto, views, *refs),
        loss_outs,
        [*parts, *loss_args],
        grid=(1,),
        in_specs=[whole(a.shape) for a in (*parts, *loss_args)],
        out_specs=[whole(a.shape) for a in loss_outs],
        streamed=range(len(parts), len(parts) + len(loss_args)),
    )
    made = {}

    def head_work(mark):
        made["head"] = head_grad_stage(
            active, grad_embedded, unit, grad_scores, devices, me, [mark]
        )
        return [made["head"][0]]

    *back, gain_head_grad, bias_head_grad, loss = settle_back(
        packed, gain_head, mean_head, root_head, crop_count, devices, [head_work]
    )
    head_sum = Scatter(*made["head"], devices, me)
    grad_hidden, *grad_pooled = call(
        lambda *refs: pooled_back_kernel(areas, big_rows, *refs),
        [shape((crops, hid)), shape((big_rows, wide)), shape((small_rows, wide))],
        [grad_active, hidden, crop_live, *back, w_hidden],
        grid=(wide // CHUNK,),
        in_specs=[
            whole((crops, hid)),
            whole((crops, hid)),
            whole((crops, 1)),
            whole((1, hid)),
            whole((1, hid)),
            whole((1, hid)),
            pl.BlockSpec((CHUNK, hid), lambda j: (j, 0)),
        ],
        out_specs=[
            whole((crops, hid)),
            pl.BlockSpec((big_rows, CHUNK), lambda j: (0, j)),
            pl.BlockSpec((small_rows, CHUNK), lambda j: (0, j)),
        ],
        flops=2 * crops * w_hidden.size,
        streamed=[6],
    )
    plane_grad = lax.all_gather(grad_hidden, "dp", axis_index_groups=planes, tiled=True)

    grad_residual, packed = residual_back_stage(
        rows,
        third,
        inputs,
        grad_pooled,
        scale_three,
        offset_three,
        mean_three,
        root_three,
        live,
        [head_sum.go()],
    )
    *back, gain_three, bias_three, _ = settle_back(
        packed, gain_wide, mean_three, root_three, pixel_count, devices
    )
    turned = call(
        lambda *refs: turn_kernel(devices, *refs),
        shape((PLANE, crops, wide // PLANE)),
        [pooled_big, pooled_small],
        after=[back[0]],
    )
    plane_pooled = lax.all_to_all(
        turned, "dp", 0, 0, axis_index_groups=planes, tiled=True
    ).reshape(PLANE * crops, wide // PLANE)
    grad_third, grad_two, packed = expand_back_stage(
        rows,
        grad_residual,
        third,
        second,
        back,
        w_expand,
        [scale_two, offset_two, mean_two, root_two],
        live,
        [turned],
    )
    packed = tie(packed, [plane_pooled])

    def expand_work(mark):
        made["expand"] = weight_grad(mid_two, grad_third, devices, me, 1, [mark], [1, 3])
        return [made["expand"][0]]

    def hidden_work(mark):
        made["hidden"] = hidden_grad_stage(plane_pooled, plane_grad, [mark])
        return [made["hidden"]]

    *back, gain_two, bias_two, _ = settle_back(
        packed,
        gain_mid[1],
        mean_two,
        root_two,
        pixel_count,
        devices,
        [expand_work, hidden_work],
    )
    expand_sum = Scatter(*made["expand"], devices, me)
    hidden_grad = lax.psum_scatter(
        made["hidden"], "dp", scatter_dimension=0, axis_index_groups=stacks, tiled=True
    )
    grad_second = norm_back_stage(
        rows, grad_two, second, back, live, [expand_sum.go([back[0]]), head_sum.go([back[0]])]
    )
    grad_mid_one = flat([conv_back(a, filters) for a in fields(grad_second)])
    grad_one, packed = slope_stage(
        rows, grad_mid_one, first, [scale_one, offset_one, mean_one, root_one], live
    )

    def big_work(mark):
        grad = tie(grad_second[0], [mark])
        made["big"] = conv_filter(mid_one[0], fields((grad, grad_second[1]))[0])
        return [made["big"]]

    def small_work(mark):
        grad = tie(grad_second[1], [mark])
        part = made["big"] + conv_filter(mid_one[1], fields((grad_second[0], grad))[1])
        made["spatial"] = part.reshape(9, devices, mid // devices, mid)
        return [made["spatial"]]

    *back, gain_one, bias_one, _ = settle_back(
        packed,
        gain_mid[0],
        mean_one,
        root_one,
        pixel_count,
        devices,
        [big_work, small_work],
    )
    spatial_send = send_rows(made["spatial"], me, [back[0]])
    spatial_sum = Scatter(made["spatial"], spatial_send, devices, me)
    mark = expand_sum.go([back[0]])
    grad_first = norm_back_stage(rows, grad_one, first, back, live, [mark])
    reduce_keep, reduce_send = weight_grad(
        inputs, grad_first, devices, me, 0, [spatial_send], [0, 2]
    )
    reduce_sum = Scatter(reduce_keep, reduce_send, devices, me)
    mark = spatial_sum.go([reduce_keep])
    mark = reduce_sum.go([mark])
    grad_inputs = input_grad_stage(rows, grad_residual, grad_first, w_reduce, [mark])
    grad_big, grad_small = fields(grad_inputs)
    mark = grad_inputs[0]
    order = (expand_sum, spatial_sum, reduce_sum, head_sum, spatial_sum, reduce_sum, expand_sum)
    for part in order + (spatial_sum, reduce_sum, head_sum) * 2:
        if not part.complete():
            mark = part.go([mark])
    head_grad = head_sum.end()[0]
    ends = w_project.shape[0] // (2 * devices)
    project_grad = jnp.concatenate([head_grad[:ends, :LANES], head_grad[:ends, LANES:]])
    proto_grad = head_grad[ends:].reshape(-1, proj // devices, TILE)
    proto_grad = jnp.transpose(proto_grad, (1, 0, 2)).reshape(proj // devices, -1)[:, :proto]
    expand_grad = expand_sum.end()[0]
    spatial_grad = spatial_sum.end()
    reduce_grad = reduce_sum.end()[0]
    return (
        loss[0, 0],
        jnp.transpose(grad_big, (2, 0, 1, 3)),
        jnp.transpose(grad_small, (2, 0, 1, 3)),
        reduce_grad,
        jnp.transpose(spatial_grad, (1, 0, 2)),
        expand_grad,
        jnp.concatenate([gain_one, gain_two]),
        jnp.concatenate([bias_one, bias_two]),
        gain_three[0],
        bias_three[0],
        hidden_grad,
        gain_head_grad[0],
        bias_head_grad[0],
        project_grad,
        proto_grad,
    )


def solution(mesh):
    placed = (
        P("dp", None, None, None),
        P("dp", None, None, None),
        P("dp"),
        P(),
        P(),
        P(),
        P(),
        P(),
        P(),
        P(),
        P(),
        P(),
        P(),
        P(),
        P(),
        P(None, "dp", None),
    )
    return jax.shard_map(
        local,
        mesh=mesh,
        in_specs=placed,
        out_specs=(
            P(),
            P("dp", None, None, None),
            P("dp", None, None, None),
            P("dp", None),
            P("dp", None, None),
            P("dp", None),
            P(),
            P(),
            P(),
            P(),
            P("dp", None),
            P(),
            P(),
            P("dp", None),
            P("dp", None),
        ),
        check_vma=False,
    )
```

time: 1730 us -> 605 us (0.35)
  blocking collectives: 605 us -> 0 us
  local copies, waits for them, and re-layouts: 342 us -> 61.8 us
  other arithmetic: 193 us -> 5.98 us
  Pallas kernels: 0 us -> 180 us
  waiting for transfers between devices: 347 us -> 167 us
  matrix products: 216 us -> 48.5 us
  starting transfers between devices: 0.42 us -> 116 us
    psum x15 -> x0, blocking collectives: 605 us -> none  [the longest x4 162 us: forward_norm(): total, extra_sum = lax.psum((jnp.sum(weighted, axis=0), extra), 'dp')]
    reduce_scatter x5 -> x1, waiting for transfers between devices: 347 us -> 0.01 us  [local(): lax.psum_scatter(made['hidden'], 'dp', scatter_dimension=0, axis_index_gr...]
    dot_general x62 -> x0, matrix products: 184 us -> none  [the longest x15 67.4 us: product_outer(): lax.dot_general(left, right, (((1,), (1,)), ((), ())), preferred_element_...]
    pallas_call x0 -> x67, Pallas kernels: none -> 180 us  [call(): pl.pallas_call(run, out_shape=out_shape, in_specs=[pl.BlockSpec(memory_sp...]
    ppermute x0 -> x105, waiting for transfers between devices: none -> 167 us  [the longest x28 95.8 us: cross(): lax.ppermute(value, 'dp', [(i, i ^ 1 << place) for i in range(self.device...]
    reshape x28 -> x4, local copies, waits for them, and re-layouts: 143 us -> 0.64 us  [the longest x1 0.6 us: local(): jnp.repeat(share, views)]
    ppermute x0 -> x105, starting transfers between devices: none -> 112 us  [the longest x77 87 us: peers(): lax.ppermute(value, 'dp', [(i, i ^ mask) for i in range(devices)])]
    reduce_sum x24 -> x0, other arithmetic: 85.8 us -> none  [the longest x2 37.9 us: backward_norm(): jnp.sum(weighted, axis=0)]
  transfers between devices with their start and end apart: 6 -> 108, of which waited for: 3 -> 62; matrix products, arithmetic and copies ran while one was open for 23% -> 4% of each run, Pallas kernels for 0% -> 17%
where the time goes in v1:
time: 605 us; the launch traced here: 595 us
  Pallas kernels  180 us (30%)
  waiting for transfers between devices  167 us (28%)
  starting transfers between devices  116 us (19%)
  local copies, waits for them, and re-layouts  61.8 us (10%)
  matrix products  48.5 us (8%)
  between operations  16 us (3%)
    pallas_call x67, Pallas kernels, call(): pl.pallas_call(run, out_shape=out_shape, in_specs=[pl.BlockSpec(memory_sp...  180 us
    ppermute x28, waiting for transfers between devices, cross(): lax.ppermute(value, 'dp', [(i, i ^ 1 << place) for i in range(self.device...  95.8 us
    ppermute x77, starting transfers between devices, peers(): lax.ppermute(value, 'dp', [(i, i ^ mask) for i in range(devices)])  87 us
    ppermute x77, waiting for transfers between devices, peers(): lax.ppermute(value, 'dp', [(i, i ^ mask) for i in range(devices)])  70.9 us
    unnamed x269, local copies, waits for them, and re-layouts  58.1 us
    ppermute x28, starting transfers between devices, cross(): lax.ppermute(value, 'dp', [(i, i ^ 1 << place) for i in range(self.device...  24.7 us
    conv_general_dilated x2, matrix products, conv_back(): lax.conv_general_dilated(field, lax.rev(weight, (0, 1)), (1, 1), ((1, 1),...  18.4 us
    conv_general_dilated x2, matrix products, conv_filter(): lax.conv_general_dilated(field, grad, (1, 1), ((1, 1), (1, 1)), dimension...  16.8 us
  transfers between devices with their start and end apart: 108, of which 62 were waited for; matrix products, arithmetic and copies ran while one was open for 4% of the time, Pallas kernels for 17%

profile of v1, /device:TPU:0, one launch (start us, length us, event | category | flops | bytes accessed | tf_op | source)
XLA Modules:
  0.0 594.8 jit_solution(10022029026533027520)
XLA Ops:
  9.8 12.3 %shard_map.271 = (f32[1568,512]{1,0:T(8,128)S(1)}, f32[1152,512]{1,0:T(8,128)S(1)}, f32[1,1152]{1,0:T(1,128)S(1)}) custom-call(bf16[1568,2048]{1,0:T(8,128)(2,1)} %bitcast.123, bf16[1152,2048]{1,0:T(8,128)(2,1)} %bitcast.127, bf16[2048,512]{1,0:T(8,128)(2,1)S(1)} %copy-done.103, f32[384,1]{1,0:T(8,128)S(1)} %bitcast.88), custom_call_target="tpu_custom_call" | custom-call | flops 5704253440 | bytes 18814976 | tf_op jit(solution)/shard_map/pallas_call | solution.py:105
  23.6 2.9 collective-permute-start.1
  28.0 2.0 collective-permute-done.2.refs_2_
  30.1 2.4 collective-permute-done.3.refs_3_
  34.2 2.6 collective-permute-start.5
  38.7 3.5 collective-permute-done.6.refs_3_
  46.7 2.5 copy-done.125
  49.2 5.7 fusion.6
  55.0 7.7 %fusion.5 = f32[7,7,32,512]{3,2,1,0:T(8,128)S(1)} fusion(bf16[7,7,32,512]{3,2,1,0:T(8,128)(2,1)S(1)} %bitcast.113, bf16[3,3,512,512]{3,2,1,0:T(8,128)(2,1)S(1)} %bitcast.119), kind=kOutput, calls=%fused_computation.24 | convolution fusion | flops 6056574976 | bytes 9535488 | tf_op jit(solution)/shard_map/conv_general_dilated | solution.py:1056
  71.6 3.6 collective-permute-start.13
  78.8 18.9 %shard_map.279 = (bf16[1568,2048]{1,0:T(8,128)(2,1)}, bf16[1152,2048]{1,0:T(8,128)(2,1)}, bf16[1568,512]{1,0:T(8,128)(2,1)S(1)}, bf16[1152,512]{1,0:T(8,128)(2,1)S(1)}, f32[1,4224]{1,0:T(1,128)S(1)}) custom-call(f32[1568,512]{1,0:T(8,128)S(1)} %bitcast.80, f32[1152,512]{1,0:T(8,128)S(1)} %bitcast.84, f32[1,512]{1,0:T(1,128)S(1)} %get-tuple-element.160.refs_2_.refs_10_, ...), custom_call_target="tpu_custom_call" | custom-call | flops 5704253440 | bytes 21616640 | tf_op jit(solution)/shard_map/pallas_call | solution.py:105
  105.4 2.6 collective-permute-done.17.refs_3_
  108.5 3.8 collective-permute-start.19
  114.1 3.8 collective-permute-done.20.refs_3_
  120.5 13.8 %shard_map.283 = (f32[32,2048]{1,0:T(8,128)S(1)}, f32[128,2048]{1,0:T(8,128)S(1)}) custom-call(bf16[1568,2048]{1,0:T(8,128)(2,1)} %get-tuple-element.162.refs_0_.refs_2_, bf16[1152,2048]{1,0:T(8,128)(2,1)} %get-tuple-element.163.refs_1_.refs_3_, bf16[1568,2048]{1,0:T(8,128)(2,1)} %bitcast.124, bf16[1152,2048]{1,0:T(8,128)(2,1)} %bitcast.128, ...), custom_call_target="tpu_custom_call" | custom-call | flops 66846720 | bytes 23609344 | tf_op jit(solution)/shard_map/pallas_call | solution.py:105
  134.3 5.9 shard_map.284
  150.2 3.6 collective-permute-start.27
  166.5 2.5 collective-permute-done.31
  169.4 3.8 collective-permute-start.33
  175.0 3.8 collective-permute-done.34.refs_3_
  188.4 3.6 collective-permute-start.41
  202.1 2.0 collective-permute-done.45
  205.3 3.8 collective-permute-start.47
  210.9 3.8 collective-permute-done.48.refs_3_
  214.8 5.0 shard_map.292
  233.7 3.6 collective-permute-start.55
  240.5 6.1 %shard_map.296 = (f32[160,2048]{1,0:T(8,128)S(1)}, f32[32,2048]{1,0:T(8,128)S(1)}, f32[128,2048]{1,0:T(8,128)S(1)}) custom-call(f32[160,2048]{1,0:T(8,128)S(1)} %copy-done.31, f32[160,2048]{1,0:T(8,128)S(1)} %copy-done.14, f32[160,1]{1,0:T(8,128)S(1)} %copy-done.34, f32[1,2048]{1,0:T(1,128)S(1)} %get-tuple-element.193.refs_3_, ...), custom_call_target="tpu_custom_call" | custom-call | flops 1342177280 | bytes 13656704 | tf_op jit(solution)/shard_map/pallas_call | solution.py:105
  249.6 3.2 collective-permute-done.56.refs_2_
  256.0 22.6 %shard_map.298 = (bf16[1568,2048]{1,0:T(8,128)(2,1)}, bf16[1152,2048]{1,0:T(8,128)(2,1)}, f32[1,4224]{1,0:T(1,128)S(1)}) custom-call(bf16[1568,2048]{1,0:T(8,128)(2,1)} %get-tuple-element.162.refs_0_.refs_2_, bf16[1152,2048]{1,0:T(8,128)(2,1)} %get-tuple-element.163.refs_1_.refs_3_, bf16[1568,2048]{1,0:T(8,128)(2,1)} %bitcast.125, ...), custom_call_target="tpu_custom_call" | custom-call | flops 89128960 | bytes 34785280 | tf_op jit(solution)/shard_map/pallas_call | solution.py:105
  286.9 4.2 collective-permute-start.62
  292.8 3.8 collective-permute-done.63.refs_3_
  299.5 4.3 all-to-all-start
  308.5 19.1 %shard_map.301 = (bf16[1568,2048]{1,0:T(8,128)(2,1)}, bf16[1152,2048]{1,0:T(8,128)(2,1)}, f32[1568,512]{1,0:T(8,128)S(1)}, f32[1152,512]{1,0:T(8,128)S(1)}, f32[1,1152]{1,0:T(1,128)S(1)}) custom-call(bf16[1568,2048]{1,0:T(8,128)(2,1)} %get-tuple-element.202.refs_0_, bf16[1152,2048]{1,0:T(8,128)(2,1)} %get-tuple-element.203.refs_1_, ...), custom_call_target="tpu_custom_call" | custom-call | flops 5704253440 | bytes 46700544 | tf_op jit(solution)/shard_map/pallas_call | solution.py:105
  334.6 10.1 %shard_map.303 = (f32[1,16,16,2048]{3,2,1,0:T(8,128)S(1)}, f32[1,16,16,2048]{3,2,1,0:T(8,128)}) custom-call(s32[1]{0:T(128)} %bitcast.20.refs_0_, bf16[1568,512]{1,0:T(8,128)(2,1)S(1)} %copy-done.119, bf16[1568,2048]{1,0:T(8,128)(2,1)} %get-tuple-element.215.refs_2_, bf16[1152,512]{1,0:T(8,128)(2,1)S(1)} %copy-done.121, ...), custom_call_target="tpu_custom_call" | custom-call | flops 5704253440 | bytes 18120704 | tf_op jit(solution)/shard_map/pallas_call | solution.py:105
  354.0 2.9 collective-permute-done.68.refs_1_
  357.7 7.0 %shard_map.305.refs_1_ = f32[256,2048]{1,0:T(8,128)} custom-call(f32[1280,256]{1,0:T(8,128)} %bitcast.24.refs_1_.refs_0_, f32[1280,2048]{1,0:T(8,128)} %all-gather.2.cloned.1.call-done.refs_1_, f32[1,1152]{1,0:T(1,128)S(1)} %add_add_fusion.6.refs_2_.refs_0_), custom_call_target="tpu_custom_call" | custom-call | flops 1342177280 | bytes 13893632 | tf_op jit(solution)/shard_map/pallas_call | solution.py:105
  366.3 2.0 shard_map.308
  369.6 2.1 copy-done.23
  373.1 12.6 %fusion.7 = f32[7,7,32,512]{3,2,1,0:T(8,128)S(1)} fusion(bf16[7,7,32,512]{3,2,1,0:T(8,128)(2,1)S(1)} %bitcast.100, bf16[3,3,512,512]{3,2,1,0:T(8,128)(2,1)} %bitcast.117), kind=kOutput, calls=%fused_computation.26 | convolution fusion | flops 6056574976 | bytes 9535488 | tf_op jit(solution)/shard_map/conv_general_dilated | solution.py:1067
  385.7 5.8 fusion.8
  391.6 3.5 shard_map.311
  397.2 2.8 collective-permute-start.77
  400.1 9.0 %fusion.9.refs_1_ = f32[3,3,512,512]{3,2,1,0:T(8,128)S(1)} fusion(bf16[7,7,32,512]{3,2,1,0:T(8,128)(2,1)S(1)} %bitcast.114, bf16[7,7,32,512]{3,2,1,0:T(8,128)(2,1)S(1)} %bitcast.101), kind=kOutput, calls=%fused_computation.28 | convolution fusion | flops 6056574976 | bytes 12648448 | tf_op jit(solution)/shard_map/conv_general_dilated | solution.py:1078
  409.3 3.6 collective-permute-start.79
  413.7 7.8 %convolution_add_fusion = f32[3,3,512,512]{3,2,1,0:T(8,128)S(1)} fusion(f32[3,3,512,512]{3,2,1,0:T(8,128)S(1)} %fusion.9.refs_1_, bf16[3,3,128,512]{3,2,1,0:T(8,128)(2,1)} %bitcast.116, bf16[3,3,128,512]{3,2,1,0:T(8,128)(2,1)S(1)} %bitcast.98), kind=kOutput, calls=%fused_computation | convolution fusion | flops 3290693632 | bytes 21233664 | tf_op jit(solution)/shard_map/conv_general_dilated | solution.py:1078
  423.1 2.0 copy-done
  425.1 2.5 shard_map.319.refs_5_
  428.3 13.7 %collective-permute-done.81.refs_2_ = f32[1,8,16,1024]{3,2,1,0:T(8,128)S(1)} collective-permute-done((f32[1,8,16,1024]{3,2,1,0:T(8,128)S(1)}, f32[1,8,16,1024]{3,2,1,0:T(8,128)S(1)}, u32[]{:S(2)}, u32[]{:S(2)}) %collective-permute-start.81) | collective-permute-done | bytes 524320 | tf_op jit(solution)/shard_map/ppermute | solution.py:328
  445.7 11.0 %shard_map.320 = (f32[1,16,64,512]{3,2,1,0:T(8,128)S(1)}, f32[1,16,64,512]{3,2,1,0:T(8,128)}) custom-call(s32[1]{0:T(128)} %bitcast.20.refs_0_, bf16[1568,2048]{1,0:T(8,128)(2,1)} %bitcast.126, bf16[1568,512]{1,0:T(8,128)(2,1)S(1)} %get-tuple-element.243.refs_2_, bf16[1152,2048]{1,0:T(8,128)(2,1)} %bitcast.130, ...), custom_call_target="tpu_custom_call" | custom-call | flops 5704253440 | bytes 18120704 | tf_op jit(solution)/shard_map/pallas_call | solution.py:105
  456.8 3.7 copy-done.1
  460.5 3.0 shard_map.321
  467.6 2.0 shard_map.322
  471.3 15.3 %shard_map.323 = (bf16[1568,2048]{1,0:T(8,128)(2,1)}, bf16[1152,2048]{1,0:T(8,128)(2,1)}) custom-call(bf16[1568,2048]{1,0:T(8,128)(2,1)} %get-tuple-element.202.refs_0_, bf16[1152,2048]{1,0:T(8,128)(2,1)} %get-tuple-element.203.refs_1_, bf16[1568,512]{1,0:T(8,128)(2,1)S(1)} %copy-done.106, bf16[1152,512]{1,0:T(8,128)(2,1)S(1)} %copy-done.109, ...), custom_call_target="tpu_custom_call" | custom-call | flops 5704253440 | bytes 27164672 | tf_op jit(solution)/shard_map/pallas_call | solution.py:105
  486.5 12.4 %collective-permute-done.89.refs_2_ = f32[1,4,16,1024]{3,2,1,0:T(8,128)S(1)} collective-permute-done((f32[1,4,16,1024]{3,2,1,0:T(8,128)S(1)}, f32[1,4,16,1024]{3,2,1,0:T(8,128)S(1)}, u32[]{:S(2)}, u32[]{:S(2)}) %collective-permute-start.89) | collective-permute-done | bytes 262176 | tf_op jit(solution)/shard_map/ppermute | solution.py:328
  498.9 2.9 copy-done.17
  505.2 3.9 collective-permute-done.85.refs_2_
  510.8 19.0 %collective-permute-done.86.refs_4_ = f32[1,8,64,256]{3,2,1,0:T(8,128)S(1)} collective-permute-done((f32[1,8,64,256]{3,2,1,0:T(8,128)S(1)}, f32[1,8,64,256]{3,2,1,0:T(8,128)S(1)}, u32[]{:S(2)}, u32[]{:S(2)}) %collective-permute-start.86) | collective-permute-done | bytes 524320 | tf_op jit(solution)/shard_map/ppermute | solution.py:328
  535.0 3.9 collective-permute-done.91.refs_2_
  541.2 14.2 %collective-permute-done.99.refs_2_ = f32[1,2,16,2048]{3,2,1,0:T(8,128)S(1)} collective-permute-done((f32[1,2,16,2048]{3,2,1,0:T(8,128)S(1)}, f32[1,2,16,2048]{3,2,1,0:T(8,128)S(1)}, u32[]{:S(2)}, u32[]{:S(2)}) %collective-permute-start.99) | collective-permute-done | bytes 262176 | tf_op jit(solution)/shard_map/ppermute | solution.py:328
  556.7 3.9 collective-permute-done.97.refs_2_
  560.5 3.1 collective-permute-done.103.refs_2_
  565.6 2.3 collective-permute-start.101
  568.5 10.8 %collective-permute-done.104.refs_1_ = f32[1,1,80,256]{3,2,1,0:T(8,128)S(1)} collective-permute-done((f32[1,1,80,256]{3,2,1,0:T(8,128)S(1)}, f32[1,1,80,256]{3,2,1,0:T(8,128)S(1)}, u32[]{:S(2)}, u32[]{:S(2)}) %collective-permute-start.104) | collective-permute-done | bytes 81952 | tf_op jit(solution)/shard_map/ppermute | solution.py:328
  580.6 5.7 collective-permute-done.100.refs_1_
  (534 shorter events, 181.7 us)
Async XLA Ops:
  7.2 350.5 %all-gather.2.cloned.1.call-start = ((), (), s32[]{:S(2)}) async-start(), calls=%async_computation.2 | async-start | bytes 11796480 | tf_op jit(solution)/shard_map/all_gather | solution.py:1255
  36.8 5.4 collective-permute-start.6
  71.6 5.4 collective-permute-start.13
  108.5 5.6 collective-permute-start.19
  112.3 5.6 collective-permute-start.20
  149.4 6.3 %collective-permute-start.25 = (f32[1,4224]{1,0:T(1,128)S(1)}, f32[1,4224]{1,0:T(1,128)S(1)}, u32[]{:S(2)}, u32[]{:S(2)}) collective-permute-start(f32[1,4224]{1,0:T(1,128)S(1)} %shard_map.286.refs_0_), channel_id=1, source_target_pairs={{0,8},{1,9},{2,10},{3,11},{4,12},{5,13},{6,14},{7,15},{8,0},{9,1},... | collective-permute-start | bytes 50696 | tf_op jit(solution)/shard_map/ppermute | solution.py:136
  149.4 6.2 %collective-permute-start.26 = (f32[1,4224]{1,0:T(1,128)S(1)}, f32[1,4224]{1,0:T(1,128)S(1)}, u32[]{:S(2)}, u32[]{:S(2)}) collective-permute-start(f32[1,4224]{1,0:T(1,128)S(1)} %shard_map.286.refs_0_), channel_id=1, source_target_pairs={{0,16},{1,17},{2,18},{3,19},{4,20},{5,21},{6,22},{7,23},{8,24},{9,... | collective-permute-start | bytes 50696 | tf_op jit(solution)/shard_map/ppermute | solution.py:136
  150.2 5.5 collective-permute-start.27
  169.4 5.6 collective-permute-start.33
  173.2 5.6 collective-permute-start.34
  187.6 4.8 collective-permute-start.40
  188.4 5.6 collective-permute-start.41
  197.2 4.9 collective-permute-start.43
  199.3 4.8 collective-permute-start.45
  204.9 6.0 %collective-permute-start.46 = (f32[1,6144]{1,0:T(1,128)S(1)}, f32[1,6144]{1,0:T(1,128)S(1)}, u32[]{:S(2)}, u32[]{:S(2)}) collective-permute-start(f32[1,6144]{1,0:T(1,128)S(1)} %add_add_fusion.refs_0_), channel_id=1, source_target_pairs={{0,8},{1,9},{2,10},{3,11},{4,12},{5,13},{6,14},{7,15},{8,0},{9,1},... | collective-permute-start | bytes 73736 | tf_op jit(solution)/shard_map/ppermute | solution.py:136
  205.3 5.6 collective-permute-start.47
  209.1 5.6 collective-permute-start.48
  223.1 8.6 %collective-permute-start.50 = (f32[1,4224]{1,0:T(1,128)S(1)}, f32[1,4224]{1,0:T(1,128)}, u32[]{:S(2)}, u32[]{:S(2)}) collective-permute-start(f32[1,4224]{1,0:T(1,128)S(1)} %add.140.refs_5_.refs_0_), channel_id=1, source_target_pairs={{0,2},{1,3},{2,0},{3,1},{4,6},{5,7},{6,4},{7,5},{8,10},{9,11},{10,... | collective-permute-start | bytes 50696 | tf_op jit(solution)/shard_map/ppermute | solution.py:136
  224.6 7.1 %collective-permute-start.51 = (f32[1,4224]{1,0:T(1,128)S(1)}, f32[1,4224]{1,0:T(1,128)}, u32[]{:S(2)}, u32[]{:S(2)}) collective-permute-start(f32[1,4224]{1,0:T(1,128)S(1)} %add.140.refs_5_.refs_0_), channel_id=1, source_target_pairs={{0,4},{1,5},{2,6},{3,7},{4,0},{5,1},{6,2},{7,3},{8,12},{9,13},{10,... | collective-permute-start | bytes 50696 | tf_op jit(solution)/shard_map/ppermute | solution.py:136
  225.1 6.9 %collective-permute-start.52 = (f32[1,4224]{1,0:T(1,128)S(1)}, f32[1,4224]{1,0:T(1,128)}, u32[]{:S(2)}, u32[]{:S(2)}) collective-permute-start(f32[1,4224]{1,0:T(1,128)S(1)} %add.140.refs_5_.refs_0_), channel_id=1, source_target_pairs={{0,6},{1,7},{2,4},{3,5},{4,2},{5,3},{6,0},{7,1},{8,14},{9,15},{10,... | collective-permute-start | bytes 50696 | tf_op jit(solution)/shard_map/ppermute | solution.py:136
  233.7 5.5 collective-permute-start.55
  281.8 5.0 collective-permute-start.60
  286.9 5.9 collective-permute-start.62
  291.1 5.5 collective-permute-start.63
  299.5 31.2 %all-to-all-start = ((f32[8,160,256]{2,1,0:T(8,128)}), f32[8,160,256]{2,1,0:T(8,128)}, u32[]{:S(2)}, u32[]{:S(2)}) async-start(f32[8,160,256]{2,1,0:T(8,128)} %copy-done.10), calls=%async_computation | async-start | bytes 2621440 | tf_op jit(solution)/shard_map/all_to_all | solution.py:1278
  303.8 284.0 %reduce-scatter.2.cloned.1.call-start = ((), (), s32[]{:S(2)}) async-start(), calls=%async_computation.3 | async-start | bytes 2621440 | tf_op jit(solution)/shard_map/reduce_scatter | solution.py:1312
  344.7 20.6 %collective-permute-start.71 = (f32[1,16,16,2048]{3,2,1,0:T(8,128)}, f32[1,16,16,2048]{3,2,1,0:T(8,128)}, u32[]{:S(2)}, u32[]{:S(2)}) collective-permute-start(f32[1,16,16,2048]{3,2,1,0:T(8,128)} %get-tuple-element.223), channel_id=1, source_target_pairs={{0,1},{1,0},{2,3},{3,2},{4,5},{5,4},{6,7},{7,6},{8,9},{9,8},{10,11... | collective-permute-start | bytes 6291464 | tf_op jit(solution)/shard_map/ppermute | solution.py:328
  345.0 6.5 %collective-permute-start.65 = (f32[1,1152]{1,0:T(1,128)S(1)}, f32[1,1152]{1,0:T(1,128)S(1)}, u32[]{:S(2)}, u32[]{:S(2)}) collective-permute-start(f32[1,1152]{1,0:T(1,128)S(1)} %add.148.refs_5_.refs_0_), channel_id=1, source_target_pairs={{0,2},{1,3},{2,0},{3,1},{4,6},{5,7},{6,4},{7,5},{8,10},{9,11},{10,... | collective-permute-start | bytes 13832 | tf_op jit(solution)/shard_map/ppermute | solution.py:136
  346.6 6.6 %collective-permute-start.66 = (f32[1,1152]{1,0:T(1,128)S(1)}, f32[1,1152]{1,0:T(1,128)S(1)}, u32[]{:S(2)}, u32[]{:S(2)}) collective-permute-start(f32[1,1152]{1,0:T(1,128)S(1)} %add.148.refs_5_.refs_0_), channel_id=1, source_target_pairs={{0,4},{1,5},{2,6},{3,7},{4,0},{5,1},{6,2},{7,3},{8,12},{9,13},{10,... | collective-permute-start | bytes 13832 | tf_op jit(solution)/shard_map/ppermute | solution.py:136
  348.4 4.9 collective-permute-start.67
  348.4 19.8 %collective-permute-start.72 = (f32[1,8,80,128]{3,2,1,0:T(8,128)}, f32[1,8,80,128]{3,2,1,0:T(8,128)}, u32[]{:S(2)}, u32[]{:S(2)}) collective-permute-start(f32[1,8,80,128]{3,2,1,0:T(8,128)} %get-tuple-element.225), channel_id=1, source_target_pairs={{0,2},{1,3},{2,0},{3,1},{4,6},{5,7},{6,4},{7,5},{8,10},{9,11},{10,... | collective-permute-start | bytes 983048 | tf_op jit(solution)/shard_map/ppermute | solution.py:328
  351.5 16.8 %collective-permute-start.73 = (f32[1,8,80,128]{3,2,1,0:T(8,128)}, f32[1,8,80,128]{3,2,1,0:T(8,128)}, u32[]{:S(2)}, u32[]{:S(2)}) collective-permute-start(f32[1,8,80,128]{3,2,1,0:T(8,128)} %get-tuple-element.227), channel_id=1, source_target_pairs={{0,4},{1,5},{2,6},{3,7},{4,0},{5,1},{6,2},{7,3},{8,12},{9,13},{10,... | collective-permute-start | bytes 983048 | tf_op jit(solution)/shard_map/ppermute | solution.py:328
  353.3 11.4 %collective-permute-start.69 = (f32[1,1152]{1,0:T(1,128)S(1)}, f32[1,1152]{1,0:T(1,128)S(1)}, u32[]{:S(2)}, u32[]{:S(2)}) collective-permute-start(f32[1,1152]{1,0:T(1,128)S(1)} %add_add_fusion.6.refs_2_.refs_0_), channel_id=1, source_target_pairs={{0,16},{1,17},{2,18},{3,19},{4,20},{5,21},{6,22},{7,23},{8,24},{9,... | collective-permute-start | bytes 13832 | tf_op jit(solution)/shard_map/ppermute | solution.py:136
  356.9 7.8 %collective-permute-start.70 = (f32[1,1152]{1,0:T(1,128)S(1)}, f32[1,1152]{1,0:T(1,128)S(1)}, u32[]{:S(2)}, u32[]{:S(2)}) collective-permute-start(f32[1,1152]{1,0:T(1,128)S(1)} %add_add_fusion.6.refs_2_.refs_0_), channel_id=1, source_target_pairs={{0,24},{1,25},{2,26},{3,27},{4,28},{5,29},{6,30},{7,31},{8,16},{9,... | collective-permute-start | bytes 13832 | tf_op jit(solution)/shard_map/ppermute | solution.py:136
  396.5 12.5 %collective-permute-start.75 = (f32[1,1152]{1,0:T(1,128)S(1)}, f32[1,1152]{1,0:T(1,128)S(1)}, u32[]{:S(2)}, u32[]{:S(2)}) collective-permute-start(f32[1,1152]{1,0:T(1,128)S(1)} %add.152.refs_1_.refs_0_), channel_id=1, source_target_pairs={{0,2},{1,3},{2,0},{3,1},{4,6},{5,7},{6,4},{7,5},{8,10},{9,11},{10,... | collective-permute-start | bytes 13832 | tf_op jit(solution)/shard_map/ppermute | solution.py:136
  397.0 12.1 %collective-permute-start.76 = (f32[1,1152]{1,0:T(1,128)S(1)}, f32[1,1152]{1,0:T(1,128)S(1)}, u32[]{:S(2)}, u32[]{:S(2)}) collective-permute-start(f32[1,1152]{1,0:T(1,128)S(1)} %add.152.refs_1_.refs_0_), channel_id=1, source_target_pairs={{0,4},{1,5},{2,6},{3,7},{4,0},{5,1},{6,2},{7,3},{8,12},{9,13},{10,... | collective-permute-start | bytes 13832 | tf_op jit(solution)/shard_map/ppermute | solution.py:136
  397.2 11.8 %collective-permute-start.77 = (f32[1,1152]{1,0:T(1,128)S(1)}, f32[1,1152]{1,0:T(1,128)S(1)}, u32[]{:S(2)}, u32[]{:S(2)}) collective-permute-start(f32[1,1152]{1,0:T(1,128)S(1)} %add.152.refs_1_.refs_0_), channel_id=1, source_target_pairs={{0,6},{1,7},{2,4},{3,5},{4,2},{5,3},{6,0},{7,1},{8,14},{9,15},{10,... | collective-permute-start | bytes 13832 | tf_op jit(solution)/shard_map/ppermute | solution.py:136
  409.2 12.3 %collective-permute-start.78 = (f32[1,1152]{1,0:T(1,128)S(1)}, f32[1,1152]{1,0:T(1,128)S(1)}, u32[]{:S(2)}, u32[]{:S(2)}) collective-permute-start(f32[1,1152]{1,0:T(1,128)S(1)} %add_add_fusion.5.refs_1_.refs_0_), channel_id=1, source_target_pairs={{0,8},{1,9},{2,10},{3,11},{4,12},{5,13},{6,14},{7,15},{8,0},{9,1},... | collective-permute-start | bytes 13832 | tf_op jit(solution)/shard_map/ppermute | solution.py:136
  409.3 12.2 %collective-permute-start.79 = (f32[1,1152]{1,0:T(1,128)S(1)}, f32[1,1152]{1,0:T(1,128)S(1)}, u32[]{:S(2)}, u32[]{:S(2)}) collective-permute-start(f32[1,1152]{1,0:T(1,128)S(1)} %add_add_fusion.5.refs_1_.refs_0_), channel_id=1, source_target_pairs={{0,16},{1,17},{2,18},{3,19},{4,20},{5,21},{6,22},{7,23},{8,24},{9,... | collective-permute-start | bytes 13832 | tf_op jit(solution)/shard_map/ppermute | solution.py:136
  412.9 8.7 %collective-permute-start.80 = (f32[1,1152]{1,0:T(1,128)S(1)}, f32[1,1152]{1,0:T(1,128)S(1)}, u32[]{:S(2)}, u32[]{:S(2)}) collective-permute-start(f32[1,1152]{1,0:T(1,128)S(1)} %add_add_fusion.5.refs_1_.refs_0_), channel_id=1, source_target_pairs={{0,24},{1,25},{2,26},{3,27},{4,28},{5,29},{6,30},{7,31},{8,16},{9,... | collective-permute-start | bytes 13832 | tf_op jit(solution)/shard_map/ppermute | solution.py:136
  427.6 29.1 %collective-permute-start.84 = (f32[9,16,16,512]{3,2,1,0:T(8,128)}, f32[9,16,16,512]{3,2,1,0:T(8,128)}, u32[]{:S(2)}, u32[]{:S(2)}) collective-permute-start(f32[9,16,16,512]{3,2,1,0:T(8,128)} %shard_map.319.refs_5_), channel_id=1, source_target_pairs={{0,1},{1,0},{2,3},{3,2},{4,5},{5,4},{6,7},{7,6},{8,9},{9,8},{10,11... | collective-permute-start | bytes 14155784 | tf_op jit(solution)/shard_map/ppermute | solution.py:328
  427.6 14.3 %collective-permute-start.81 = (f32[1,8,16,1024]{3,2,1,0:T(8,128)S(1)}, f32[1,8,16,1024]{3,2,1,0:T(8,128)S(1)}, u32[]{:S(2)}, u32[]{:S(2)}) collective-permute-start(f32[1,8,16,1024]{3,2,1,0:T(8,128)S(1)} %get-tuple-element.239), channel_id=1, source_target_pairs={{0,2},{1,3},{2,0},{3,1},{4,6},{5,7},{6,4},{7,5},{8,10},{9,11},{10,... | collective-permute-start | bytes 1572872 | tf_op jit(solution)/shard_map/ppermute | solution.py:328
  428.0 14.1 %collective-permute-start.82 = (f32[1,8,16,1024]{3,2,1,0:T(8,128)S(1)}, f32[1,8,16,1024]{3,2,1,0:T(8,128)S(1)}, u32[]{:S(2)}, u32[]{:S(2)}) collective-permute-start(f32[1,8,16,1024]{3,2,1,0:T(8,128)S(1)} %get-tuple-element.241), channel_id=1, source_target_pairs={{0,4},{1,5},{2,6},{3,7},{4,0},{5,1},{6,2},{7,3},{8,12},{9,13},{10,... | collective-permute-start | bytes 1572872 | tf_op jit(solution)/shard_map/ppermute | solution.py:328
  456.7 10.9 %collective-permute-start.83 = (f32[1,16,64,512]{3,2,1,0:T(8,128)}, f32[1,16,64,512]{3,2,1,0:T(8,128)}, u32[]{:S(2)}, u32[]{:S(2)}) collective-permute-start(f32[1,16,64,512]{3,2,1,0:T(8,128)} %get-tuple-element.246), channel_id=1, source_target_pairs={{0,1},{1,0},{2,3},{3,2},{4,5},{5,4},{6,7},{7,6},{8,9},{9,8},{10,11... | collective-permute-start | bytes 6291464 | tf_op jit(solution)/shard_map/ppermute | solution.py:328
  463.4 38.4 %collective-permute-start.87 = (f32[9,8,16,256]{3,2,1,0:T(8,128)S(1)}, f32[9,8,16,256]{3,2,1,0:T(8,128)S(1)}, u32[]{:S(2)}, u32[]{:S(2)}) collective-permute-start(f32[9,8,16,256]{3,2,1,0:T(8,128)S(1)} %get-tuple-element.254), channel_id=1, source_target_pairs={{0,2},{1,3},{2,0},{3,1},{4,6},{5,7},{6,4},{7,5},{8,10},{9,11},{10,... | collective-permute-start | bytes 3538952 | tf_op jit(solution)/shard_map/ppermute | solution.py:328
  465.1 36.7 %collective-permute-start.88 = (f32[9,8,16,256]{3,2,1,0:T(8,128)S(1)}, f32[9,8,16,256]{3,2,1,0:T(8,128)S(1)}, u32[]{:S(2)}, u32[]{:S(2)}) collective-permute-start(f32[9,8,16,256]{3,2,1,0:T(8,128)S(1)} %get-tuple-element.256), channel_id=1, source_target_pairs={{0,4},{1,5},{2,6},{3,7},{4,0},{5,1},{6,2},{7,3},{8,12},{9,13},{10,... | collective-permute-start | bytes 3538952 | tf_op jit(solution)/shard_map/ppermute | solution.py:328
  465.5 33.4 %collective-permute-start.89 = (f32[1,4,16,1024]{3,2,1,0:T(8,128)S(1)}, f32[1,4,16,1024]{3,2,1,0:T(8,128)S(1)}, u32[]{:S(2)}, u32[]{:S(2)}) collective-permute-start(f32[1,4,16,1024]{3,2,1,0:T(8,128)S(1)} %copy-done.113), channel_id=1, source_target_pairs={{0,4},{1,5},{2,6},{3,7},{4,0},{5,1},{6,2},{7,3},{8,12},{9,13},{10,... | collective-permute-start | bytes 786440 | tf_op jit(solution)/shard_map/ppermute | solution.py:328
  467.2 31.7 %collective-permute-start.90 = (f32[1,4,16,1024]{3,2,1,0:T(8,128)S(1)}, f32[1,4,16,1024]{3,2,1,0:T(8,128)S(1)}, u32[]{:S(2)}, u32[]{:S(2)}) collective-permute-start(f32[1,4,16,1024]{3,2,1,0:T(8,128)S(1)} %copy-done.111), channel_id=1, source_target_pairs={{0,2},{1,3},{2,0},{3,1},{4,6},{5,7},{6,4},{7,5},{8,10},{9,11},{10,... | collective-permute-start | bytes 786440 | tf_op jit(solution)/shard_map/ppermute | solution.py:328
  469.5 39.6 %collective-permute-start.85 = (f32[1,8,64,256]{3,2,1,0:T(8,128)S(1)}, f32[1,8,64,256]{3,2,1,0:T(8,128)S(1)}, u32[]{:S(2)}, u32[]{:S(2)}) collective-permute-start(f32[1,8,64,256]{3,2,1,0:T(8,128)S(1)} %get-tuple-element.251), channel_id=1, source_target_pairs={{0,2},{1,3},{2,0},{3,1},{4,6},{5,7},{6,4},{7,5},{8,10},{9,11},{10,... | collective-permute-start | bytes 1572872 | tf_op jit(solution)/shard_map/ppermute | solution.py:328
  502.2 29.6 %collective-permute-start.93 = (f32[9,4,16,256]{3,2,1,0:T(8,128)S(1)}, f32[9,4,16,256]{3,2,1,0:T(8,128)S(1)}, u32[]{:S(2)}, u32[]{:S(2)}) collective-permute-start(f32[9,4,16,256]{3,2,1,0:T(8,128)S(1)} %get-tuple-element.266), channel_id=1, source_target_pairs={{0,4},{1,5},{2,6},{3,7},{4,0},{5,1},{6,2},{7,3},{8,12},{9,13},{10,... | collective-permute-start | bytes 1769480 | tf_op jit(solution)/shard_map/ppermute | solution.py:328
  502.5 29.3 %collective-permute-start.94 = (f32[9,4,16,256]{3,2,1,0:T(8,128)S(1)}, f32[9,4,16,256]{3,2,1,0:T(8,128)S(1)}, u32[]{:S(2)}, u32[]{:S(2)}) collective-permute-start(f32[9,4,16,256]{3,2,1,0:T(8,128)S(1)} %get-tuple-element.268), channel_id=1, source_target_pairs={{0,2},{1,3},{2,0},{3,1},{4,6},{5,7},{6,4},{7,5},{8,10},{9,11},{10,... | collective-permute-start | bytes 1769480 | tf_op jit(solution)/shard_map/ppermute | solution.py:328
  503.2 26.6 %collective-permute-start.86 = (f32[1,8,64,256]{3,2,1,0:T(8,128)S(1)}, f32[1,8,64,256]{3,2,1,0:T(8,128)S(1)}, u32[]{:S(2)}, u32[]{:S(2)}) collective-permute-start(f32[1,8,64,256]{3,2,1,0:T(8,128)S(1)} %get-tuple-element.253), channel_id=1, source_target_pairs={{0,4},{1,5},{2,6},{3,7},{4,0},{5,1},{6,2},{7,3},{8,12},{9,13},{10,... | collective-permute-start | bytes 1572872 | tf_op jit(solution)/shard_map/ppermute | solution.py:328
  504.9 26.8 %collective-permute-start.95 = (f32[1,4,80,128]{3,2,1,0:T(8,128)S(1)}, f32[1,4,80,128]{3,2,1,0:T(8,128)S(1)}, u32[]{:S(2)}, u32[]{:S(2)}) collective-permute-start(f32[1,4,80,128]{3,2,1,0:T(8,128)S(1)} %copy-done.117), channel_id=1, source_target_pairs={{0,4},{1,5},{2,6},{3,7},{4,0},{5,1},{6,2},{7,3},{8,12},{9,13},{10,... | collective-permute-start | bytes 491528 | tf_op jit(solution)/shard_map/ppermute | solution.py:328
  509.1 22.6 %collective-permute-start.96 = (f32[1,4,80,128]{3,2,1,0:T(8,128)S(1)}, f32[1,4,80,128]{3,2,1,0:T(8,128)S(1)}, u32[]{:S(2)}, u32[]{:S(2)}) collective-permute-start(f32[1,4,80,128]{3,2,1,0:T(8,128)S(1)} %copy-done.115), channel_id=1, source_target_pairs={{0,2},{1,3},{2,0},{3,1},{4,6},{5,7},{6,4},{7,5},{8,10},{9,11},{10,... | collective-permute-start | bytes 491528 | tf_op jit(solution)/shard_map/ppermute | solution.py:328
  532.0 24.6 %collective-permute-start.98 = (f32[9,2,16,512]{3,2,1,0:T(8,128)S(1)}, f32[9,2,16,512]{3,2,1,0:T(8,128)S(1)}, u32[]{:S(2)}, u32[]{:S(2)}) collective-permute-start(f32[9,2,16,512]{3,2,1,0:T(8,128)S(1)} %get-tuple-element.276), channel_id=1, source_target_pairs={{0,8},{1,9},{2,10},{3,11},{4,12},{5,13},{6,14},{7,15},{8,0},{9,1},... | collective-permute-start | bytes 1769480 | tf_op jit(solution)/shard_map/ppermute | solution.py:328
  532.1 6.8 %collective-permute-start.91 = (f32[1,4,64,256]{3,2,1,0:T(8,128)S(1)}, f32[1,4,64,256]{3,2,1,0:T(8,128)S(1)}, u32[]{:S(2)}, u32[]{:S(2)}) collective-permute-start(f32[1,4,64,256]{3,2,1,0:T(8,128)S(1)} %get-tuple-element.263), channel_id=1, source_target_pairs={{0,4},{1,5},{2,6},{3,7},{4,0},{5,1},{6,2},{7,3},{8,12},{9,13},{10,... | collective-permute-start | bytes 786440 | tf_op jit(solution)/shard_map/ppermute | solution.py:328
  532.5 6.5 %collective-permute-start.92 = (f32[1,4,64,256]{3,2,1,0:T(8,128)S(1)}, f32[1,4,64,256]{3,2,1,0:T(8,128)S(1)}, u32[]{:S(2)}, u32[]{:S(2)}) collective-permute-start(f32[1,4,64,256]{3,2,1,0:T(8,128)S(1)} %get-tuple-element.265), channel_id=1, source_target_pairs={{0,2},{1,3},{2,0},{3,1},{4,6},{5,7},{6,4},{7,5},{8,10},{9,11},{10,... | collective-permute-start | bytes 786440 | tf_op jit(solution)/shard_map/ppermute | solution.py:328
  533.0 22.3 %collective-permute-start.99 = (f32[1,2,16,2048]{3,2,1,0:T(8,128)S(1)}, f32[1,2,16,2048]{3,2,1,0:T(8,128)S(1)}, u32[]{:S(2)}, u32[]{:S(2)}) collective-permute-start(f32[1,2,16,2048]{3,2,1,0:T(8,128)S(1)} %get-tuple-element.277), channel_id=1, source_target_pairs={{0,8},{1,9},{2,10},{3,11},{4,12},{5,13},{6,14},{7,15},{8,0},{9,1},... | collective-permute-start | bytes 786440 | tf_op jit(solution)/shard_map/ppermute | solution.py:328
  539.1 21.4 %collective-permute-start.97 = (f32[1,2,64,512]{3,2,1,0:T(8,128)S(1)}, f32[1,2,64,512]{3,2,1,0:T(8,128)S(1)}, u32[]{:S(2)}, u32[]{:S(2)}) collective-permute-start(f32[1,2,64,512]{3,2,1,0:T(8,128)S(1)} %get-tuple-element.275), channel_id=1, source_target_pairs={{0,8},{1,9},{2,10},{3,11},{4,12},{5,13},{6,14},{7,15},{8,0},{9,1},... | collective-permute-start | bytes 786440 | tf_op jit(solution)/shard_map/ppermute | solution.py:328
  540.9 22.7 %collective-permute-start.103 = (f32[1,2,80,256]{3,2,1,0:T(8,128)S(1)}, f32[1,2,80,256]{3,2,1,0:T(8,128)S(1)}, u32[]{:S(2)}, u32[]{:S(2)}) collective-permute-start(f32[1,2,80,256]{3,2,1,0:T(8,128)S(1)} %get-tuple-element.292), channel_id=1, source_target_pairs={{0,8},{1,9},{2,10},{3,11},{4,12},{5,13},{6,14},{7,15},{8,0},{9,1},... | collective-permute-start | bytes 491528 | tf_op jit(solution)/shard_map/ppermute | solution.py:328
  555.4 9.6 %collective-permute-start.102 = (f32[1,1,16,2048]{3,2,1,0:T(8,128)S(1)}, f32[1,1,16,2048]{3,2,1,0:T(8,128)S(1)}, u32[]{:S(2)}, u32[]{:S(2)}) collective-permute-start(f32[1,1,16,2048]{3,2,1,0:T(8,128)S(1)} %get-tuple-element.283), channel_id=1, source_target_pairs={{0,16},{1,17},{2,18},{3,19},{4,20},{5,21},{6,22},{7,23},{8,24},{9,... | collective-permute-start | bytes 393224 | tf_op jit(solution)/shard_map/ppermute | solution.py:328
  563.7 15.6 %collective-permute-start.104 = (f32[1,1,80,256]{3,2,1,0:T(8,128)S(1)}, f32[1,1,80,256]{3,2,1,0:T(8,128)S(1)}, u32[]{:S(2)}, u32[]{:S(2)}) collective-permute-start(f32[1,1,80,256]{3,2,1,0:T(8,128)S(1)} %get-tuple-element.294), channel_id=1, source_target_pairs={{0,16},{1,17},{2,18},{3,19},{4,20},{5,21},{6,22},{7,23},{8,24},{9,... | collective-permute-start | bytes 245768 | tf_op jit(solution)/shard_map/ppermute | solution.py:328
  565.6 21.4 %collective-permute-start.101 = (f32[9,1,16,512]{3,2,1,0:T(8,128)S(1)}, f32[9,1,16,512]{3,2,1,0:T(8,128)S(1)}, u32[]{:S(2)}, u32[]{:S(2)}) collective-permute-start(f32[9,1,16,512]{3,2,1,0:T(8,128)S(1)} %get-tuple-element.282), channel_id=1, source_target_pairs={{0,16},{1,17},{2,18},{3,19},{4,20},{5,21},{6,22},{7,23},{8,24},{9,... | collective-permute-start | bytes 884744 | tf_op jit(solution)/shard_map/ppermute | solution.py:328
  568.0 18.4 %collective-permute-start.100 = (f32[1,1,64,512]{3,2,1,0:T(8,128)S(1)}, f32[1,1,64,512]{3,2,1,0:T(8,128)S(1)}, u32[]{:S(2)}, u32[]{:S(2)}) collective-permute-start(f32[1,1,64,512]{3,2,1,0:T(8,128)S(1)} %get-tuple-element.281), channel_id=1, source_target_pairs={{0,16},{1,17},{2,18},{3,19},{4,20},{5,21},{6,22},{7,23},{8,24},{9,... | collective-permute-start | bytes 393224 | tf_op jit(solution)/shard_map/ppermute | solution.py:328
  (176 other events, 1339.2 us)
Sparse Core Ops, SparseCore 0:
  249.7 72.6 all-gather.1
  456.9 43.8 reduce-scatter.1

commit v2 on v1

--- a/solution.py
+++ b/solution.py
@@ -19,6 +19,8 @@
 TILE = 256
 ROWS = 32
 VMEM_LIMIT = 60 << 20
+GRID_LIMIT = 16 << 20
+SLOTS = 3
 FLOAT = jnp.float32
 HALF = jnp.bfloat16
 
@@ -66,6 +68,11 @@
 
 def whole(dims):
     return pl.BlockSpec(dims, lambda *_: (0,) * len(dims))
+
+
+class Far:
+    def __init__(self, array):
+        self.array = array
 
 
 def call(
@@ -79,21 +86,23 @@
     after=(),
     scalars=(),
     streamed=(),
-    aliases=None,
-    spill=0,
+    scratch=(),
 ):
     flat = out_shape if isinstance(out_shape, (list, tuple)) else [out_shape]
     size = sum(a.size * a.dtype.itemsize for a in args)
     size += sum(math.prod(a.shape) * jnp.dtype(a.dtype).itemsize for a in flat)
     args = [far(a) if k in streamed else a for k, a in enumerate(args)]
     here = pl.BlockSpec(memory_space=pltpu.VMEM)
-    limit = spill
+    limit = 0
     if grid is None:
         in_specs = [here] * len(args)
         out_specs = jax.tree.map(lambda _: here, out_shape)
         limit = max(limit, size + size // 4 + (2 << 20))
     else:
-        limit = 20 << 20
+        limit = GRID_LIMIT + sum(
+            math.prod(a.shape) * jnp.dtype(a.dtype).itemsize for a in scratch[:-1]
+        )
+    limit += sum(a.size * a.dtype.itemsize for a in after if not isinstance(a, Far))
     first, last = len(scalars), len(scalars) + len(args)
 
     def run(*refs):
@@ -107,12 +116,12 @@
         out_shape=out_shape,
         in_specs=[pl.BlockSpec(memory_space=pltpu.SMEM)] * first
         + list(in_specs)
-        + [pl.BlockSpec(memory_space=pl.ANY)] * len(after),
-        input_output_aliases={first + k: v for k, v in (aliases or {}).items()},
+        + [pl.BlockSpec(memory_space=pl.ANY if isinstance(a, Far) else pltpu.VMEM) for a in after],
+        scratch_shapes=list(scratch),
         compiler_params=pltpu.CompilerParams(vmem_limit_bytes=min(limit, VMEM_LIMIT)),
         cost_estimate=pl.CostEstimate(flops=flops, bytes_accessed=size, transcendentals=0),
         **specs,
-    )(*scalars, *args, *after)
+    )(*scalars, *args, *(a.array if isinstance(a, Far) else a for a in after))
 
 
 def copy_kernel(source, out):
@@ -423,13 +432,23 @@
     def shapes(self, channels, dtype, place=shape):
         return [place((s * r, channels), dtype) for s, r in zip(self.steps, self.rows)]
 
-    def run(self, body, args, row_outs, whole_outs, flops, after=(), streamed=(), aliases=None):
+    def run(self, body, args, row_outs, whole_outs, flops, after=(), streamed=()):
         pairs = [a for a in args if isinstance(a, tuple)]
         rest = [a for a in args if not isinstance(a, tuple)]
         in_specs, flat = [], []
-        for pair in pairs:
-            in_specs += self.specs(pair[0].shape[1])
+        scratch = []
+        for k, pair in enumerate(pairs):
             flat += list(pair)
+            if k in streamed:
+                in_specs += [pl.BlockSpec(memory_space=pl.ANY)] * 2
+                scratch += [
+                    pltpu.VMEM((SLOTS, rows, pair[0].shape[1]), pair[0].dtype)
+                    for rows in self.rows
+                ]
+            else:
+                in_specs += self.specs(pair[0].shape[1])
+        if streamed:
+            scratch.append(pltpu.SemaphoreType.DMA((2 * len(streamed), SLOTS)))
         in_specs += [whole(a.shape) for a in rest]
         out_shapes, out_specs = [], []
         for channels, dtype, *place in row_outs:
@@ -441,21 +460,57 @@
 
         def kernel(*refs):
             i = pl.program_id(0)
+            refs, held = refs[: len(refs) - len(scratch)], refs[len(refs) - len(scratch) :]
             given, fixed = refs[: 2 * n_in], refs[2 * n_in : 2 * n_in + n_rest]
             made = refs[2 * n_in + n_rest :]
+
+            def fetch(kind, step, slot):
+                start = step * self.rows[kind]
+                if not isinstance(step, int):
+                    start = pl.multiple_of(start, self.rows[kind])
+                return [
+                    pltpu.make_async_copy(
+                        given[2 * k + kind].at[pl.ds(start, self.rows[kind]), :],
+                        held[2 * n + kind].at[slot],
+                        held[-1].at[2 * n + kind, slot],
+                    )
+                    for n, k in enumerate(streamed)
+                ]
+
+            def start_big(step):
+                for copy in fetch(0, step, lax.rem(step, SLOTS)):
+                    copy.start()
+
+            if streamed:
+
+                @pl.when(i == 0)
+                def _():
+                    for step in range(SLOTS - 1):
+                        for copy in fetch(0, step, step):
+                            copy.start()
+
+                pl.when(i + SLOTS - 1 < self.steps[0])(lambda: start_big(i + SLOTS - 1))
+                for step in range(self.steps[1]):
+
+                    @pl.when(i == self.steps[0] - self.steps[1] + step)
+                    def _(step=step):
+                        for copy in fetch(1, step, step):
+                            copy.start()
+
             for kind in range(2):
                 here = i < self.steps[0] if kind == 0 else i >= self.steps[0]
 
                 @pl.when(here)
                 def _(kind=kind):
-                    body(
-                        i,
-                        kind,
-                        given[kind : 2 * n_in : 2],
-                        fixed,
-                        made[kind : 2 * n_out : 2],
-                        made[2 * n_out :],
-                    )
+                    blocks = list(given[kind : 2 * n_in : 2])
+                    if streamed:
+                        step = i if kind == 0 else i - self.steps[0]
+                        slot = lax.rem(step, SLOTS)
+                        for copy in fetch(kind, step, slot):
+                            copy.wait()
+                        for n, k in enumerate(streamed):
+                            blocks[k] = held[2 * n + kind].at[slot]
+                    body(i, kind, blocks, fixed, made[kind : 2 * n_out : 2], made[2 * n_out :])
 
         made = call(
             kernel,
@@ -467,7 +522,7 @@
             flops=flops,
             after=after,
             streamed=[2 * k + j for k in streamed for j in range(2)],
-            aliases={2 * k + j: 2 * v + j for k, v in (aliases or {}).items() for j in range(2)},
+            scratch=scratch,
         )
         return [tuple(made[2 * k : 2 * k + 2]) for k in range(n_out)] + list(made[2 * n_out :])
 
@@ -480,32 +535,34 @@
     width = value.shape[1]
     here = slice(start, start + width)
     there = slice(channels + start, channels + start + width)
+    rows = value.shape[0]
+    count = jnp.full((1, 1), rows, FLOAT) if kind == 0 else column_sum(weight)
+    pivot = column_sum(value[:ROWS]) * (1.0 / ROWS)
+    means, spreads = [], []
+    for left in range(0, width, TILE):
+        center = pivot[:, left : left + TILE]
+        total, squares = 0.0, 0.0
+        for low in range(0, rows, ROWS):
+            apart = value[low : low + ROWS, left : left + TILE] - center
+            weighted = apart if kind == 0 else apart * weight[low : low + ROWS]
+            total = total + weighted
+            squares = squares + weighted * apart
+        total = column_sum(total) / count
+        means.append(center + total)
+        spreads.append(column_sum(squares) - count * jnp.square(total))
+    mean, spread = jnp.concatenate(means, axis=1), jnp.concatenate(spreads, axis=1)
+
+    before = packed[:, 2 * channels : 2 * channels + 1]
+    part = count / (before + count)
+    old = packed[:, here]
+    delta = mean - old
+    new_mean = old + delta * part
+    new_spread = packed[:, there] + spread + jnp.square(delta) * (before * part)
     if kind == 0:
-        count = jnp.full((1, 1), value.shape[0], FLOAT)
-        mean = column_sum(value) * (1.0 / value.shape[0])
-        spread = column_sum(jnp.square(value - mean))
-    else:
-        count = column_sum(weight)
-        mean = column_sum(value * weight) / count
-        spread = column_sum(jnp.square(value - mean) * weight)
-
-    def begin():
-        packed[:, here] = mean
-        packed[:, there] = spread
-
-    def go_on():
-        before = packed[:, 2 * channels : 2 * channels + 1]
-        part = count / (before + count)
-        old = packed[:, here]
-        delta = mean - old
-        packed[:, here] = old + delta * part
-        packed[:, there] = packed[:, there] + spread + jnp.square(delta) * (before * part)
-
-    if kind == 0:
-        pl.when(i == 0)(begin)
-        pl.when(i > 0)(go_on)
-    else:
-        go_on()
+        new_mean = jnp.where(i == 0, mean, new_mean)
+        new_spread = jnp.where(i == 0, spread, new_spread)
+    packed[:, here] = new_mean
+    packed[:, there] = new_spread
     return count
 
 
@@ -514,17 +571,8 @@
     lanes = slice(2 * channels, 2 * channels + LANES)
     wide_count = jnp.broadcast_to(count, (1, LANES))
 
-    def begin():
-        packed[:, lanes] = wide_count
-
-    def go_on():
-        packed[:, lanes] = packed[:, lanes] + wide_count
-
-    if kind == 0:
-        pl.when(i == 0)(begin)
-        pl.when(i > 0)(go_on)
-    else:
-        go_on()
+    total = packed[:, lanes] + wide_count
+    packed[:, lanes] = jnp.where(i == 0, wide_count, total) if kind == 0 else total
 
 
 def add_sums(i, kind, packed, low, high, start):
@@ -533,21 +581,14 @@
     here = slice(start, start + width)
     there = slice(channels + start, channels + start + width)
 
-    def begin():
-        packed[:, here] = low
-        packed[:, there] = high
-        if start == 0:
-            packed[:, 2 * channels :] = jnp.zeros((1, LANES), FLOAT)
-
-    def go_on():
-        packed[:, here] = packed[:, here] + low
-        packed[:, there] = packed[:, there] + high
-
+    new_low, new_high = packed[:, here] + low, packed[:, there] + high
     if kind == 0:
-        pl.when(i == 0)(begin)
-        pl.when(i > 0)(go_on)
-    else:
-        go_on()
+        new_low = jnp.where(i == 0, low, new_low)
+        new_high = jnp.where(i == 0, high, new_high)
+    packed[:, here] = new_low
+    packed[:, there] = new_high
+    if start == 0:
+        packed[:, 2 * channels :] = jnp.zeros((1, LANES), FLOAT)
 
 
 def reduce_stage(rows, inputs, weight, live):
@@ -746,7 +787,7 @@
     )
 
 
-def slope_stage(rows, grad, value, norm, live):
+def slope_stage(rows, grad, value, norm, live, after):
     mid = grad[0].shape[1]
 
     def body(i, kind, given, fixed, made, totals):
@@ -765,6 +806,7 @@
         [(mid, FLOAT)],
         [(1, 2 * mid + LANES)],
         16 * rows.total() * mid,
+        after,
     )
 
 
@@ -1266,6 +1308,7 @@
         live,
         [head_sum.go()],
     )
+    packed = tie(packed, head_sum.got)
     *back, gain_three, bias_three, _ = settle_back(
         packed, gain_wide, mean_three, root_three, pixel_count, devices
     )
@@ -1287,9 +1330,9 @@
         w_expand,
         [scale_two, offset_two, mean_two, root_two],
         live,
-        [turned],
-    )
-    packed = tie(packed, [plane_pooled])
+        [turned, head_sum.go([turned])],
+    )
+    packed = tie(packed, [Far(plane_pooled), *head_sum.got])
 
     def expand_work(mark):
         made["expand"] = weight_grad(mid_two, grad_third, devices, me, 1, [mark], [1, 3])
@@ -1317,7 +1360,12 @@
     )
     grad_mid_one = flat([conv_back(a, filters) for a in fields(grad_second)])
     grad_one, packed = slope_stage(
-        rows, grad_mid_one, first, [scale_one, offset_one, mean_one, root_one], live
+        rows,
+        grad_mid_one,
+        first,
+        [scale_one, offset_one, mean_one, root_one],
+        live,
+        [*expand_sum.got, *head_sum.got],
     )
 
     def big_work(mark):
@@ -1329,7 +1377,8 @@
         grad = tie(grad_second[1], [mark])
         part = made["big"] + conv_filter(mid_one[1], fields((grad_second[0], grad))[1])
         made["spatial"] = part.reshape(9, devices, mid // devices, mid)
-        return [made["spatial"]]
+        made["send"] = send_rows(made["spatial"], me, [])
+        return [Far(made["send"])]
 
     *back, gain_one, bias_one, _ = settle_back(
         packed,
@@ -1340,21 +1389,17 @@
         devices,
         [big_work, small_work],
     )
-    spatial_send = send_rows(made["spatial"], me, [back[0]])
-    spatial_sum = Scatter(made["spatial"], spatial_send, devices, me)
-    mark = expand_sum.go([back[0]])
+    spatial_sum = Scatter(made["spatial"], made["send"], devices, me)
+    mark = expand_sum.go([head_sum.go([back[0]])])
     grad_first = norm_back_stage(rows, grad_one, first, back, live, [mark])
-    reduce_keep, reduce_send = weight_grad(
-        inputs, grad_first, devices, me, 0, [spatial_send], [0, 2]
-    )
-    reduce_sum = Scatter(reduce_keep, reduce_send, devices, me)
-    mark = spatial_sum.go([reduce_keep])
-    mark = reduce_sum.go([mark])
+    reduce_keep, reduce_send = weight_grad(inputs, grad_first, devices, me, 0, (), [0, 2])
+    mark = spatial_sum.go([reduce_keep, *expand_sum.got, *head_sum.got])
+    reduce_sum = Scatter(reduce_keep, tie(reduce_send, [mark]), devices, me)
+    mark = expand_sum.go([mark])
     grad_inputs = input_grad_stage(rows, grad_residual, grad_first, w_reduce, [mark])
     grad_big, grad_small = fields(grad_inputs)
-    mark = grad_inputs[0]
-    order = (expand_sum, spatial_sum, reduce_sum, head_sum, spatial_sum, reduce_sum, expand_sum)
-    for part in order + (spatial_sum, reduce_sum, head_sum) * 2:
+    mark = expand_sum.go([Far(grad_inputs[0])])
+    for part in (spatial_sum, reduce_sum) * 4:
         if not part.complete():
             mark = part.go([mark])
     head_grad = head_sum.end()[0]

time: 605 us -> 560 us (0.926)
  waiting for transfers between devices: 167 us -> 134 us
  Pallas kernels: 180 us -> 152 us
  local copies, waits for them, and re-layouts: 61.8 us -> 74.2 us
    ppermute x28, waiting for transfers between devices: 95.8 us -> 59.5 us  [cross(): lax.ppermute(value, 'dp', [(i, i ^ 1 << place) for i in range(self.device...]
    pallas_call x67 -> x69, Pallas kernels: 180 us -> 152 us  [call(): pl.pallas_call(run, out_shape=out_shape, in_specs=[pl.BlockSpec(memory_sp...]
    unnamed x269 -> x303, local copies, waits for them, and re-layouts: 58.1 us -> 70.5 us
  transfers between devices with their start and end apart: 108 -> 108, of which waited for: 62 -> 67; matrix products, arithmetic and copies ran while one was open for 4% -> 4% of each run, Pallas kernels for 17% -> 16%
where the time goes in v2:
time: 560 us; the launch traced here: 551 us
  Pallas kernels  152 us (27%)
  waiting for transfers between devices  134 us (24%)
  starting transfers between devices  121 us (22%)
  local copies, waits for them, and re-layouts  74.2 us (13%)
  matrix products  47 us (8%)
  between operations  16.2 us (3%)
  other arithmetic  5.98 us (1%)
    pallas_call x69, Pallas kernels, call(): pl.pallas_call(run, out_shape=out_shape, in_specs=[pl.BlockSpec(memory_sp...  152 us
    ppermute x77, starting transfers between devices, peers(): lax.ppermute(value, 'dp', [(i, i ^ mask) for i in range(devices)])  89.6 us
    ppermute x77, waiting for transfers between devices, peers(): lax.ppermute(value, 'dp', [(i, i ^ mask) for i in range(devices)])  74.8 us
    unnamed x303, local copies, waits for them, and re-layouts  70.5 us
    ppermute x28, waiting for transfers between devices, cross(): lax.ppermute(value, 'dp', [(i, i ^ 1 << place) for i in range(self.device...  59.5 us
    ppermute x28, starting transfers between devices, cross(): lax.ppermute(value, 'dp', [(i, i ^ 1 << place) for i in range(self.device...  27.1 us
    conv_general_dilated x2, matrix products, conv_back(): lax.conv_general_dilated(field, lax.rev(weight, (0, 1)), (1, 1), ((1, 1),...  18.3 us
    conv_general_dilated x2, matrix products, conv_filter(): lax.conv_general_dilated(field, grad, (1, 1), ((1, 1), (1, 1)), dimension...  15.4 us
  transfers between devices with their start and end apart: 108, of which 67 were waited for; matrix products, arithmetic and copies ran while one was open for 4% of the time, Pallas kernels for 16%

profile of v2, /device:TPU:0, one launch (start us, length us, event | category | flops | bytes accessed | tf_op | source)
XLA Modules:
  0.0 550.6 jit_solution(3021655706647870227)
XLA Ops:
  9.8 9.7 %shard_map.271 = (f32[1568,512]{1,0:T(8,128)S(1)}, f32[1152,512]{1,0:T(8,128)S(1)}, f32[1,1152]{1,0:T(1,128)S(1)}) custom-call(bf16[1568,2048]{1,0:T(8,128)(2,1)} %bitcast.124, bf16[1152,2048]{1,0:T(8,128)(2,1)} %bitcast.128, bf16[2048,512]{1,0:T(8,128)(2,1)S(1)} %copy-done.128, f32[384,1]{1,0:T(8,128)S(1)} %bitcast.89), custom_call_target="tpu_custom_call" | custom-call | flops 5704253440 | bytes 18814976 | tf_op jit(solution)/shard_map/pallas_call | solution.py:114
  21.0 2.9 collective-permute-start.1
  25.4 2.0 collective-permute-done.2.refs_2_
  27.4 2.4 collective-permute-done.3.refs_3_
  31.6 2.6 collective-permute-start.5
  36.1 3.5 collective-permute-done.6.refs_3_
  43.0 2.3 copy-done.139
  45.3 5.7 %fusion.6 = f32[3,3,128,512]{3,2,1,0:T(8,128)S(1)} fusion(bf16[3,3,128,512]{3,2,1,0:T(8,128)(2,1)S(1)} %bitcast.116, bf16[3,3,512,512]{3,2,1,0:T(8,128)(2,1)S(1)} %bitcast.119), kind=kOutput, calls=%fused_computation.25 | convolution fusion | flops 3288334336 | bytes 8257536 | tf_op jit(solution)/shard_map/conv_general_dilated | solution.py:1098
  51.0 7.7 %fusion.5 = f32[7,7,32,512]{3,2,1,0:T(8,128)S(1)} fusion(bf16[7,7,32,512]{3,2,1,0:T(8,128)(2,1)S(1)} %bitcast.114, bf16[3,3,512,512]{3,2,1,0:T(8,128)(2,1)S(1)} %bitcast.120), kind=kOutput, calls=%fused_computation.24 | convolution fusion | flops 6056574976 | bytes 9535488 | tf_op jit(solution)/shard_map/conv_general_dilated | solution.py:1098
  67.7 3.6 collective-permute-start.13
  74.9 12.1 %shard_map.279 = (bf16[1568,2048]{1,0:T(8,128)(2,1)}, bf16[1152,2048]{1,0:T(8,128)(2,1)}, bf16[1568,512]{1,0:T(8,128)(2,1)S(1)}, bf16[1152,512]{1,0:T(8,128)(2,1)S(1)}, f32[1,4224]{1,0:T(1,128)S(1)}) custom-call(f32[1568,512]{1,0:T(8,128)S(1)} %bitcast.81, f32[1152,512]{1,0:T(8,128)S(1)} %bitcast.85, f32[1,512]{1,0:T(1,128)S(1)} %get-tuple-element.160.refs_2_.refs_10_, ...), custom_call_target="tpu_custom_call" | custom-call | flops 5704253440 | bytes 21616640 | tf_op jit(solution)/shard_map/pallas_call | solution.py:114
  91.0 1.7 collective-permute-start.16
  94.7 2.6 collective-permute-done.17.refs_3_
  97.8 3.8 collective-permute-start.19
  103.5 3.8 collective-permute-done.20.refs_3_
  109.8 10.3 %shard_map.283 = (f32[32,2048]{1,0:T(8,128)S(1)}, f32[128,2048]{1,0:T(8,128)S(1)}) custom-call(bf16[1568,2048]{1,0:T(8,128)(2,1)} %get-tuple-element.162.refs_0_.refs_2_, bf16[1152,2048]{1,0:T(8,128)(2,1)} %get-tuple-element.163.refs_1_.refs_3_, bf16[1568,2048]{1,0:T(8,128)(2,1)} %bitcast.125, bf16[1152,2048]{1,0:T(8,128)(2,1)} %bitcast.129, ...), custom_call_target="tpu_custom_call" | custom-call | flops 66846720 | bytes 23609344 | tf_op jit(solution)/shard_map/pallas_call | solution.py:114
  120.2 5.7 %shard_map.284 = (f32[160,2048]{1,0:T(8,128)S(1)}, f32[1,4224]{1,0:T(1,128)S(1)}) custom-call(f32[32,2048]{1,0:T(8,128)S(1)} %get-tuple-element.167.refs_0_, f32[128,2048]{1,0:T(8,128)S(1)} %get-tuple-element.168.refs_1_, bf16[2048,2048]{1,0:T(8,128)(2,1)} %refs_6_.1, f32[160,1]{1,0:T(8,128)S(1)} %copy.36.refs_3_.refs_7_.refs_2_), custom_call_target="tpu_custom_call" | custom-call | flops 1342177280 | bytes 11027584 | tf_op jit(solution)/shard_map/pallas_call | solution.py:114
  135.9 3.6 collective-permute-start.27
  152.1 2.5 collective-permute-done.31
  155.0 3.8 collective-permute-start.33
  160.7 3.8 collective-permute-done.34.refs_3_
  170.2 1.8 collective-permute-done.37
  174.0 3.6 collective-permute-start.41
  187.8 2.0 collective-permute-done.45
  191.0 3.8 collective-permute-start.47
  196.6 3.8 collective-permute-done.48.refs_3_
  200.4 5.0 shard_map.292
  219.3 3.6 collective-permute-start.55
  226.1 6.1 %shard_map.296 = (f32[160,2048]{1,0:T(8,128)S(1)}, f32[32,2048]{1,0:T(8,128)S(1)}, f32[128,2048]{1,0:T(8,128)S(1)}) custom-call(f32[160,2048]{1,0:T(8,128)S(1)} %copy-done.44, f32[160,2048]{1,0:T(8,128)S(1)} %copy-done.17, f32[160,1]{1,0:T(8,128)S(1)} %copy-done.47, f32[1,2048]{1,0:T(1,128)S(1)} %get-tuple-element.193.refs_3_, ...), custom_call_target="tpu_custom_call" | custom-call | flops 1342177280 | bytes 13656704 | tf_op jit(solution)/shard_map/pallas_call | solution.py:114
  235.2 3.2 collective-permute-done.56.refs_2_
  242.7 19.2 %shard_map.298 = (bf16[1568,2048]{1,0:T(8,128)(2,1)}, bf16[1152,2048]{1,0:T(8,128)(2,1)}, f32[1,4224]{1,0:T(1,128)S(1)}) custom-call(bf16[1568,2048]{1,0:T(8,128)(2,1)} %get-tuple-element.162.refs_0_.refs_2_, bf16[1152,2048]{1,0:T(8,128)(2,1)} %get-tuple-element.163.refs_1_.refs_3_, bf16[1568,2048]{1,0:T(8,128)(2,1)} %bitcast.126, ...), custom_call_target="tpu_custom_call" | custom-call | flops 89128960 | bytes 34785280 | tf_op jit(solution)/shard_map/pallas_call | solution.py:114
  267.7 2.4 collective-permute-done.62
  270.4 4.0 collective-permute-start.64
  276.0 3.8 collective-permute-done.65.refs_3_
  282.7 4.4 all-to-all-start
  299.7 15.6 %shard_map.303 = (bf16[1568,2048]{1,0:T(8,128)(2,1)}, bf16[1152,2048]{1,0:T(8,128)(2,1)}, f32[1568,512]{1,0:T(8,128)S(1)}, f32[1152,512]{1,0:T(8,128)S(1)}, f32[1,1152]{1,0:T(1,128)S(1)}) custom-call(bf16[1568,2048]{1,0:T(8,128)(2,1)} %get-tuple-element.202.refs_0_, bf16[1152,2048]{1,0:T(8,128)(2,1)} %get-tuple-element.203.refs_1_, ...), custom_call_target="tpu_custom_call" | custom-call | flops 5704253440 | bytes 46700544 | tf_op jit(solution)/shard_map/pallas_call | solution.py:114
  325.4 10.1 %shard_map.305 = (f32[1,16,16,2048]{3,2,1,0:T(8,128)S(1)}, f32[1,16,16,2048]{3,2,1,0:T(8,128)}) custom-call(s32[1]{0:T(128)} %bitcast.20.refs_0_, bf16[1568,512]{1,0:T(8,128)(2,1)S(1)} %copy-done.132, bf16[1568,2048]{1,0:T(8,128)(2,1)} %get-tuple-element.221.refs_2_, bf16[1152,512]{1,0:T(8,128)(2,1)S(1)} %copy-done.134, ...), custom_call_target="tpu_custom_call" | custom-call | flops 5704253440 | bytes 18120704 | tf_op jit(solution)/shard_map/pallas_call | solution.py:114
  343.1 2.4 collective-permute-start.73
  346.6 6.0 %shard_map.307.refs_1_ = f32[256,2048]{1,0:T(8,128)S(1)} custom-call(f32[1280,256]{1,0:T(8,128)} %bitcast.24.refs_1_.refs_0_, f32[1280,2048]{1,0:T(8,128)} %all-gather.2.cloned.1.call-done.refs_1_, f32[1,1152]{1,0:T(1,128)S(1)} %add_add_fusion.6.refs_2_.refs_0_), custom_call_target="tpu_custom_call" | custom-call | flops 1342177280 | bytes 13893632 | tf_op jit(solution)/shard_map/pallas_call | solution.py:114
  359.9 2.0 shard_map.310
  363.0 1.9 copy-done.26
  366.2 12.6 %fusion.7 = f32[7,7,32,512]{3,2,1,0:T(8,128)S(1)} fusion(bf16[7,7,32,512]{3,2,1,0:T(8,128)(2,1)S(1)} %bitcast.101, bf16[3,3,512,512]{3,2,1,0:T(8,128)(2,1)} %bitcast.118), kind=kOutput, calls=%fused_computation.26 | convolution fusion | flops 6056574976 | bytes 9535488 | tf_op jit(solution)/shard_map/conv_general_dilated | solution.py:1109
  381.1 5.7 %fusion.8 = f32[3,3,128,512]{3,2,1,0:T(8,128)S(1)} fusion(bf16[3,3,128,512]{3,2,1,0:T(8,128)(2,1)S(1)} %bitcast.88, bf16[3,3,512,512]{3,2,1,0:T(8,128)(2,1)S(1)} %bitcast.123), kind=kOutput, calls=%fused_computation.27 | convolution fusion | flops 3288334336 | bytes 8257536 | tf_op jit(solution)/shard_map/conv_general_dilated | solution.py:1109
  386.8 3.7 collective-permute-done.76.refs_9_.refs_2_
  391.2 3.6 shard_map.313
  399.7 8.8 %fusion.9.refs_1_ = f32[3,3,512,512]{3,2,1,0:T(8,128)S(1)} fusion(bf16[7,7,32,512]{3,2,1,0:T(8,128)(2,1)S(1)} %bitcast.115, bf16[7,7,32,512]{3,2,1,0:T(8,128)(2,1)S(1)} %bitcast.102), kind=kOutput, calls=%fused_computation.28 | convolution fusion | flops 6056574976 | bytes 12648448 | tf_op jit(solution)/shard_map/conv_general_dilated | solution.py:1120
  409.8 6.6 %convolution_add_fusion = f32[3,3,512,512]{3,2,1,0:T(8,128)S(1)} fusion(f32[3,3,512,512]{3,2,1,0:T(8,128)S(1)} %fusion.9.refs_1_, bf16[3,3,128,512]{3,2,1,0:T(8,128)(2,1)S(1)} %bitcast.117, bf16[3,3,128,512]{3,2,1,0:T(8,128)(2,1)S(1)} %bitcast.99), kind=kOutput, calls=%fused_computation | convolution fusion | flops 3290693632 | bytes 21233664 | tf_op jit(solution)/shard_map/conv_general_dilated | solution.py:1120
  416.4 2.7 shard_map.317.refs_1_
  419.2 2.3 copy-done
  422.2 3.3 collective-permute-start.84
  427.1 4.0 collective-permute-done.85.refs_3_
  438.8 10.0 %shard_map.323 = (f32[1,16,64,512]{3,2,1,0:T(8,128)S(1)}, f32[1,16,64,512]{3,2,1,0:T(8,128)S(1)}) custom-call(s32[1]{0:T(128)} %bitcast.20.refs_0_, bf16[1568,2048]{1,0:T(8,128)(2,1)} %bitcast.127, bf16[1568,512]{1,0:T(8,128)(2,1)S(1)} %get-tuple-element.249.refs_2_, bf16[1152,2048]{1,0:T(8,128)(2,1)} %bitcast.131, ...), custom_call_target="tpu_custom_call" | custom-call | flops 5704253440 | bytes 18120704 | tf_op jit(solution)/shard_map/pallas_call | solution.py:114
  448.8 2.9 shard_map.324
  456.1 11.9 %shard_map.326 = (bf16[1568,2048]{1,0:T(8,128)(2,1)}, bf16[1152,2048]{1,0:T(8,128)(2,1)}) custom-call(bf16[1568,2048]{1,0:T(8,128)(2,1)} %get-tuple-element.202.refs_0_, bf16[1152,2048]{1,0:T(8,128)(2,1)} %get-tuple-element.203.refs_1_, bf16[1568,512]{1,0:T(8,128)(2,1)S(1)} %get-tuple-element.249.refs_2_, ...), custom_call_target="tpu_custom_call" | custom-call | flops 5704253440 | bytes 27164672 | tf_op jit(solution)/shard_map/pallas_call | solution.py:114
  467.9 2.0 collective-permute-done.93.refs_2_
  470.0 2.9 copy-done.20
  473.5 6.9 %collective-permute-done.91.refs_2_ = f32[9,8,16,256]{3,2,1,0:T(8,128)S(1)} collective-permute-done((f32[9,8,16,256]{3,2,1,0:T(8,128)S(1)}, f32[9,8,16,256]{3,2,1,0:T(8,128)S(1)}, u32[]{:S(2)}, u32[]{:S(2)}) %collective-permute-start.91) | collective-permute-done | bytes 1179680 | tf_op jit(solution)/shard_map/ppermute | solution.py:337
  486.2 11.9 %collective-permute-done.96.refs_2_ = f32[9,4,16,256]{3,2,1,0:T(8,128)S(1)} collective-permute-done((f32[9,4,16,256]{3,2,1,0:T(8,128)S(1)}, f32[9,4,16,256]{3,2,1,0:T(8,128)S(1)}, u32[]{:S(2)}, u32[]{:S(2)}) %collective-permute-start.96) | collective-permute-done | bytes 589856 | tf_op jit(solution)/shard_map/ppermute | solution.py:337
  500.8 8.0 %collective-permute-done.94.refs_2_ = f32[1,8,64,256]{3,2,1,0:T(8,128)S(1)} collective-permute-done((f32[1,8,64,256]{3,2,1,0:T(8,128)S(1)}, f32[1,8,64,256]{3,2,1,0:T(8,128)S(1)}, u32[]{:S(2)}, u32[]{:S(2)}) %collective-permute-start.94) | collective-permute-done | bytes 524320 | tf_op jit(solution)/shard_map/ppermute | solution.py:337
  512.0 3.4 collective-permute-done.98.refs_2_
  521.2 4.0 collective-permute-done.101.refs_2_
  525.3 3.0 collective-permute-start.102
  529.6 6.5 %collective-permute-done.104.refs_1_ = f32[1,1,16,2048]{3,2,1,0:T(8,128)S(1)} collective-permute-done((f32[1,1,16,2048]{3,2,1,0:T(8,128)}, f32[1,1,16,2048]{3,2,1,0:T(8,128)S(1)}, u32[]{:S(2)}, u32[]{:S(2)}) %collective-permute-start.104) | collective-permute-done | bytes 131104 | tf_op jit(solution)/shard_map/ppermute | solution.py:337
  536.8 4.4 collective-permute-done.103.refs_1_
  (571 shorter events, 202.6 us)
Async XLA Ops:
  7.2 339.4 %all-gather.2.cloned.1.call-start = ((), (), s32[]{:S(2)}) async-start(), calls=%async_computation.2 | async-start | bytes 11796480 | tf_op jit(solution)/shard_map/all_gather | solution.py:1297
  34.2 5.4 collective-permute-start.6
  67.7 5.4 collective-permute-start.13
  97.8 5.6 %collective-permute-start.19 = (f32[1,4224]{1,0:T(1,128)S(1)}, f32[1,4224]{1,0:T(1,128)}, u32[]{:S(2)}, u32[]{:S(2)}) collective-permute-start(f32[1,4224]{1,0:T(1,128)S(1)} %shard_map.281.refs_0_), channel_id=1, source_target_pairs={{0,16},{1,17},{2,18},{3,19},{4,20},{5,21},{6,22},{7,23},{8,24},{9,... | collective-permute-start | bytes 50696 | tf_op jit(solution)/shard_map/ppermute | solution.py:145
  101.7 5.6 %collective-permute-start.20 = (f32[1,4224]{1,0:T(1,128)S(1)}, f32[1,4224]{1,0:T(1,128)}, u32[]{:S(2)}, u32[]{:S(2)}) collective-permute-start(f32[1,4224]{1,0:T(1,128)S(1)} %shard_map.281.refs_0_), channel_id=1, source_target_pairs={{0,24},{1,25},{2,26},{3,27},{4,28},{5,29},{6,30},{7,31},{8,16},{9,... | collective-permute-start | bytes 50696 | tf_op jit(solution)/shard_map/ppermute | solution.py:145
  135.0 6.3 %collective-permute-start.25 = (f32[1,4224]{1,0:T(1,128)S(1)}, f32[1,4224]{1,0:T(1,128)S(1)}, u32[]{:S(2)}, u32[]{:S(2)}) collective-permute-start(f32[1,4224]{1,0:T(1,128)S(1)} %shard_map.286.refs_0_), channel_id=1, source_target_pairs={{0,8},{1,9},{2,10},{3,11},{4,12},{5,13},{6,14},{7,15},{8,0},{9,1},... | collective-permute-start | bytes 50696 | tf_op jit(solution)/shard_map/ppermute | solution.py:145
  135.1 6.2 %collective-permute-start.26 = (f32[1,4224]{1,0:T(1,128)S(1)}, f32[1,4224]{1,0:T(1,128)S(1)}, u32[]{:S(2)}, u32[]{:S(2)}) collective-permute-start(f32[1,4224]{1,0:T(1,128)S(1)} %shard_map.286.refs_0_), channel_id=1, source_target_pairs={{0,16},{1,17},{2,18},{3,19},{4,20},{5,21},{6,22},{7,23},{8,24},{9,... | collective-permute-start | bytes 50696 | tf_op jit(solution)/shard_map/ppermute | solution.py:145
  135.9 5.5 %collective-permute-start.27 = (f32[1,4224]{1,0:T(1,128)S(1)}, f32[1,4224]{1,0:T(1,128)S(1)}, u32[]{:S(2)}, u32[]{:S(2)}) collective-permute-start(f32[1,4224]{1,0:T(1,128)S(1)} %shard_map.286.refs_0_), channel_id=1, source_target_pairs={{0,24},{1,25},{2,26},{3,27},{4,28},{5,29},{6,30},{7,31},{8,16},{9,... | collective-permute-start | bytes 50696 | tf_op jit(solution)/shard_map/ppermute | solution.py:145
  149.9 4.7 collective-permute-start.31
  155.0 5.6 %collective-permute-start.33 = (f32[1,6144]{1,0:T(1,128)S(1)}, f32[1,6144]{1,0:T(1,128)S(1)}, u32[]{:S(2)}, u32[]{:S(2)}) collective-permute-start(f32[1,6144]{1,0:T(1,128)S(1)} %add_add_fusion.2.refs_0_), channel_id=1, source_target_pairs={{0,16},{1,17},{2,18},{3,19},{4,20},{5,21},{6,22},{7,23},{8,24},{9,... | collective-permute-start | bytes 73736 | tf_op jit(solution)/shard_map/ppermute | solution.py:145
  158.8 5.6 %collective-permute-start.34 = (f32[1,6144]{1,0:T(1,128)S(1)}, f32[1,6144]{1,0:T(1,128)S(1)}, u32[]{:S(2)}, u32[]{:S(2)}) collective-permute-start(f32[1,6144]{1,0:T(1,128)S(1)} %add_add_fusion.2.refs_0_), channel_id=1, source_target_pairs={{0,24},{1,25},{2,26},{3,27},{4,28},{5,29},{6,30},{7,31},{8,16},{9,... | collective-permute-start | bytes 73736 | tf_op jit(solution)/shard_map/ppermute | solution.py:145
  168.3 4.7 collective-permute-start.38
  173.2 4.8 collective-permute-start.40
  174.0 5.6 %collective-permute-start.41 = (f32[1,6144]{1,0:T(1,128)S(1)}, f32[1,6144]{1,0:T(1,128)S(1)}, u32[]{:S(2)}, u32[]{:S(2)}) collective-permute-start(f32[1,6144]{1,0:T(1,128)S(1)} %add_add_fusion.1.refs_0_), channel_id=1, source_target_pairs={{0,24},{1,25},{2,26},{3,27},{4,28},{5,29},{6,30},{7,31},{8,16},{9,... | collective-permute-start | bytes 73736 | tf_op jit(solution)/shard_map/ppermute | solution.py:145
  182.9 4.9 collective-permute-start.43
  185.0 4.8 collective-permute-start.45
  190.6 6.0 %collective-permute-start.46 = (f32[1,6144]{1,0:T(1,128)S(1)}, f32[1,6144]{1,0:T(1,128)S(1)}, u32[]{:S(2)}, u32[]{:S(2)}) collective-permute-start(f32[1,6144]{1,0:T(1,128)S(1)} %add_add_fusion.refs_0_), channel_id=1, source_target_pairs={{0,8},{1,9},{2,10},{3,11},{4,12},{5,13},{6,14},{7,15},{8,0},{9,1},... | collective-permute-start | bytes 73736 | tf_op jit(solution)/shard_map/ppermute | solution.py:145
  191.0 5.6 %collective-permute-start.47 = (f32[1,6144]{1,0:T(1,128)S(1)}, f32[1,6144]{1,0:T(1,128)S(1)}, u32[]{:S(2)}, u32[]{:S(2)}) collective-permute-start(f32[1,6144]{1,0:T(1,128)S(1)} %add_add_fusion.refs_0_), channel_id=1, source_target_pairs={{0,16},{1,17},{2,18},{3,19},{4,20},{5,21},{6,22},{7,23},{8,24},{9,... | collective-permute-start | bytes 73736 | tf_op jit(solution)/shard_map/ppermute | solution.py:145
  194.8 5.6 %collective-permute-start.48 = (f32[1,6144]{1,0:T(1,128)S(1)}, f32[1,6144]{1,0:T(1,128)S(1)}, u32[]{:S(2)}, u32[]{:S(2)}) collective-permute-start(f32[1,6144]{1,0:T(1,128)S(1)} %add_add_fusion.refs_0_), channel_id=1, source_target_pairs={{0,24},{1,25},{2,26},{3,27},{4,28},{5,29},{6,30},{7,31},{8,16},{9,... | collective-permute-start | bytes 73736 | tf_op jit(solution)/shard_map/ppermute | solution.py:145
  208.6 8.6 %collective-permute-start.50 = (f32[1,4224]{1,0:T(1,128)S(1)}, f32[1,4224]{1,0:T(1,128)}, u32[]{:S(2)}, u32[]{:S(2)}) collective-permute-start(f32[1,4224]{1,0:T(1,128)S(1)} %add.140.refs_5_.refs_0_), channel_id=1, source_target_pairs={{0,2},{1,3},{2,0},{3,1},{4,6},{5,7},{6,4},{7,5},{8,10},{9,11},{10,... | collective-permute-start | bytes 50696 | tf_op jit(solution)/shard_map/ppermute | solution.py:145
  210.2 7.0 %collective-permute-start.51 = (f32[1,4224]{1,0:T(1,128)S(1)}, f32[1,4224]{1,0:T(1,128)}, u32[]{:S(2)}, u32[]{:S(2)}) collective-permute-start(f32[1,4224]{1,0:T(1,128)S(1)} %add.140.refs_5_.refs_0_), channel_id=1, source_target_pairs={{0,4},{1,5},{2,6},{3,7},{4,0},{5,1},{6,2},{7,3},{8,12},{9,13},{10,... | collective-permute-start | bytes 50696 | tf_op jit(solution)/shard_map/ppermute | solution.py:145
  210.7 6.9 %collective-permute-start.52 = (f32[1,4224]{1,0:T(1,128)S(1)}, f32[1,4224]{1,0:T(1,128)}, u32[]{:S(2)}, u32[]{:S(2)}) collective-permute-start(f32[1,4224]{1,0:T(1,128)S(1)} %add.140.refs_5_.refs_0_), channel_id=1, source_target_pairs={{0,6},{1,7},{2,4},{3,5},{4,2},{5,3},{6,0},{7,1},{8,14},{9,15},{10,... | collective-permute-start | bytes 50696 | tf_op jit(solution)/shard_map/ppermute | solution.py:145
  218.5 4.7 collective-permute-start.54
  219.3 5.5 %collective-permute-start.55 = (f32[1,4224]{1,0:T(1,128)S(1)}, f32[1,4224]{1,0:T(1,128)S(1)}, u32[]{:S(2)}, u32[]{:S(2)}) collective-permute-start(f32[1,4224]{1,0:T(1,128)S(1)} %add_add_fusion.4.refs_0_), channel_id=1, source_target_pairs={{0,24},{1,25},{2,26},{3,27},{4,28},{5,29},{6,30},{7,31},{8,16},{9,... | collective-permute-start | bytes 50696 | tf_op jit(solution)/shard_map/ppermute | solution.py:145
  240.6 21.3 %collective-permute-start.57 = (f32[1,8,80,128]{3,2,1,0:T(8,128)S(1)}, f32[1,8,80,128]{3,2,1,0:T(8,128)S(1)}, u32[]{:S(2)}, u32[]{:S(2)}) collective-permute-start(f32[1,8,80,128]{3,2,1,0:T(8,128)S(1)} %get-tuple-element.205), channel_id=1, source_target_pairs={{0,2},{1,3},{2,0},{3,1},{4,6},{5,7},{6,4},{7,5},{8,10},{9,11},{10,... | collective-permute-start | bytes 983048 | tf_op jit(solution)/shard_map/ppermute | solution.py:337
  242.1 19.8 %collective-permute-start.58 = (f32[1,8,80,128]{3,2,1,0:T(8,128)S(1)}, f32[1,8,80,128]{3,2,1,0:T(8,128)S(1)}, u32[]{:S(2)}, u32[]{:S(2)}) collective-permute-start(f32[1,8,80,128]{3,2,1,0:T(8,128)S(1)} %get-tuple-element.206), channel_id=1, source_target_pairs={{0,4},{1,5},{2,6},{3,7},{4,0},{5,1},{6,2},{7,3},{8,12},{9,13},{10,... | collective-permute-start | bytes 983048 | tf_op jit(solution)/shard_map/ppermute | solution.py:337
  270.4 5.7 %collective-permute-start.64 = (f32[1,4224]{1,0:T(1,128)S(1)}, f32[1,4224]{1,0:T(1,128)S(1)}, u32[]{:S(2)}, u32[]{:S(2)}) collective-permute-start(f32[1,4224]{1,0:T(1,128)S(1)} %add_add_fusion.3.refs_0_), channel_id=1, source_target_pairs={{0,16},{1,17},{2,18},{3,19},{4,20},{5,21},{6,22},{7,23},{8,24},{9,... | collective-permute-start | bytes 50696 | tf_op jit(solution)/shard_map/ppermute | solution.py:145
  274.3 5.5 %collective-permute-start.65 = (f32[1,4224]{1,0:T(1,128)S(1)}, f32[1,4224]{1,0:T(1,128)S(1)}, u32[]{:S(2)}, u32[]{:S(2)}) collective-permute-start(f32[1,4224]{1,0:T(1,128)S(1)} %add_add_fusion.3.refs_0_), channel_id=1, source_target_pairs={{0,24},{1,25},{2,26},{3,27},{4,28},{5,29},{6,30},{7,31},{8,16},{9,... | collective-permute-start | bytes 50696 | tf_op jit(solution)/shard_map/ppermute | solution.py:145
  282.7 37.0 %all-to-all-start = ((f32[8,160,256]{2,1,0:T(8,128)}), f32[8,160,256]{2,1,0:T(8,128)}, u32[]{:S(2)}, u32[]{:S(2)}) async-start(f32[8,160,256]{2,1,0:T(8,128)} %copy-done.9), calls=%async_computation | async-start | bytes 2621440 | tf_op jit(solution)/shard_map/all_to_all | solution.py:1321
  287.1 256.2 %reduce-scatter.2.cloned.1.call-start = ((), (), s32[]{:S(2)}) async-start(), calls=%async_computation.3 | async-start | bytes 2621440 | tf_op jit(solution)/shard_map/reduce_scatter | solution.py:1355
  293.4 24.9 %collective-permute-start.66 = (f32[1,4,80,128]{3,2,1,0:T(8,128)S(1)}, f32[1,4,80,128]{3,2,1,0:T(8,128)S(1)}, u32[]{:S(2)}, u32[]{:S(2)}) collective-permute-start(f32[1,4,80,128]{3,2,1,0:T(8,128)S(1)} %get-tuple-element.218), channel_id=1, source_target_pairs={{0,4},{1,5},{2,6},{3,7},{4,0},{5,1},{6,2},{7,3},{8,12},{9,13},{10,... | collective-permute-start | bytes 491528 | tf_op jit(solution)/shard_map/ppermute | solution.py:337
  295.1 23.8 %collective-permute-start.67 = (f32[1,4,80,128]{3,2,1,0:T(8,128)S(1)}, f32[1,4,80,128]{3,2,1,0:T(8,128)S(1)}, u32[]{:S(2)}, u32[]{:S(2)}) collective-permute-start(f32[1,4,80,128]{3,2,1,0:T(8,128)S(1)} %get-tuple-element.219), channel_id=1, source_target_pairs={{0,2},{1,3},{2,0},{3,1},{4,6},{5,7},{6,4},{7,5},{8,10},{9,11},{10,... | collective-permute-start | bytes 491528 | tf_op jit(solution)/shard_map/ppermute | solution.py:337
  335.5 24.4 %collective-permute-start.75 = (f32[1,16,16,2048]{3,2,1,0:T(8,128)}, f32[1,16,16,2048]{3,2,1,0:T(8,128)}, u32[]{:S(2)}, u32[]{:S(2)}) collective-permute-start(f32[1,16,16,2048]{3,2,1,0:T(8,128)} %get-tuple-element.229), channel_id=1, source_target_pairs={{0,1},{1,0},{2,3},{3,2},{4,5},{5,4},{6,7},{7,6},{8,9},{9,8},{10,11... | collective-permute-start | bytes 6291464 | tf_op jit(solution)/shard_map/ppermute | solution.py:337
  335.7 4.9 collective-permute-start.69
  342.1 13.4 %collective-permute-start.72 = (f32[1,1152]{1,0:T(1,128)S(1)}, f32[1,1152]{1,0:T(1,128)S(1)}, u32[]{:S(2)}, u32[]{:S(2)}) collective-permute-start(f32[1,1152]{1,0:T(1,128)S(1)} %add_add_fusion.6.refs_2_.refs_0_), channel_id=1, source_target_pairs={{0,8},{1,9},{2,10},{3,11},{4,12},{5,13},{6,14},{7,15},{8,0},{9,1},... | collective-permute-start | bytes 13832 | tf_op jit(solution)/shard_map/ppermute | solution.py:145
  343.1 12.5 %collective-permute-start.73 = (f32[1,1152]{1,0:T(1,128)S(1)}, f32[1,1152]{1,0:T(1,128)S(1)}, u32[]{:S(2)}, u32[]{:S(2)}) collective-permute-start(f32[1,1152]{1,0:T(1,128)S(1)} %add_add_fusion.6.refs_2_.refs_0_), channel_id=1, source_target_pairs={{0,16},{1,17},{2,18},{3,19},{4,20},{5,21},{6,22},{7,23},{8,24},{9,... | collective-permute-start | bytes 13832 | tf_op jit(solution)/shard_map/ppermute | solution.py:145
  345.5 10.1 %collective-permute-start.74 = (f32[1,1152]{1,0:T(1,128)S(1)}, f32[1,1152]{1,0:T(1,128)S(1)}, u32[]{:S(2)}, u32[]{:S(2)}) collective-permute-start(f32[1,1152]{1,0:T(1,128)S(1)} %add_add_fusion.6.refs_2_.refs_0_), channel_id=1, source_target_pairs={{0,24},{1,25},{2,26},{3,27},{4,28},{5,29},{6,30},{7,31},{8,16},{9,... | collective-permute-start | bytes 13832 | tf_op jit(solution)/shard_map/ppermute | solution.py:145
  378.8 11.7 %collective-permute-start.76 = (f32[1,8,16,1024]{3,2,1,0:T(8,128)S(1)}, f32[1,8,16,1024]{3,2,1,0:T(8,128)S(1)}, u32[]{:S(2)}, u32[]{:S(2)}) collective-permute-start(f32[1,8,16,1024]{3,2,1,0:T(8,128)S(1)} %get-tuple-element.237), channel_id=1, source_target_pairs={{0,2},{1,3},{2,0},{3,1},{4,6},{5,7},{6,4},{7,5},{8,10},{9,11},{10,... | collective-permute-start | bytes 1572872 | tf_op jit(solution)/shard_map/ppermute | solution.py:337
  379.8 11.4 %collective-permute-start.77 = (f32[1,8,16,1024]{3,2,1,0:T(8,128)S(1)}, f32[1,8,16,1024]{3,2,1,0:T(8,128)S(1)}, u32[]{:S(2)}, u32[]{:S(2)}) collective-permute-start(f32[1,8,16,1024]{3,2,1,0:T(8,128)S(1)} %get-tuple-element.238), channel_id=1, source_target_pairs={{0,4},{1,5},{2,6},{3,7},{4,0},{5,1},{6,2},{7,3},{8,12},{9,13},{10,... | collective-permute-start | bytes 1572872 | tf_op jit(solution)/shard_map/ppermute | solution.py:337
  381.0 5.8 %collective-permute-start.78 = (f32[1,2,80,256]{3,2,1,0:T(8,128)S(1)}, f32[1,2,80,256]{3,2,1,0:T(8,128)S(1)}, u32[]{:S(2)}, u32[]{:S(2)}) collective-permute-start(f32[1,2,80,256]{3,2,1,0:T(8,128)S(1)} %get-tuple-element.239), channel_id=1, source_target_pairs={{0,8},{1,9},{2,10},{3,11},{4,12},{5,13},{6,14},{7,15},{8,0},{9,1},... | collective-permute-start | bytes 491528 | tf_op jit(solution)/shard_map/ppermute | solution.py:337
  396.2 12.4 %collective-permute-start.80 = (f32[1,1152]{1,0:T(1,128)S(1)}, f32[1,1152]{1,0:T(1,128)S(1)}, u32[]{:S(2)}, u32[]{:S(2)}) collective-permute-start(f32[1,1152]{1,0:T(1,128)S(1)} %add.152.refs_1_.refs_0_), channel_id=1, source_target_pairs={{0,2},{1,3},{2,0},{3,1},{4,6},{5,7},{6,4},{7,5},{8,10},{9,11},{10,... | collective-permute-start | bytes 13832 | tf_op jit(solution)/shard_map/ppermute | solution.py:145
  397.3 11.2 %collective-permute-start.81 = (f32[1,1152]{1,0:T(1,128)S(1)}, f32[1,1152]{1,0:T(1,128)S(1)}, u32[]{:S(2)}, u32[]{:S(2)}) collective-permute-start(f32[1,1152]{1,0:T(1,128)S(1)} %add.152.refs_1_.refs_0_), channel_id=1, source_target_pairs={{0,4},{1,5},{2,6},{3,7},{4,0},{5,1},{6,2},{7,3},{8,12},{9,13},{10,... | collective-permute-start | bytes 13832 | tf_op jit(solution)/shard_map/ppermute | solution.py:145
  398.9 9.7 %collective-permute-start.82 = (f32[1,1152]{1,0:T(1,128)S(1)}, f32[1,1152]{1,0:T(1,128)S(1)}, u32[]{:S(2)}, u32[]{:S(2)}) collective-permute-start(f32[1,1152]{1,0:T(1,128)S(1)} %add.152.refs_1_.refs_0_), channel_id=1, source_target_pairs={{0,6},{1,7},{2,4},{3,5},{4,2},{5,3},{6,0},{7,1},{8,14},{9,15},{10,... | collective-permute-start | bytes 13832 | tf_op jit(solution)/shard_map/ppermute | solution.py:145
  421.5 27.3 %collective-permute-start.88 = (f32[9,16,16,512]{3,2,1,0:T(8,128)}, f32[9,16,16,512]{3,2,1,0:T(8,128)}, u32[]{:S(2)}, u32[]{:S(2)}) collective-permute-start(f32[9,16,16,512]{3,2,1,0:T(8,128)} %shard_map.317.refs_1_), channel_id=1, source_target_pairs={{0,1},{1,0},{2,3},{3,2},{4,5},{5,4},{6,7},{7,6},{8,9},{9,8},{10,11... | collective-permute-start | bytes 14155784 | tf_op jit(solution)/shard_map/ppermute | solution.py:337
  422.2 4.9 collective-permute-start.84
  425.5 5.5 %collective-permute-start.85 = (f32[1,1152]{1,0:T(1,128)S(1)}, f32[1,1152]{1,0:T(1,128)S(1)}, u32[]{:S(2)}, u32[]{:S(2)}) collective-permute-start(f32[1,1152]{1,0:T(1,128)S(1)} %add_add_fusion.5.refs_1_.refs_0_), channel_id=1, source_target_pairs={{0,24},{1,25},{2,26},{3,27},{4,28},{5,29},{6,30},{7,31},{8,16},{9,... | collective-permute-start | bytes 13832 | tf_op jit(solution)/shard_map/ppermute | solution.py:145
  433.4 15.4 %collective-permute-start.89 = (f32[1,1,80,256]{3,2,1,0:T(8,128)S(1)}, f32[1,1,80,256]{3,2,1,0:T(8,128)S(1)}, u32[]{:S(2)}, u32[]{:S(2)}) collective-permute-start(f32[1,1,80,256]{3,2,1,0:T(8,128)S(1)} %get-tuple-element.255), channel_id=1, source_target_pairs={{0,16},{1,17},{2,18},{3,19},{4,20},{5,21},{6,22},{7,23},{8,24},{9,... | collective-permute-start | bytes 245768 | tf_op jit(solution)/shard_map/ppermute | solution.py:337
  434.7 14.1 %collective-permute-start.86 = (f32[1,4,16,1024]{3,2,1,0:T(8,128)S(1)}, f32[1,4,16,1024]{3,2,1,0:T(8,128)S(1)}, u32[]{:S(2)}, u32[]{:S(2)}) collective-permute-start(f32[1,4,16,1024]{3,2,1,0:T(8,128)S(1)} %get-tuple-element.251), channel_id=1, source_target_pairs={{0,4},{1,5},{2,6},{3,7},{4,0},{5,1},{6,2},{7,3},{8,12},{9,13},{10,... | collective-permute-start | bytes 786440 | tf_op jit(solution)/shard_map/ppermute | solution.py:337
  435.2 13.6 %collective-permute-start.87 = (f32[1,4,16,1024]{3,2,1,0:T(8,128)S(1)}, f32[1,4,16,1024]{3,2,1,0:T(8,128)S(1)}, u32[]{:S(2)}, u32[]{:S(2)}) collective-permute-start(f32[1,4,16,1024]{3,2,1,0:T(8,128)S(1)} %get-tuple-element.253), channel_id=1, source_target_pairs={{0,2},{1,3},{2,0},{3,1},{4,6},{5,7},{6,4},{7,5},{8,10},{9,11},{10,... | collective-permute-start | bytes 786440 | tf_op jit(solution)/shard_map/ppermute | solution.py:337
  451.9 31.9 %collective-permute-start.90 = (f32[1,16,64,512]{3,2,1,0:T(8,128)S(1)}, f32[1,16,64,512]{3,2,1,0:T(8,128)S(1)}, u32[]{:S(2)}, u32[]{:S(2)}) collective-permute-start(f32[1,16,64,512]{3,2,1,0:T(8,128)S(1)} %shard_map.327), channel_id=1, source_target_pairs={{0,1},{1,0},{2,3},{3,2},{4,5},{5,4},{6,7},{7,6},{8,9},{9,8},{10,11... | collective-permute-start | bytes 6291464 | tf_op jit(solution)/shard_map/ppermute | solution.py:337
  452.0 28.4 %collective-permute-start.91 = (f32[9,8,16,256]{3,2,1,0:T(8,128)S(1)}, f32[9,8,16,256]{3,2,1,0:T(8,128)S(1)}, u32[]{:S(2)}, u32[]{:S(2)}) collective-permute-start(f32[9,8,16,256]{3,2,1,0:T(8,128)S(1)} %get-tuple-element.261), channel_id=1, source_target_pairs={{0,2},{1,3},{2,0},{3,1},{4,6},{5,7},{6,4},{7,5},{8,10},{9,11},{10,... | collective-permute-start | bytes 3538952 | tf_op jit(solution)/shard_map/ppermute | solution.py:337
  453.4 28.0 %collective-permute-start.92 = (f32[9,8,16,256]{3,2,1,0:T(8,128)S(1)}, f32[9,8,16,256]{3,2,1,0:T(8,128)S(1)}, u32[]{:S(2)}, u32[]{:S(2)}) collective-permute-start(f32[9,8,16,256]{3,2,1,0:T(8,128)S(1)} %get-tuple-element.263), channel_id=1, source_target_pairs={{0,4},{1,5},{2,6},{3,7},{4,0},{5,1},{6,2},{7,3},{8,12},{9,13},{10,... | collective-permute-start | bytes 3538952 | tf_op jit(solution)/shard_map/ppermute | solution.py:337
  455.0 15.0 %collective-permute-start.93 = (f32[1,2,16,2048]{3,2,1,0:T(8,128)S(1)}, f32[1,2,16,2048]{3,2,1,0:T(8,128)S(1)}, u32[]{:S(2)}, u32[]{:S(2)}) collective-permute-start(f32[1,2,16,2048]{3,2,1,0:T(8,128)S(1)} %get-tuple-element.264), channel_id=1, source_target_pairs={{0,8},{1,9},{2,10},{3,11},{4,12},{5,13},{6,14},{7,15},{8,0},{9,1},... | collective-permute-start | bytes 786440 | tf_op jit(solution)/shard_map/ppermute | solution.py:337
  481.8 16.3 %collective-permute-start.96 = (f32[9,4,16,256]{3,2,1,0:T(8,128)S(1)}, f32[9,4,16,256]{3,2,1,0:T(8,128)S(1)}, u32[]{:S(2)}, u32[]{:S(2)}) collective-permute-start(f32[9,4,16,256]{3,2,1,0:T(8,128)S(1)} %get-tuple-element.271), channel_id=1, source_target_pairs={{0,4},{1,5},{2,6},{3,7},{4,0},{5,1},{6,2},{7,3},{8,12},{9,13},{10,... | collective-permute-start | bytes 1769480 | tf_op jit(solution)/shard_map/ppermute | solution.py:337
  483.3 16.3 %collective-permute-start.97 = (f32[9,4,16,256]{3,2,1,0:T(8,128)S(1)}, f32[9,4,16,256]{3,2,1,0:T(8,128)S(1)}, u32[]{:S(2)}, u32[]{:S(2)}) collective-permute-start(f32[9,4,16,256]{3,2,1,0:T(8,128)S(1)} %get-tuple-element.273), channel_id=1, source_target_pairs={{0,2},{1,3},{2,0},{3,1},{4,6},{5,7},{6,4},{7,5},{8,10},{9,11},{10,... | collective-permute-start | bytes 1769480 | tf_op jit(solution)/shard_map/ppermute | solution.py:337
  484.1 24.8 %collective-permute-start.94 = (f32[1,8,64,256]{3,2,1,0:T(8,128)S(1)}, f32[1,8,64,256]{3,2,1,0:T(8,128)S(1)}, u32[]{:S(2)}, u32[]{:S(2)}) collective-permute-start(f32[1,8,64,256]{3,2,1,0:T(8,128)S(1)} %get-tuple-element.268), channel_id=1, source_target_pairs={{0,2},{1,3},{2,0},{3,1},{4,6},{5,7},{6,4},{7,5},{8,10},{9,11},{10,... | collective-permute-start | bytes 1572872 | tf_op jit(solution)/shard_map/ppermute | solution.py:337
  485.7 23.2 %collective-permute-start.95 = (f32[1,8,64,256]{3,2,1,0:T(8,128)S(1)}, f32[1,8,64,256]{3,2,1,0:T(8,128)S(1)}, u32[]{:S(2)}, u32[]{:S(2)}) collective-permute-start(f32[1,8,64,256]{3,2,1,0:T(8,128)S(1)} %get-tuple-element.270), channel_id=1, source_target_pairs={{0,4},{1,5},{2,6},{3,7},{4,0},{5,1},{6,2},{7,3},{8,12},{9,13},{10,... | collective-permute-start | bytes 1572872 | tf_op jit(solution)/shard_map/ppermute | solution.py:337
  499.8 11.5 %collective-permute-start.100 = (f32[9,2,16,512]{3,2,1,0:T(8,128)S(1)}, f32[9,2,16,512]{3,2,1,0:T(8,128)S(1)}, u32[]{:S(2)}, u32[]{:S(2)}) collective-permute-start(f32[9,2,16,512]{3,2,1,0:T(8,128)S(1)} %get-tuple-element.279), channel_id=1, source_target_pairs={{0,8},{1,9},{2,10},{3,11},{4,12},{5,13},{6,14},{7,15},{8,0},{9,1},... | collective-permute-start | bytes 1769480 | tf_op jit(solution)/shard_map/ppermute | solution.py:337
  509.0 6.4 %collective-permute-start.98 = (f32[1,4,64,256]{3,2,1,0:T(8,128)S(1)}, f32[1,4,64,256]{3,2,1,0:T(8,128)S(1)}, u32[]{:S(2)}, u32[]{:S(2)}) collective-permute-start(f32[1,4,64,256]{3,2,1,0:T(8,128)S(1)} %get-tuple-element.276), channel_id=1, source_target_pairs={{0,4},{1,5},{2,6},{3,7},{4,0},{5,1},{6,2},{7,3},{8,12},{9,13},{10,... | collective-permute-start | bytes 786440 | tf_op jit(solution)/shard_map/ppermute | solution.py:337
  509.6 6.4 %collective-permute-start.99 = (f32[1,4,64,256]{3,2,1,0:T(8,128)S(1)}, f32[1,4,64,256]{3,2,1,0:T(8,128)S(1)}, u32[]{:S(2)}, u32[]{:S(2)}) collective-permute-start(f32[1,4,64,256]{3,2,1,0:T(8,128)S(1)} %get-tuple-element.278), channel_id=1, source_target_pairs={{0,2},{1,3},{2,0},{3,1},{4,6},{5,7},{6,4},{7,5},{8,10},{9,11},{10,... | collective-permute-start | bytes 786440 | tf_op jit(solution)/shard_map/ppermute | solution.py:337
  516.0 9.2 %collective-permute-start.101 = (f32[1,2,64,512]{3,2,1,0:T(8,128)S(1)}, f32[1,2,64,512]{3,2,1,0:T(8,128)S(1)}, u32[]{:S(2)}, u32[]{:S(2)}) collective-permute-start(f32[1,2,64,512]{3,2,1,0:T(8,128)S(1)} %get-tuple-element.282), channel_id=1, source_target_pairs={{0,8},{1,9},{2,10},{3,11},{4,12},{5,13},{6,14},{7,15},{8,0},{9,1},... | collective-permute-start | bytes 786440 | tf_op jit(solution)/shard_map/ppermute | solution.py:337
  518.3 17.9 %collective-permute-start.104 = (f32[1,1,16,2048]{3,2,1,0:T(8,128)}, f32[1,1,16,2048]{3,2,1,0:T(8,128)S(1)}, u32[]{:S(2)}, u32[]{:S(2)}) collective-permute-start(f32[1,1,16,2048]{3,2,1,0:T(8,128)} %get-tuple-element.286), channel_id=1, source_target_pairs={{0,16},{1,17},{2,18},{3,19},{4,20},{5,21},{6,22},{7,23},{8,24},{9,... | collective-permute-start | bytes 393224 | tf_op jit(solution)/shard_map/ppermute | solution.py:337
  519.6 21.6 %collective-permute-start.103 = (f32[9,1,16,512]{3,2,1,0:T(8,128)}, f32[9,1,16,512]{3,2,1,0:T(8,128)S(1)}, u32[]{:S(2)}, u32[]{:S(2)}) collective-permute-start(f32[9,1,16,512]{3,2,1,0:T(8,128)} %get-tuple-element.285), channel_id=1, source_target_pairs={{0,16},{1,17},{2,18},{3,19},{4,20},{5,21},{6,22},{7,23},{8,24},{9,... | collective-permute-start | bytes 884744 | tf_op jit(solution)/shard_map/ppermute | solution.py:337
  525.3 17.3 %collective-permute-start.102 = (f32[1,1,64,512]{3,2,1,0:T(8,128)S(1)}, f32[1,1,64,512]{3,2,1,0:T(8,128)S(1)}, u32[]{:S(2)}, u32[]{:S(2)}) collective-permute-start(f32[1,1,64,512]{3,2,1,0:T(8,128)S(1)} %get-tuple-element.284), channel_id=1, source_target_pairs={{0,16},{1,17},{2,18},{3,19},{4,20},{5,21},{6,22},{7,23},{8,24},{9,... | collective-permute-start | bytes 393224 | tf_op jit(solution)/shard_map/ppermute | solution.py:337
  (193 other events, 1377.2 us)
Sparse Core Ops, SparseCore 0:
  235.2 85.0 all-gather.1
  421.6 50.0 reduce-scatter.1
